TPU v7x, 32 devices: a whole 2x2x4 slice. The times are simulated.
32 devices in a mesh: seq: 8 (over y, x, core), fsdp: 4 (over z).
Axes of the slice: x: 2, y: 2, z: 4, core: 2. Of those that a mesh axis runs over, the one named last changes fastest.
Arguments:
- inputs: bfloat16 [4, 1024, 1152], P('fsdp', 'seq'), may hold values from -6 to 6
- segments: int32 [4, 1024], P('fsdp', 'seq'), may hold values from 0 to 1023, as said below
- cotangent: bfloat16 [4, 1024, 1152], P('fsdp', 'seq'), may hold values from -6 to 6
- gain_attn_in: bfloat16 [1152], P('fsdp'), may hold values from 0.099609375 to 1.8984375
- w_query: bfloat16 [1152, 1024], P('fsdp'), may hold values from -0.1875 to 0.1875
- w_key: bfloat16 [1152, 256], P('fsdp'), may hold values from -0.1875 to 0.1875
- w_value: bfloat16 [1152, 256], P('fsdp'), may hold values from -0.1875 to 0.1875
- gain_query: bfloat16 [256], P('fsdp'), may hold values from 0.099609375 to 1.8984375
- gain_key: bfloat16 [256], P('fsdp'), may hold values from 0.099609375 to 1.8984375
- w_output: bfloat16 [1024, 1152], P('fsdp'), may hold values from -0.1875 to 0.1875
- gain_attn_out: bfloat16 [1152], P('fsdp'), may hold values from 0.099609375 to 1.8984375
- gain_ffn_in: bfloat16 [1152], P('fsdp'), may hold values from 0.099609375 to 1.8984375
- w_gate: bfloat16 [1152, 6912], P('fsdp'), may hold values from -0.1875 to 0.1875
- w_up: bfloat16 [1152, 6912], P('fsdp'), may hold values from -0.1875 to 0.1875
- w_down: bfloat16 [6912, 1152], P('fsdp'), may hold values from -0.078125 to 0.078125
- gain_ffn_out: bfloat16 [1152], P('fsdp'), may hold values from 0.099609375 to 1.8984375
Outputs:
- outputs: bfloat16 [4, 1024, 1152], P('fsdp', 'seq')
- d_inputs: float32 [4, 1024, 1152], P('fsdp', 'seq')
- grad_gain_attn_in: float32 [1152], P('fsdp')
- grad_w_query: float32 [1152, 1024], P('fsdp')
- grad_w_key: float32 [1152, 256], P('fsdp')
- grad_w_value: float32 [1152, 256], P('fsdp')
- grad_gain_query: float32 [256], P('fsdp')
- grad_gain_key: float32 [256], P('fsdp')
- grad_w_output: float32 [1024, 1152], P('fsdp')
- grad_gain_attn_out: float32 [1152], P('fsdp')
- grad_gain_ffn_in: float32 [1152], P('fsdp')
- grad_w_gate: float32 [1152, 6912], P('fsdp')
- grad_w_up: float32 [1152, 6912], P('fsdp')
- grad_w_down: float32 [6912, 1152], P('fsdp')
- grad_gain_ffn_out: float32 [1152], P('fsdp')
Inputs may be any that keep to these rules, and one draw needn't show every extreme that they name: `segments`: each token's number is the position within its sequence of its document's first token, so numbers never fall along a sequence and the first is 0. In every sequence one document begins within the first 64 positions and ends within the last 64 positions; the other documents are short, and the last position is a document of one token.
All inputs are finite; a program needn't handle non-finite values.
Results may differ from a plain program's by a relative error of at most 0.022.
Values may be sent and summed in bfloat16 or wider, within the bound.
A program may use at most 448 MiB of HBM per device.

v0:
```python
import jax
import jax.numpy as jnp
from jax import lax
from jax.sharding import PartitionSpec as P

WINDOW = 512


epsilon = 1e-06
masked_value = -1e30


def from_behind(block, axis, distance):
    devices = range(lax.axis_size(axis))
    route = [(i - distance, i) for i in devices if i - distance in devices]
    return lax.ppermute(block, axis, route)


def norm_rows(rows_in, gain_vec):
    return (
        rows_in
        * lax.rsqrt(jnp.mean(rows_in * rows_in, axis=-1, keepdims=True) + epsilon)
        * gain_vec
    )


def angles(positions, head_width):
    inv_rates = 10000.0 ** (-(jnp.arange(head_width // 2, dtype=jnp.float32) * 2.0) / head_width)
    return positions.astype(jnp.float32)[:, None] * inv_rates[None, :]


def rotate(rows_in, angles_at):
    half_width = rows_in.shape[-1] // 2
    lower_half = rows_in[..., :half_width]
    upper_half = rows_in[..., half_width:]
    cosine = jnp.cos(angles_at)
    sine_part = jnp.sin(angles_at)
    return jnp.concatenate(
        [
            lower_half * cosine - upper_half * sine_part,
            upper_half * cosine + lower_half * sine_part,
        ],
        axis=-1,
    )


def geglu_act(gate_proj, up_proj):
    return jax.nn.gelu(gate_proj, approximate=True) * up_proj


def inner_rows(left, right):
    return lax.dot_general(
        left, right, (((0,), (0,)), ((), ())), preferred_element_type=jnp.float32
    )


def outer_cols(left, right):
    return lax.dot_general(
        left, right, (((1,), (1,)), ((), ())), preferred_element_type=jnp.float32
    )


def shards(
    inputs,
    segments,
    cotangent,
    gain_attn_in,
    w_query,
    w_key,
    w_value,
    gain_query,
    gain_key,
    w_output,
    gain_attn_out,
    gain_ffn_in,
    w_gate,
    w_up,
    w_down,
    gain_ffn_out,
):
    rows_here = inputs.shape[1]
    head_width = w_key.shape[1]
    head_count = w_query.shape[1] // head_width
    reach_devs = (WINDOW - 2 + rows_here) // rows_here
    score_scale = head_width ** (-0.5)
    first_row = lax.axis_index("seq") * rows_here
    tokens = inputs[0].astype(jnp.float32)
    seg_here = segments[0]
    positions = first_row + jnp.arange(rows_here, dtype=jnp.int32)
    angles_at = angles(positions - seg_here, head_width)
    wq_all, wk_all, wv_all, wo_all, g_attn_in, g_query, g_key, g_attn_out, g_ffn_in, g_ffn_out = (
        lax.all_gather(w_query, "fsdp", axis=0, tiled=True),
        lax.all_gather(w_key, "fsdp", axis=0, tiled=True),
        lax.all_gather(w_value, "fsdp", axis=0, tiled=True),
        lax.all_gather(w_output, "fsdp", axis=0, tiled=True),
        lax.all_gather(gain_attn_in, "fsdp", axis=0, tiled=True),
        lax.all_gather(gain_query, "fsdp", axis=0, tiled=True),
        lax.all_gather(gain_key, "fsdp", axis=0, tiled=True),
        lax.all_gather(gain_attn_out, "fsdp", axis=0, tiled=True),
        lax.all_gather(gain_ffn_in, "fsdp", axis=0, tiled=True),
        lax.all_gather(gain_ffn_out, "fsdp", axis=0, tiled=True),
    )
    g_attn_in = g_attn_in.astype(jnp.float32)
    g_query = g_query.astype(jnp.float32)
    g_key = g_key.astype(jnp.float32)
    g_attn_out = g_attn_out.astype(jnp.float32)
    g_ffn_in = g_ffn_in.astype(jnp.float32)
    g_ffn_out = g_ffn_out.astype(jnp.float32)
    normed_one, pull_one = jax.vjp(norm_rows, tokens, g_attn_in)
    h_one = normed_one.astype(jnp.bfloat16)
    q_raw = jnp.dot(h_one, wq_all, preferred_element_type=jnp.float32)
    k_raw = jnp.dot(h_one, wk_all, preferred_element_type=jnp.float32)
    v_raw = jnp.dot(h_one, wv_all, preferred_element_type=jnp.float32)

    def prepare(q_in, k_in, gq_in, gk_in):
        q_rows = q_in.reshape(q_in.shape[0], head_count, head_width)
        q_fin = rotate(norm_rows(q_rows, gq_in), angles_at[:, None, :])
        k_fin = rotate(norm_rows(k_in, gk_in), angles_at)
        return (q_fin, k_fin)

    (q_fin, k_fin), pull_prep = jax.vjp(prepare, q_raw, k_raw, g_query, g_key)
    q_low = q_fin.astype(jnp.bfloat16).reshape(rows_here * head_count, head_width)
    k_low = k_fin.astype(jnp.bfloat16)
    v_low = v_raw.astype(jnp.bfloat16)
    key_parts = []
    value_parts = []
    seg_parts = []
    for offset in range(reach_devs, 0, -1):
        k_came, v_came, s_came = from_behind((k_low, v_low, seg_here), "seq", offset)
        key_parts.append(k_came)
        value_parts.append(v_came)
        seg_parts.append(s_came)
    key_rows = jnp.concatenate(key_parts + [k_low], axis=0)
    value_rows = jnp.concatenate(value_parts + [v_low], axis=0)
    key_segs = jnp.concatenate(seg_parts + [seg_here], axis=0)
    key_place = (
        first_row
        - reach_devs * rows_here
        + jnp.arange((reach_devs + 1) * rows_here, dtype=jnp.int32)
    )
    distance = positions[:, None] - key_place[None, :]
    allowed = (
        (distance >= 0)
        & (distance < WINDOW)
        & (key_place[None, :] >= 0)
        & (seg_here[:, None] == key_segs[None, :])
    )
    scores = (outer_cols(q_low, key_rows) * score_scale).reshape(rows_here, head_count, -1)
    masked = jnp.where(allowed[:, None, :], scores, masked_value)
    attn_probs = jax.nn.softmax(masked, axis=-1).reshape(rows_here * head_count, -1)
    probs_low = attn_probs.astype(jnp.bfloat16)
    attended = jnp.dot(probs_low, value_rows, preferred_element_type=jnp.float32)
    att_low = attended.reshape(rows_here, head_count * head_width).astype(jnp.bfloat16)
    o_raw = jnp.dot(att_low, wo_all, preferred_element_type=jnp.float32)
    branch_att, pull_att = jax.vjp(norm_rows, o_raw, g_attn_out)
    middle = tokens + branch_att
    normed_two, pull_mid = jax.vjp(norm_rows, middle, g_ffn_in)
    h_two = normed_two.astype(jnp.bfloat16)
    gate_all, up_all, down_all = (
        lax.all_gather(w_gate, "fsdp", axis=0, tiled=True),
        lax.all_gather(w_up, "fsdp", axis=0, tiled=True),
        lax.all_gather(w_down, "fsdp", axis=0, tiled=True),
    )
    gate_proj = jnp.dot(h_two, gate_all, preferred_element_type=jnp.float32)
    up_proj = jnp.dot(h_two, up_all, preferred_element_type=jnp.float32)
    act_full, pull_act = jax.vjp(geglu_act, gate_proj, up_proj)
    act_low = act_full.astype(jnp.bfloat16)
    f_raw = jnp.dot(act_low, down_all, preferred_element_type=jnp.float32)
    branch_ffn, pull_out = jax.vjp(norm_rows, f_raw, g_ffn_out)
    outputs = (middle + branch_ffn).astype(jnp.bfloat16)
    upstream = cotangent[0].astype(jnp.float32)
    d_fraw, d_gffn_out = pull_out(upstream)
    d_flow = d_fraw.astype(jnp.bfloat16)
    gate_shard, up_shard, down_shard, d_flow = lax.optimization_barrier(
        (w_gate, w_up, w_down, d_flow)
    )
    gate_back, up_back, down_back = (
        lax.all_gather(gate_shard, "fsdp", axis=0, tiled=True),
        lax.all_gather(up_shard, "fsdp", axis=0, tiled=True),
        lax.all_gather(down_shard, "fsdp", axis=0, tiled=True),
    )
    d_act = outer_cols(d_flow, down_back)
    d_gate, d_up = pull_act(d_act)
    dg_low = d_gate.astype(jnp.bfloat16)
    du_low = d_up.astype(jnp.bfloat16)
    d_htwo = outer_cols(dg_low, gate_back) + outer_cols(du_low, up_back)
    grad_down_part = lax.psum_scatter(
        inner_rows(act_low, d_flow).astype(jnp.bfloat16), "fsdp", scatter_dimension=0, tiled=True
    )
    grad_in_part = lax.psum_scatter(
        jnp.concatenate([inner_rows(h_two, dg_low), inner_rows(h_two, du_low)], axis=1).astype(
            jnp.bfloat16
        ),
        "fsdp",
        scatter_dimension=0,
        tiled=True,
    ).astype(jnp.float32)
    hidden_width = w_gate.shape[1]
    grad_gate_part = grad_in_part[:, :hidden_width]
    grad_up_part = grad_in_part[:, hidden_width:]
    d_mid_norm, d_gffn_in = pull_mid(d_htwo)
    d_middle = upstream + d_mid_norm
    d_oraw, d_gattn_out = pull_att(d_middle)
    d_olow = d_oraw.astype(jnp.bfloat16)
    grad_wo = inner_rows(att_low, d_olow)
    d_att_low = (
        outer_cols(d_olow, wo_all).astype(jnp.bfloat16).reshape(rows_here * head_count, head_width)
    )
    d_probs = outer_cols(d_att_low, value_rows)
    d_scores = attn_probs * (d_probs - jnp.sum(attn_probs * d_probs, axis=-1, keepdims=True))
    ds_low = d_scores.astype(jnp.bfloat16)
    d_qfin = jnp.dot(ds_low, key_rows, preferred_element_type=jnp.float32) * score_scale
    d_keys = inner_rows(ds_low, q_low) * score_scale
    d_values = inner_rows(probs_low, d_att_low)
    d_kfin = d_keys[reach_devs * rows_here :]
    d_vsum = d_values[reach_devs * rows_here :]
    for offset in range(1, reach_devs + 1):
        slot_index = reach_devs - offset
        k_back, v_back = (
            from_behind(
                d_keys[slot_index * rows_here : (slot_index + 1) * rows_here].astype(jnp.bfloat16),
                "seq",
                -offset,
            ).astype(jnp.float32),
            from_behind(
                d_values[slot_index * rows_here : (slot_index + 1) * rows_here].astype(
                    jnp.bfloat16
                ),
                "seq",
                -offset,
            ).astype(jnp.float32),
        )
        d_kfin = d_kfin + k_back
        d_vsum = d_vsum + v_back
    d_qraw, d_kraw, d_gquery, d_gkey = pull_prep(
        (d_qfin.reshape(rows_here, head_count, head_width), d_kfin)
    )
    dq_low = d_qraw.astype(jnp.bfloat16)
    dk_low = d_kraw.astype(jnp.bfloat16)
    dv_low = d_vsum.astype(jnp.bfloat16)
    d_hone = outer_cols(dq_low, wq_all) + outer_cols(dk_low, wk_all) + outer_cols(dv_low, wv_all)
    grad_wq = inner_rows(h_one, dq_low)
    grad_wk = inner_rows(h_one, dk_low)
    grad_wv = inner_rows(h_one, dv_low)
    d_tok_norm, d_gattn_in = pull_one(d_hone)
    d_inputs = d_middle + d_tok_norm
    part_wq, part_wk, part_wv, part_wo, part_gai, part_gq, part_gk, part_gao, part_gfi, part_gfo = (
        lax.psum_scatter(
            grad_wq.astype(jnp.bfloat16), "fsdp", scatter_dimension=0, tiled=True
        ).astype(jnp.float32),
        lax.psum_scatter(
            grad_wk.astype(jnp.bfloat16), "fsdp", scatter_dimension=0, tiled=True
        ).astype(jnp.float32),
        lax.psum_scatter(
            grad_wv.astype(jnp.bfloat16), "fsdp", scatter_dimension=0, tiled=True
        ).astype(jnp.float32),
        lax.psum_scatter(
            grad_wo.astype(jnp.bfloat16), "fsdp", scatter_dimension=0, tiled=True
        ).astype(jnp.float32),
        lax.psum_scatter(
            d_gattn_in.astype(jnp.bfloat16), "fsdp", scatter_dimension=0, tiled=True
        ).astype(jnp.float32),
        lax.psum_scatter(
            d_gquery.astype(jnp.bfloat16), "fsdp", scatter_dimension=0, tiled=True
        ).astype(jnp.float32),
        lax.psum_scatter(
            d_gkey.astype(jnp.bfloat16), "fsdp", scatter_dimension=0, tiled=True
        ).astype(jnp.float32),
        lax.psum_scatter(
            d_gattn_out.astype(jnp.bfloat16), "fsdp", scatter_dimension=0, tiled=True
        ).astype(jnp.float32),
        lax.psum_scatter(
            d_gffn_in.astype(jnp.bfloat16), "fsdp", scatter_dimension=0, tiled=True
        ).astype(jnp.float32),
        lax.psum_scatter(
            d_gffn_out.astype(jnp.bfloat16), "fsdp", scatter_dimension=0, tiled=True
        ).astype(jnp.float32),
    )
    cols_wq, cols_wk, cols_wv, cols_wo, cols_gate, cols_up, cols_down = (
        lax.psum_scatter(
            part_wq.astype(jnp.bfloat16), "seq", scatter_dimension=1, tiled=True
        ).astype(jnp.float32),
        lax.psum_scatter(
            part_wk.astype(jnp.bfloat16), "seq", scatter_dimension=1, tiled=True
        ).astype(jnp.float32),
        lax.psum_scatter(
            part_wv.astype(jnp.bfloat16), "seq", scatter_dimension=1, tiled=True
        ).astype(jnp.float32),
        lax.psum_scatter(
            part_wo.astype(jnp.bfloat16), "seq", scatter_dimension=1, tiled=True
        ).astype(jnp.float32),
        lax.psum_scatter(
            grad_gate_part.astype(jnp.bfloat16), "seq", scatter_dimension=1, tiled=True
        ).astype(jnp.float32),
        lax.psum_scatter(
            grad_up_part.astype(jnp.bfloat16), "seq", scatter_dimension=1, tiled=True
        ).astype(jnp.float32),
        lax.psum_scatter(grad_down_part, "seq", scatter_dimension=1, tiled=True).astype(
            jnp.float32
        ),
    )
    sum_wq, sum_wk, sum_wv, sum_wo, sum_gate, sum_up, sum_down = (
        lax.all_gather(cols_wq.astype(jnp.bfloat16), "seq", axis=1, tiled=True).astype(
            cols_wq.dtype
        ),
        lax.all_gather(cols_wk.astype(jnp.bfloat16), "seq", axis=1, tiled=True).astype(
            cols_wk.dtype
        ),
        lax.all_gather(cols_wv.astype(jnp.bfloat16), "seq", axis=1, tiled=True).astype(
            cols_wv.dtype
        ),
        lax.all_gather(cols_wo.astype(jnp.bfloat16), "seq", axis=1, tiled=True).astype(
            cols_wo.dtype
        ),
        lax.all_gather(cols_gate.astype(jnp.bfloat16), "seq", axis=1, tiled=True).astype(
            cols_gate.dtype
        ),
        lax.all_gather(cols_up.astype(jnp.bfloat16), "seq", axis=1, tiled=True).astype(
            cols_up.dtype
        ),
        lax.all_gather(cols_down.astype(jnp.bfloat16), "seq", axis=1, tiled=True).astype(
            cols_down.dtype
        ),
    )
    sum_gai, sum_gq, sum_gk, sum_gao, sum_gfi, sum_gfo = lax.psum(
        (part_gai, part_gq, part_gk, part_gao, part_gfi, part_gfo), "seq"
    )
    return (
        outputs[None],
        d_inputs[None],
        sum_gai,
        sum_wq,
        sum_wk,
        sum_wv,
        sum_gq,
        sum_gk,
        sum_wo,
        sum_gao,
        sum_gfi,
        sum_gate,
        sum_up,
        sum_down,
        sum_gfo,
    )


def solution(mesh):
    placed = (
        P("fsdp", "seq", None),
        P("fsdp", "seq"),
        P("fsdp", "seq", None),
        P("fsdp"),
        P("fsdp", None),
        P("fsdp", None),
        P("fsdp", None),
        P("fsdp"),
        P("fsdp"),
        P("fsdp", None),
        P("fsdp"),
        P("fsdp"),
        P("fsdp", None),
        P("fsdp", None),
        P("fsdp", None),
        P("fsdp"),
    )
    return jax.shard_map(
        shards,
        mesh=mesh,
        in_specs=placed,
        out_specs=(
            P("fsdp", "seq", None),
            P("fsdp", "seq", None),
            P("fsdp"),
            P("fsdp", None),
            P("fsdp", None),
            P("fsdp", None),
            P("fsdp"),
            P("fsdp"),
            P("fsdp", None),
            P("fsdp"),
            P("fsdp"),
            P("fsdp", None),
            P("fsdp", None),
            P("fsdp", None),
            P("fsdp"),
        ),
        check_vma=False,
    )
```

profile of v0, /device:TPU:9, one launch (start us, length us, event | category | flops | bytes accessed | tf_op | source)
XLA Modules:
  0.0 3182.2 jit_solution(12789918370317179240)
XLA Ops:
  14.2 13.3 all-reduce.18
  27.6 23.8 all_gather.74
  54.6 7.7 collective-permute-start.9
  69.0 12.8 all_gather.72
  129.1 268.1 %all-gather.18.cloned.1.call-done = bf16[1152,6912]{1,0:T(8,128)(2,1)} async-done(((bf16[288,6912]{1,0:T(8,128)(2,1)}), bf16[1152,6912]{1,0:T(8,128)(2,1)}) %all-gather.18.cloned.1.call-update) | async-done | bytes 15925264 | tf_op jit(solution)/shard_map/all_gather | solution.py:160
  397.1 9.8 fusion.90
  406.9 262.7 %all-gather.20.cloned.1.call-done = bf16[1152,6912]{1,0:T(8,128)(2,1)} async-done(((bf16[288,6912]{1,0:T(8,128)(2,1)}), bf16[1152,6912]{1,0:T(8,128)(2,1)}) %all-gather.20.cloned.1.call-update) | async-done | bytes 15925264 | tf_op jit(solution)/shard_map/all_gather | solution.py:161
  669.6 11.2 multiply_convert_fusion.1
  680.9 261.3 %all-gather.22.cloned.1.call-done = bf16[6912,1152]{1,0:T(8,128)(2,1)} async-done(((bf16[1728,1152]{1,0:T(8,128)(2,1)}), bf16[6912,1152]{1,0:T(8,128)(2,1)}) %all-gather.22.cloned.1.call-update) | async-done | bytes 15925264 | tf_op jit(solution)/shard_map/all_gather | solution.py:162
  942.1 8.1 multiply_reduce_fusion.5
  953.9 9.8 convolution_convert_fusion
  963.8 259.6 %all-gather.24.cloned.1.call-done = bf16[6912,1152]{1,0:T(8,128)(2,1)} async-done(((bf16[1728,1152]{1,0:T(8,128)(2,1)}), bf16[6912,1152]{1,0:T(8,128)(2,1)}) %all-gather.24.cloned.1.call-update) | async-done | bytes 15925264 | tf_op jit(solution)/shard_map/all_gather | solution.py:180
  1223.4 10.3 multiply_convert_fusion
  1233.7 9.3 convolution_convert_fusion.1
  1243.0 7.8 convolution_convert_fusion.2
  1250.9 21.8 pad_maximum_fusion
  1273.0 223.1 %all-gather.26.cloned.1.call-done = bf16[1152,6912]{1,0:T(8,128)(2,1)} async-done(((bf16[288,6912]{1,0:T(8,128)(2,1)}), bf16[1152,6912]{1,0:T(8,128)(2,1)}) %all-gather.26.cloned.1.call-update) | async-done | bytes 15925264 | tf_op jit(solution)/shard_map/all_gather | solution.py:178
  1496.0 11.9 fusion.91
  1507.9 260.7 %all-gather.28.cloned.1.call-done = bf16[1152,6912]{1,0:T(8,128)(2,1)} async-done(((bf16[288,6912]{1,0:T(8,128)(2,1)}), bf16[1152,6912]{1,0:T(8,128)(2,1)}) %all-gather.28.cloned.1.call-update) | async-done | bytes 15925264 | tf_op jit(solution)/shard_map/all_gather | solution.py:179
  1768.7 11.4 multiply_reduce_fusion.1
  1817.9 218.6 %reduce-scatter.38.cloned.1.call-done = bf16[1728,1152]{1,0:T(8,128)(2,1)} async-done(((bf16[6912,1152]{1,0:T(8,128)(2,1)}), bf16[1728,1152]{1,0:T(8,128)(2,1)}) %reduce-scatter.38.cloned.1.call-update) | async-done | bytes 3981328 | tf_op jit(solution)/shard_map/reduce_scatter | solution.py:187
  2036.5 6.3 copy.68
  2042.9 522.7 %reduce-scatter.36.cloned.1.call-done = bf16[288,13824]{1,0:T(8,128)(2,1)} async-done(((bf16[1152,13824]{1,0:T(8,128)(2,1)}), bf16[288,13824]{1,0:T(8,128)(2,1)}) %reduce-scatter.36.cloned.1.call-update) | async-done | bytes 7962640 | tf_op jit(solution)/shard_map/reduce_scatter | solution.py:190
  2571.3 6.5 copy.64
  2577.9 6.6 copy.66
  2591.8 21.3 reduce-scatter.32.cloned.1.call-done
  2614.9 48.1 %reduce-scatter.28.cloned.1.call-done = bf16[288,1024]{1,0:T(8,128)(2,1)} async-done(((bf16[1152,1024]{1,0:T(8,128)(2,1)}), bf16[288,1024]{1,0:T(8,128)(2,1)}) %reduce-scatter.28.cloned.1.call-update) | async-done | bytes 589840 | tf_op jit(solution)/shard_map/reduce_scatter | solution.py:248
  2665.4 47.4 %reduce-scatter.34.cloned.1.call-done = bf16[256,1152]{1,0:T(8,128)(2,1)} async-done(((bf16[1024,1152]{1,0:T(8,128)(2,1)}), bf16[256,1152]{1,0:T(8,128)(2,1)}) %reduce-scatter.34.cloned.1.call-update) | async-done | bytes 589840 | tf_op jit(solution)/shard_map/reduce_scatter | solution.py:257
  2715.0 54.6 %reduce-scatter.52.cloned.1.call-done = bf16[144,1728]{1,0:T(8,128)(2,1)} async-done(((bf16[1152,1728]{1,0:T(8,128)(2,1)}), bf16[144,1728]{1,0:T(8,128)(2,1)}) %reduce-scatter.52.cloned.1.call-update) | async-done | bytes 497680
  2769.7 60.7 %reduce-scatter.48.cloned.1.call-done = bf16[864,288]{1,0:T(8,128)(2,1)} async-done(((bf16[6912,288]{1,0:T(8,128)(2,1)}), bf16[864,288]{1,0:T(8,128)(2,1)}) %reduce-scatter.48.cloned.1.call-update) | async-done | bytes 497680
  2832.6 59.0 %reduce-scatter.50.cloned.1.call-done = bf16[864,288]{1,0:T(8,128)(2,1)} async-done(((bf16[6912,288]{1,0:T(8,128)(2,1)}), bf16[864,288]{1,0:T(8,128)(2,1)}) %reduce-scatter.50.cloned.1.call-update) | async-done | bytes 497680
  2898.5 11.9 all-reduce.17
  2910.7 16.2 all-reduce.16
  2928.2 10.1 all_gather.86
  2939.1 25.8 reduce-scatter.44.cloned.1.call-done
  2965.0 10.2 all_gather.87
  2976.0 27.7 reduce-scatter.40.cloned.1.call-done
  3004.7 11.0 all_gather.85
  3016.8 24.3 reduce-scatter.46.cloned.1.call-done
  3041.1 11.2 all_gather.88
  3053.5 26.8 all-gather.30.cloned.1.call-done
  3080.4 6.9 copy.55
  3087.2 32.1 %all-gather.32.cloned.1.call-done = bf16[8,864,288]{1,2,0:T(8,128)(2,1)} async-done(((bf16[1,864,288]{1,2,0:T(8,128)(2,1)}), bf16[8,864,288]{1,2,0:T(8,128)(2,1)}) %all-gather.32.cloned.1.call-update) | async-done | bytes 3981328 | tf_op jit(solution)/shard_map/all_gather | solution.py:315
  3119.3 6.8 copy.49
  3126.1 10.0 reshape.396
  3136.1 22.0 all-gather.34.cloned.1.call-done
  3158.1 6.8 copy.50
  3164.9 9.9 reshape.397
  (369 shorter events, 137.0 us)
Async XLA Ops:
  7.2 106.8 %all-gather.14.cloned.1.call-start = ((), (), s32[]{:S(2)}) async-start(), calls=%async_computation.13 | async-start | bytes 2949120 | tf_op jit(solution)/shard_map/all_gather | solution.py:92
  7.9 116.9 %all-gather.16.cloned.1.call-start = ((), (), s32[]{:S(2)}) async-start(), calls=%async_computation.14 | async-start | bytes 2949120 | tf_op jit(solution)/shard_map/all_gather | solution.py:95
  8.7 388.5 %all-gather.18.cloned.1.call-start = ((), (), s32[]{:S(2)}) async-start(), calls=%async_computation.15 | async-start | bytes 19906560 | tf_op jit(solution)/shard_map/all_gather | solution.py:160
  9.5 660.1 %all-gather.20.cloned.1.call-start = ((), (), s32[]{:S(2)}) async-start(), calls=%async_computation.16 | async-start | bytes 19906560 | tf_op jit(solution)/shard_map/all_gather | solution.py:161
  10.1 932.0 %all-gather.22.cloned.1.call-start = ((), (), s32[]{:S(2)}) async-start(), calls=%async_computation.17 | async-start | bytes 19906560 | tf_op jit(solution)/shard_map/all_gather | solution.py:162
  10.7 1212.7 %all-gather.24.cloned.1.call-start = ((), (), s32[]{:S(2)}) async-start(), calls=%async_computation.18 | async-start | bytes 19906560 | tf_op jit(solution)/shard_map/all_gather | solution.py:180
  52.3 66.1 %copy-start.36 = (f32[128]{0:T(128)}, f32[128]{0:T(128)S(1)}, u32[]{:S(2)}) copy-start(f32[128]{0:T(128)S(1)} %fusion.67) | copy-start | bytes 1540
  52.6 50.6 %collective-permute-start.8 = (bf16[128,256]{1,0:T(8,128)(2,1)S(1)}, bf16[128,256]{1,0:T(8,128)(2,1)S(1)}, u32[]{:S(2)}, u32[]{:S(2)}) collective-permute-start(bf16[128,256]{1,0:T(8,128)(2,1)S(1)} %convolution_convert_fusion.9), channel_id=1, source_target_pairs={{0,16},{4,20},{8,24},{12,28},{1,17},{5,21},{9,25},{13,29},{2,18},{... | collective-permute-start | bytes 196616 | tf_op jit(solution)/shard_map/ppermute | solution.py:16
  54.6 52.7 %collective-permute-start.9 = (bf16[128,256]{1,0:T(8,128)(2,1)S(1)}, bf16[128,256]{1,0:T(8,128)(2,1)S(1)}, u32[]{:S(2)}, u32[]{:S(2)}) collective-permute-start(bf16[128,256]{1,0:T(8,128)(2,1)S(1)} %convolution_convert_fusion.9), channel_id=1, source_target_pairs={{0,12},{4,16},{8,20},{12,24},{16,28},{1,13},{5,17},{9,21},{13,25},... | collective-permute-start | bytes 196616 | tf_op jit(solution)/shard_map/ppermute | solution.py:16
  62.3 46.4 %collective-permute-start.10 = (bf16[128,256]{1,0:T(8,128)(2,1)S(1)}, bf16[128,256]{1,0:T(8,128)(2,1)S(1)}, u32[]{:S(2)}, u32[]{:S(2)}) collective-permute-start(bf16[128,256]{1,0:T(8,128)(2,1)S(1)} %convolution_convert_fusion.9), channel_id=1, source_target_pairs={{0,8},{4,12},{8,16},{12,20},{16,24},{20,28},{1,9},{5,13},{9,17},{1... | collective-permute-start | bytes 196616 | tf_op jit(solution)/shard_map/ppermute | solution.py:16
  65.4 47.8 %collective-permute-start.11 = (bf16[128,256]{1,0:T(8,128)(2,1)S(1)}, bf16[128,256]{1,0:T(8,128)(2,1)S(1)}, u32[]{:S(2)}, u32[]{:S(2)}) collective-permute-start(bf16[128,256]{1,0:T(8,128)(2,1)S(1)} %convolution_convert_fusion.9), channel_id=1, source_target_pairs={{0,4},{4,8},{8,12},{12,16},{16,20},{20,24},{24,28},{1,5},{5,9},{9,... | collective-permute-start | bytes 196616 | tf_op jit(solution)/shard_map/ppermute | solution.py:16
  67.6 16.8 collective-permute-start
  84.5 4.1 collective-permute-start.1
  88.6 5.5 collective-permute-start.2
  94.1 4.2 collective-permute-start.3
  99.4 13.8 collective-permute-start.4
  103.2 10.0 collective-permute-start.5
  107.3 6.0 collective-permute-start.6
  108.7 5.2 collective-permute-start.7
  952.2 543.8 %all-gather.26.cloned.1.call-start = ((), (), s32[]{:S(2)}) async-start(), calls=%async_computation.19 | async-start | bytes 19906560 | tf_op jit(solution)/shard_map/all_gather | solution.py:178
  952.9 815.7 %all-gather.28.cloned.1.call-start = ((), (), s32[]{:S(2)}) async-start(), calls=%async_computation.20 | async-start | bytes 19906560 | tf_op jit(solution)/shard_map/all_gather | solution.py:179
  953.7 1082.8 %reduce-scatter.38.cloned.1.call-start = ((), (), s32[]{:S(2)}) async-start(), calls=%async_computation.26 | async-start | bytes 19906560 | tf_op jit(solution)/shard_map/reduce_scatter | solution.py:187
  963.7 1601.9 %reduce-scatter.36.cloned.1.call-start = ((), (), s32[]{:S(2)}) async-start(), calls=%async_computation.25 | async-start | bytes 39813120 | tf_op jit(solution)/shard_map/reduce_scatter | solution.py:190
  1272.7 1317.3 %reduce-scatter.30.cloned.1.call-start = ((), (), s32[]{:S(2)}) async-start(), calls=%async_computation.22 | async-start | bytes 737280 | tf_op jit(solution)/shard_map/reduce_scatter | solution.py:251
  1507.9 272.2 %copy-start.10 = (bf16[1,128,1152]{2,1,0:T(8,128)(2,1)S(1)}, bf16[1,128,1152]{2,1,0:T(8,128)(2,1)}, u32[]{:S(2)}) copy-start(bf16[1,128,1152]{2,1,0:T(8,128)(2,1)} %param.18) | copy-start | bytes 884740
  1784.7 6.3 collective-permute-start.15
  1786.0 7.0 collective-permute-start.14
  1787.3 7.1 collective-permute-start.13
  1788.6 7.0 collective-permute-start.12
  1797.6 815.6 %reduce-scatter.32.cloned.1.call-start = ((), (), s32[]{:S(2)}) async-start(), calls=%async_computation.23 | async-start | bytes 737280 | tf_op jit(solution)/shard_map/reduce_scatter | solution.py:254
  1799.2 6.7 collective-permute-start.19
  1800.6 6.0 collective-permute-start.18
  1801.9 7.6 collective-permute-start.17
  1803.2 6.6 collective-permute-start.16
  1812.0 851.1 %reduce-scatter.28.cloned.1.call-start = ((), (), s32[]{:S(2)}) async-start(), calls=%async_computation.21 | async-start | bytes 2949120 | tf_op jit(solution)/shard_map/reduce_scatter | solution.py:248
  1815.6 897.2 %reduce-scatter.34.cloned.1.call-start = ((), (), s32[]{:S(2)}) async-start(), calls=%async_computation.24 | async-start | bytes 2949120 | tf_op jit(solution)/shard_map/reduce_scatter | solution.py:257
  1817.9 951.7 %reduce-scatter.52.cloned.1.call-start = ((), (), s32[]{:S(2)}) async-start(), calls=%async_computation.36 | async-start | bytes 4644864
  2042.9 787.5 %reduce-scatter.48.cloned.1.call-start = ((), (), s32[]{:S(2)}) async-start(), calls=%async_computation.34 | async-start | bytes 5971968
  2577.8 313.8 %reduce-scatter.50.cloned.1.call-start = ((), (), s32[]{:S(2)}) async-start(), calls=%async_computation.35 | async-start | bytes 5971968
  2584.5 343.7 %reduce-scatter.42.cloned.1.call-start = ((), (), s32[]{:S(2)}) async-start(), calls=%async_computation.31 | async-start | bytes 221184
  2591.8 373.2 %reduce-scatter.44.cloned.1.call-start = ((), (), s32[]{:S(2)}) async-start(), calls=%async_computation.32 | async-start | bytes 221184
  2614.9 388.8 %reduce-scatter.40.cloned.1.call-start = ((), (), s32[]{:S(2)}) async-start(), calls=%async_computation.30 | async-start | bytes 884736
  2665.3 375.8 %reduce-scatter.46.cloned.1.call-start = ((), (), s32[]{:S(2)}) async-start(), calls=%async_computation.33 | async-start | bytes 663552
  2715.0 365.4 %all-gather.30.cloned.1.call-start = ((), (), s32[]{:S(2)}) async-start(), calls=%async_computation.27 | async-start | bytes 4644864 | tf_op jit(solution)/shard_map/all_gather | solution.py:321
  2769.6 128.1 %copy-start.12 = (bf16[1152,256]{1,0:T(8,128)(2,1)S(1)}, bf16[1152,256]{1,0:T(8,128)(2,1)}, u32[]{:S(2)}) copy-start(bf16[1152,256]{1,0:T(8,128)(2,1)} %copy-done.11) | copy-start | bytes 1769476
  2769.6 349.7 %all-gather.32.cloned.1.call-start = ((), (), s32[]{:S(2)}) async-start(), calls=%async_computation.28 | async-start | bytes 4644864 | tf_op jit(solution)/shard_map/all_gather | solution.py:315
  2832.5 65.5 %copy-start.14 = (bf16[1152,256]{1,0:T(8,128)(2,1)S(1)}, bf16[1152,256]{1,0:T(8,128)(2,1)}, u32[]{:S(2)}) copy-start(bf16[1152,256]{1,0:T(8,128)(2,1)} %copy-done.13) | copy-start | bytes 1769476
  2832.5 325.6 %all-gather.34.cloned.1.call-start = ((), (), s32[]{:S(2)}) async-start(), calls=%async_computation.29 | async-start | bytes 4644864 | tf_op jit(solution)/shard_map/all_gather | solution.py:318
  (75 other events, 864.2 us)
Sparse Core Ops, SparseCore 0:
  9.6 59.6 all-gather.13
  70.8 53.9 all-gather.15
  126.4 270.6 all-gather.17
  398.6 271.0 all-gather.19
  671.0 271.0 all-gather.21
  952.3 271.0 all-gather.23
  1225.0 271.0 all-gather.25
  1497.6 271.0 all-gather.27
  1771.0 265.4 reduce-scatter.37
  2038.8 526.7 reduce-scatter.35
  2567.9 22.0 reduce-scatter.29
  2592.7 20.3 reduce-scatter.31
  2615.4 47.6 reduce-scatter.27
  2665.2 47.5 reduce-scatter.33
  2716.7 52.8 reduce-scatter.51
  2773.4 56.9 reduce-scatter.47
  2834.6 56.9 reduce-scatter.49
  2895.0 33.0 reduce-scatter.41
  2931.5 33.4 reduce-scatter.43
  2968.5 35.1 reduce-scatter.39
  3006.8 34.2 reduce-scatter.45
  3043.0 37.3 all-gather.29
  3082.8 36.4 all-gather.31
  3121.6 36.4 all-gather.33
where the time goes:
time: 3190 us; the launch traced here: 3180 us
  waiting for transfers between devices  2750 us (86%)
  blocking collectives  121 us (4%)
  matrix products  110 us (3%)
  local copies, waits for them, and re-layouts  95.5 us (3%)
  starting transfers between devices  55.4 us (2%)
  other arithmetic  32.1 us (1%)
    reduce_scatter x1, waiting for transfers between devices, shards(): lax.psum_scatter(jnp.concatenate([inner_rows(h_two, dg_low), inner_rows(h...  523 us
    all_gather x1, waiting for transfers between devices, shards(): lax.all_gather(w_gate, 'fsdp', axis=0, tiled=True)  268 us
    all_gather x1, waiting for transfers between devices, shards(): lax.all_gather(w_up, 'fsdp', axis=0, tiled=True)  263 us
    all_gather x1, waiting for transfers between devices, shards(): lax.all_gather(w_down, 'fsdp', axis=0, tiled=True)  261 us
    all_gather x1, waiting for transfers between devices, shards(): lax.all_gather(up_shard, 'fsdp', axis=0, tiled=True)  261 us
    all_gather x1, waiting for transfers between devices, shards(): lax.all_gather(down_shard, 'fsdp', axis=0, tiled=True)  260 us
    unnamed x31, waiting for transfers between devices  257 us
    all_gather x1, waiting for transfers between devices, shards(): lax.all_gather(gate_shard, 'fsdp', axis=0, tiled=True)  223 us
  transfers between devices with their start and end apart: 44, of which 34 were waited for; matrix products, arithmetic and copies ran while one was open for 6% of the time, Pallas kernels for 0%

commit v1 on v0

--- a/solution.py
+++ b/solution.py
@@ -1,6 +1,10 @@
+import functools
+
 import jax
 import jax.numpy as jnp
 from jax import lax
+from jax.experimental import pallas as pl
+from jax.experimental.pallas import tpu as pltpu
 from jax.sharding import PartitionSpec as P
 
 WINDOW = 512
@@ -60,7 +64,7 @@
     )
 
 
-def shards(
+def shards_plain(
     inputs,
     segments,
     cotangent,
@@ -344,6 +348,983 @@
     )
 
 
+MESH = pl.DeviceIdType.MESH
+BF16 = jnp.bfloat16
+F32 = jnp.float32
+GELU_RATE = 0.7978845608028654
+GELU_CUBE = 0.044715
+HID_TILE = 256
+
+
+def bit_of(value, mask):
+    return lax.rem(lax.div(value, mask), 2)
+
+
+def flip(value, masks, bits):
+    for b in range(bits):
+        if (masks >> b) & 1:
+            value = value + (1 << b) * (1 - 2 * bit_of(value, 1 << b))
+    return value
+
+
+def greet(devices):
+    barrier = pltpu.get_barrier_semaphore()
+    for device in devices:
+        pl.semaphore_signal(barrier, inc=1, device_id=device, device_id_type=MESH)
+    pl.semaphore_wait(barrier, len(devices))
+
+
+def remote(src, dst, send, recv, device):
+    return pltpu.make_async_remote_copy(
+        src_ref=src, dst_ref=dst, send_sem=send, recv_sem=recv,
+        device_id=device, device_id_type=MESH,
+    )
+
+
+def many(offset, size):
+    return pl.ds(pl.multiple_of(offset, size if size % 128 == 0 else 16), size)
+
+
+def lanes(offset, size):
+    return pl.ds(pl.multiple_of(offset, 128), size)
+
+
+class Place:
+    def __init__(self, n_seq, n_fsdp):
+        self.n_seq, self.n_fsdp = n_seq, n_fsdp
+        self.s = lax.axis_index("seq")
+        self.z = lax.axis_index("fsdp")
+        self.c = bit_of(self.s, 1)
+        self.x = bit_of(self.s, 2)
+        self.y = bit_of(self.s, 4)
+
+    def plane(self, masks):
+        return (flip(self.s, masks, 3), self.z)
+
+    def line(self, masks):
+        return (self.s, flip(self.z, masks, 2))
+
+    def halves(self, first_x):
+        if first_x:
+            return self.x, self.y, 2, 4
+        return self.y, self.x, 4, 2
+
+
+def spread_kernel(
+    n_seq, n_fsdp,
+    gu_ref, qkv_ref, wo_ref, pack_ref, seg_ref,
+    gu_all, qkv_all, wo_all, pack_all, seg_all,
+    send, recv, own_sem, small_send, small_recv, seg_send, seg_recv,
+):
+    at = Place(n_seq, n_fsdp)
+    z, c = at.z, at.c
+    depth, heads_width = qkv_ref.shape
+    rows_o, width = wo_ref.shape
+    hidden = gu_ref.shape[3]
+    greet([at.plane(k) for k in range(1, n_seq)] + [at.line(m) for m in range(1, n_fsdp)])
+
+    own = [
+        pltpu.make_async_copy(gu_ref.at[i, z], gu_all.at[i, many(z * depth, depth)], own_sem.at[i])
+        for i in range(2)
+    ]
+    own.append(pltpu.make_async_copy(qkv_ref, qkv_all.at[many(z * depth, depth)], own_sem.at[2]))
+    own.append(pltpu.make_async_copy(wo_ref, wo_all.at[many(z * rows_o, rows_o)], own_sem.at[3]))
+    own.append(pltpu.make_async_copy(pack_ref, pack_all.at[z], own_sem.at[4]))
+    own.append(pltpu.make_async_copy(seg_ref, seg_all.at[at.s], own_sem.at[5]))
+
+    small = [
+        remote(pack_ref, pack_all.at[z], small_send.at[m], small_recv.at[m], at.line(m))
+        for m in range(1, n_fsdp)
+    ] + [
+        remote(seg_ref, seg_all.at[at.s], seg_send.at[k], seg_recv.at[k], at.plane(k))
+        for k in range(1, n_seq)
+    ]
+
+    def region(kind, whose, hi, lo, level):
+        base = whose * depth
+        if kind == "qkv":
+            cols = {
+                0: lanes(hi * (heads_width // 2) + lo * (heads_width // 4), heads_width // 4),
+                1: lanes(hi * (heads_width // 2), heads_width // 2),
+                2: slice(None),
+            }[level]
+            return qkv_all.at[many(base + c * (depth // 2), depth // 2), cols]
+        if kind == "wo":
+            start = whose * rows_o + c * (rows_o // 2)
+            if level < 2:
+                start = start + hi * (rows_o // 4)
+            if level < 1:
+                start = start + lo * (rows_o // 8)
+            return wo_all.at[many(start, rows_o // (8, 4, 2)[level])]
+        if level == 2:
+            return gu_all.at[c, many(base, depth)]
+        rows = many(base + hi * (depth // 2), depth // 2)
+        if level == 1:
+            return gu_all.at[c, rows]
+        return gu_all.at[c, rows, lanes(lo * (hidden // 2), hidden // 2)]
+
+    def source(kind, to, hi, lo):
+        if kind == "qkv":
+            cols = lanes(hi * (heads_width // 2) + lo * (heads_width // 4), heads_width // 4)
+            return qkv_ref.at[many(c * (depth // 2), depth // 2), cols]
+        if kind == "wo":
+            start = c * (rows_o // 2) + hi * (rows_o // 4) + lo * (rows_o // 8)
+            return wo_ref.at[many(start, rows_o // 8)]
+        rows = many(hi * (depth // 2), depth // 2)
+        return gu_ref.at[c, to, rows, lanes(lo * (hidden // 2), hidden // 2)]
+
+    items = []
+    for kind in ("qkv", "wo", "gu"):
+        for m in range(1, n_fsdp):
+            items.append((kind, m, (m % 2 == 1) != (kind == "wo")))
+    steps = []
+    for i, (kind, m, first_x) in enumerate(items):
+        hi, lo, mask_hi, mask_lo = at.halves(first_x)
+        there = flip(z, m, 2)
+        steps.append((
+            remote(source(kind, there, hi, lo), region(kind, z, hi, lo, 0),
+                   send.at[i, 0], recv.at[i, 0], at.line(m)),
+            remote(region(kind, there, hi, lo, 0), region(kind, there, hi, lo, 0),
+                   send.at[i, 1], recv.at[i, 1], at.plane(mask_lo)),
+            remote(region(kind, there, hi, lo, 1), region(kind, there, hi, lo, 1),
+                   send.at[i, 2], recv.at[i, 2], at.plane(mask_hi)),
+            remote(region(kind, there, hi, lo, 2), region(kind, there, hi, lo, 2),
+                   send.at[i, 3], recv.at[i, 3], at.plane(1)),
+        ))
+    for i in range(len(items)):
+        steps[i][0].start()
+    for copy in small:
+        copy.start()
+    for copy in own:
+        copy.start()
+    for t in range(len(items) + 2):
+        for stage in (3, 2, 1):
+            i = t - (stage - 1)
+            if 0 <= i < len(items):
+                steps[i][stage - 1].wait_recv()
+                steps[i][stage].start()
+    for i in range(len(items)):
+        steps[i][3].wait_recv()
+        for stage in range(4):
+            steps[i][stage].wait_send()
+    for copy in small:
+        copy.wait()
+    for copy in own:
+        copy.wait()
+
+
+def spread(n_seq, n_fsdp, gu_blocks, qkv, wo, pack, segs):
+    depth, heads_width = qkv.shape
+    rows_o, width = wo.shape
+    hidden = gu_blocks.shape[3]
+    n_items = 3 * (n_fsdp - 1)
+    anywhere = pl.BlockSpec(memory_space=pl.ANY)
+    return pl.pallas_call(
+        functools.partial(spread_kernel, n_seq, n_fsdp),
+        out_shape=[
+            jax.ShapeDtypeStruct((2, n_fsdp * depth, hidden), BF16),
+            jax.ShapeDtypeStruct((n_fsdp * depth, heads_width), BF16),
+            jax.ShapeDtypeStruct((n_fsdp * rows_o, width), BF16),
+            jax.ShapeDtypeStruct((n_fsdp,) + pack.shape, BF16),
+            jax.ShapeDtypeStruct((n_seq,) + segs.shape, jnp.int32),
+        ],
+        in_specs=[anywhere] * 5,
+        out_specs=[anywhere] * 5,
+        scratch_shapes=[
+            pltpu.SemaphoreType.DMA((n_items, 4)),
+            pltpu.SemaphoreType.DMA((n_items, 4)),
+            pltpu.SemaphoreType.DMA((6,)),
+            pltpu.SemaphoreType.DMA((n_fsdp,)),
+            pltpu.SemaphoreType.DMA((n_fsdp,)),
+            pltpu.SemaphoreType.DMA((n_seq,)),
+            pltpu.SemaphoreType.DMA((n_seq,)),
+        ],
+        compiler_params=pltpu.CompilerParams(collective_id=0, has_side_effects=True),
+        name="spread_weights",
+    )(gu_blocks, qkv, wo, pack, segs)
+
+
+def behind_kernel(n_seq, reach, kv_ref, came_ref, send, recv):
+    s, z = lax.axis_index("seq"), lax.axis_index("fsdp")
+    greet([(lax.rem(s + n_seq - o, n_seq), z) for o in range(1, reach + 1)])
+    copies = [
+        remote(kv_ref, came_ref.at[reach - o], send.at[o - 1], recv.at[o - 1],
+               (lax.rem(s + o, n_seq), z))
+        for o in range(1, reach + 1)
+    ]
+    for copy in copies:
+        copy.start()
+    came_ref[reach] = kv_ref[...]
+    for copy in copies:
+        copy.wait()
+
+
+def from_blocks_behind(n_seq, reach, keys_values):
+    return pl.pallas_call(
+        functools.partial(behind_kernel, n_seq, reach),
+        out_shape=jax.ShapeDtypeStruct((reach + 1,) + keys_values.shape, keys_values.dtype),
+        in_specs=[pl.BlockSpec(memory_space=pltpu.VMEM)],
+        out_specs=pl.BlockSpec(memory_space=pltpu.VMEM),
+        scratch_shapes=[pltpu.SemaphoreType.DMA((reach,)), pltpu.SemaphoreType.DMA((reach,))],
+        compiler_params=pltpu.CompilerParams(collective_id=1, has_side_effects=True),
+        name="keys_values_behind",
+    )(keys_values)
+
+
+def return_kernel(n_seq, reach, parts_ref, own_ref, sum_ref, came, send, recv):
+    s, z = lax.axis_index("seq"), lax.axis_index("fsdp")
+    greet([(lax.rem(s + o, n_seq), z) for o in range(1, reach + 1)])
+    copies = [
+        remote(parts_ref.at[reach - o], came.at[o - 1], send.at[o - 1], recv.at[o - 1],
+               (lax.rem(s + n_seq - o, n_seq), z))
+        for o in range(1, reach + 1)
+    ]
+    for copy in copies:
+        copy.start()
+    for copy in copies:
+        copy.wait()
+    total = own_ref[...]
+    for o in range(reach):
+        total = total + came[o].astype(F32)
+    sum_ref[...] = total
+
+
+def return_to_blocks(n_seq, reach, parts, own):
+    in_vmem = pl.BlockSpec(memory_space=pltpu.VMEM)
+    return pl.pallas_call(
+        functools.partial(return_kernel, n_seq, reach),
+        out_shape=jax.ShapeDtypeStruct(own.shape, F32),
+        in_specs=[in_vmem] * 2,
+        out_specs=in_vmem,
+        scratch_shapes=[
+            pltpu.VMEM(parts.shape, BF16),
+            pltpu.SemaphoreType.DMA((reach,)),
+            pltpu.SemaphoreType.DMA((reach,)),
+        ],
+        compiler_params=pltpu.CompilerParams(collective_id=2, has_side_effects=True),
+        name="keys_values_return",
+    )(parts, own)
+
+
+def dot_nt(left, right):
+    return lax.dot_general(left, right, (((1,), (1,)), ((), ())), preferred_element_type=F32)
+
+
+def dot_nn(left, right):
+    return jnp.dot(left, right, preferred_element_type=F32)
+
+
+def ffn_kernel(
+    n_seq, n_fsdp,
+    h_ref, mid_ref, cot_ref, gains_ref, gu_ref, wd_ref,
+    out_ref, dmid_ref, ggu_ref, gd_ref, dgain_ref,
+    w_in, w_down, h_all, df_all, gelu_s, slope_s, act, dgate, dup, h_turn,
+    part_out, part_in, total, stage, w_sem, ex_send, ex_recv, stage_sem,
+):
+    at = Place(n_seq, n_fsdp)
+    rows, width = h_ref.shape
+    hidden = w_in.shape[2]
+    hidden_used = wd_ref.shape[0]
+    n_hid = hidden // HID_TILE
+    out_tile = width // 3
+    loads = [
+        pltpu.make_async_copy(gu_ref.at[0], w_in.at[0], w_sem.at[0]),
+        pltpu.make_async_copy(gu_ref.at[1], w_in.at[1], w_sem.at[1]),
+        pltpu.make_async_copy(wd_ref, w_down.at[pl.ds(0, hidden_used)], w_sem.at[2]),
+    ]
+    for load in loads:
+        load.start()
+    h_all[0] = h_ref[...]
+    greet([at.line(m) for m in range(1, n_fsdp)])
+
+    def exchange(phase, src, dst):
+        copies = {}
+        for m in range(1, n_fsdp):
+            copies[m] = remote(
+                src(m), dst(m), ex_send.at[phase, m], ex_recv.at[phase, m], at.line(m)
+            )
+        return copies
+
+    send_h = exchange(0, lambda m: h_all.at[0], lambda m: h_all.at[m])
+    send_f = exchange(1, lambda m: part_out.at[0, m], lambda m: part_in.at[0, m])
+    send_df = exchange(2, lambda m: df_all.at[0], lambda m: df_all.at[m])
+    send_dh = exchange(3, lambda m: part_out.at[1, m], lambda m: part_in.at[1, m])
+    for m in range(1, n_fsdp):
+        send_h[m].start()
+    if hidden > hidden_used:
+        w_down[pl.ds(hidden_used, hidden - hidden_used)] = jnp.zeros(
+            (hidden - hidden_used, width), BF16
+        )
+    for load in loads:
+        load.wait()
+
+    def hid(n):
+        return pl.ds(pl.multiple_of(n * HID_TILE, HID_TILE), HID_TILE)
+
+    def outs(n):
+        return pl.ds(pl.multiple_of(n * out_tile, 128), out_tile)
+
+    for m in range(n_fsdp):
+        if m:
+            send_h[m].wait_recv()
+
+        @pl.loop(0, n_hid)
+        def _(n):
+            rows_h = h_all[m]
+            gate = dot_nn(rows_h, w_in[0, :, hid(n)])
+            up = dot_nn(rows_h, w_in[1, :, hid(n)])
+            squared = gate * gate
+            bent = jnp.tanh(GELU_RATE * (gate + GELU_CUBE * squared * gate))
+            gelu = 0.5 * gate * (1.0 + bent)
+            slope = 0.5 * (1.0 + bent) + 0.5 * gate * (1.0 - bent * bent) * (
+                GELU_RATE * (1.0 + 3.0 * GELU_CUBE * squared)
+            )
+            gelu_s[m, :, hid(n)] = gelu
+            slope_s[m, :, hid(n)] = slope * up
+            act[m, :, hid(n)] = (gelu * up).astype(BF16)
+
+        @pl.loop(0, 3)
+        def _(n):
+            part = dot_nn(act[m], w_down[:, outs(n)])
+            if m:
+                part_out[0, m, :, outs(n)] = part.astype(BF16)
+            else:
+                total[:, outs(n)] = part
+
+        if m:
+            send_f[m].start()
+
+    for m in range(n_fsdp):
+        h_turn[:, pl.ds(m * rows, rows)] = h_all[m].T
+
+    for m in range(1, n_fsdp):
+        send_f[m].wait_recv()
+    f_raw = total[...]
+    for m in range(1, n_fsdp):
+        f_raw = f_raw + part_in[0, m].astype(F32)
+    cot = cot_ref[...].astype(F32)
+    gain = gains_ref[0:1, :]
+    scale = lax.rsqrt(jnp.mean(f_raw * f_raw, axis=-1, keepdims=True) + epsilon)
+    out_ref[...] = (mid_ref[...] + f_raw * scale * gain).astype(BF16)
+    pulled = cot * gain
+    inner = jnp.mean(pulled * f_raw, axis=-1, keepdims=True)
+    df_all[0] = (scale * pulled - f_raw * (scale * scale * scale * inner)).astype(BF16)
+    for m in range(1, n_fsdp):
+        send_df[m].start()
+    dgain_ref[...] = jnp.zeros(dgain_ref.shape, F32)
+    dgain_ref[0:1, :] = jnp.sum(cot * f_raw * scale, axis=0, keepdims=True)
+
+    for m in range(n_fsdp):
+        if m:
+            send_df[m].wait_recv()
+
+        @pl.loop(0, n_hid)
+        def _(n):
+            dact = dot_nt(df_all[m], w_down[hid(n), :])
+            dgate[m, :, hid(n)] = (dact * slope_s[m, :, hid(n)]).astype(BF16)
+            dup[m, :, hid(n)] = (dact * gelu_s[m, :, hid(n)]).astype(BF16)
+
+        @pl.loop(0, 3)
+        def _(n):
+            part = dot_nt(dgate[m], w_in[0, outs(n), :]) + dot_nt(dup[m], w_in[1, outs(n), :])
+            if m:
+                part_out[1, m, :, outs(n)] = part.astype(BF16)
+            else:
+                total[:, outs(n)] = part
+
+        if m:
+            send_dh[m].start()
+
+    tokens = n_fsdp * rows
+    df_rows = df_all[...].reshape(tokens, width)
+
+    def leave(slot, dst):
+        return pltpu.make_async_copy(stage.at[slot], dst, stage_sem.at[slot])
+
+    def leave_down(n):
+        return pltpu.make_async_copy(
+            stage.at[2, pl.ds(0, HID_TILE), :], gd_ref.at[hid(n), :], stage_sem.at[2]
+        )
+
+    @pl.loop(0, n_hid)
+    def _(n):
+        @pl.when(n > 0)
+        def _():
+            leave_down(n - 1).wait()
+
+        left = act[:, :, hid(n)].reshape(tokens, HID_TILE)
+        stage[2, pl.ds(0, HID_TILE), :] = inner_rows(left, df_rows).astype(BF16)
+        leave_down(n).start()
+
+    leave_down(n_hid - 1).wait()
+
+    def leave_in(i, n):
+        return pltpu.make_async_copy(
+            stage_in(i), ggu_ref.at[i, :, hid(n)], stage_sem.at[i]
+        )
+
+    def stage_in(i):
+        return stage.at[i, :, pl.ds(0, HID_TILE)]
+
+    for i, grads in enumerate((dgate, dup)):
+
+        @pl.loop(0, n_hid)
+        def _(n):
+            @pl.when(n > 0)
+            def _():
+                leave_in(i, n - 1).wait()
+
+            right = grads[:, :, hid(n)].reshape(tokens, HID_TILE)
+            stage[i, :, pl.ds(0, HID_TILE)] = dot_nn(h_turn[...], right).astype(BF16)
+            leave_in(i, n).start()
+
+        leave_in(i, n_hid - 1).wait()
+
+    for m in range(1, n_fsdp):
+        send_dh[m].wait_recv()
+    dh = total[...]
+    for m in range(1, n_fsdp):
+        dh = dh + part_in[1, m].astype(F32)
+    mid = mid_ref[...]
+    gain = gains_ref[1:2, :]
+    scale = lax.rsqrt(jnp.mean(mid * mid, axis=-1, keepdims=True) + epsilon)
+    pulled = dh * gain
+    inner = jnp.mean(pulled * mid, axis=-1, keepdims=True)
+    dmid_ref[...] = (
+        cot_ref[...].astype(F32) + scale * pulled - mid * (scale * scale * scale * inner)
+    )
+    dgain_ref[1:2, :] = jnp.sum(dh * mid * scale, axis=0, keepdims=True)
+    for copies in (send_h, send_f, send_df, send_dh):
+        for m in range(1, n_fsdp):
+            copies[m].wait_send()
+
+
+def feed_forward(n_seq, n_fsdp, h_two, middle, cot, gains, gu_all, w_down):
+    rows, width = h_two.shape
+    hidden = gu_all.shape[2]
+    in_vmem = pl.BlockSpec(memory_space=pltpu.VMEM)
+    anywhere = pl.BlockSpec(memory_space=pl.ANY)
+    return pl.pallas_call(
+        functools.partial(ffn_kernel, n_seq, n_fsdp),
+        out_shape=[
+            jax.ShapeDtypeStruct((rows, width), BF16),
+            jax.ShapeDtypeStruct((rows, width), F32),
+            jax.ShapeDtypeStruct((2, width, hidden), BF16),
+            jax.ShapeDtypeStruct((hidden, width), BF16),
+            jax.ShapeDtypeStruct((8, width), F32),
+        ],
+        in_specs=[in_vmem] * 4 + [anywhere] * 2,
+        out_specs=[in_vmem, in_vmem, anywhere, anywhere, in_vmem],
+        scratch_shapes=[
+            pltpu.VMEM((2, width, hidden), BF16),
+            pltpu.VMEM((hidden, width), BF16),
+            pltpu.VMEM((n_fsdp, rows, width), BF16),
+            pltpu.VMEM((n_fsdp, rows, width), BF16),
+            pltpu.VMEM((n_fsdp, rows, hidden), F32),
+            pltpu.VMEM((n_fsdp, rows, hidden), F32),
+            pltpu.VMEM((n_fsdp, rows, hidden), BF16),
+            pltpu.VMEM((n_fsdp, rows, hidden), BF16),
+            pltpu.VMEM((n_fsdp, rows, hidden), BF16),
+            pltpu.VMEM((width, n_fsdp * rows), BF16),
+            pltpu.VMEM((2, n_fsdp, rows, width), BF16),
+            pltpu.VMEM((2, n_fsdp, rows, width), BF16),
+            pltpu.VMEM((rows, width), F32),
+            pltpu.VMEM((3, width, width), BF16),
+            pltpu.SemaphoreType.DMA((3,)),
+            pltpu.SemaphoreType.DMA((4, n_fsdp)),
+            pltpu.SemaphoreType.DMA((4, n_fsdp)),
+            pltpu.SemaphoreType.DMA((3,)),
+        ],
+        compiler_params=pltpu.CompilerParams(
+            collective_id=3, has_side_effects=True, vmem_limit_bytes=60 << 20
+        ),
+        name="feed_forward",
+    )(h_two, middle, cot, gains, gu_all, w_down)
+
+
+def grads_kernel(
+    n_seq, n_fsdp,
+    gu_ref, gd_ref, qkv_ref, wo_ref, gains_ref,
+    fin_gu, fin_d, fin_qkv, fin_wo, gains_out,
+    own_d, own_g, own_q, own_o, c_d, c_g, c_q, c_o,
+    hi_d, hi_g, hi_q, hi_o, lo_d, lo_g, lo_q, lo_o, z_q, z_o, gain_in, gain_line,
+    load_sem, c_send, c_recv, hi_send, hi_recv, lo_send, lo_recv, z_send, z_recv,
+    put_sem, ag_send, ag_recv, gain_send, gain_recv,
+):
+    at = Place(n_seq, n_fsdp)
+    z, c = at.z, at.c
+    hidden = gd_ref.shape[0]
+    width = gd_ref.shape[1]
+    depth = width // n_fsdp
+    heads_width = qkv_ref.shape[1]
+    rows_o = wo_ref.shape[0] // n_fsdp
+    greet([at.plane(k) for k in range(1, n_seq)] + [at.line(m) for m in range(1, n_fsdp)])
+
+    chunks = [("d", i, i == 0) for i in range(2)]
+    chunks += [("g", m, m % 2 == 0) for m in range(n_fsdp)]
+    chunks += [("q", m, True) for m in range(n_fsdp)]
+    chunks += [("o", m, False) for m in range(n_fsdp)]
+    own = {"d": own_d, "g": own_g, "q": own_q, "o": own_o}
+    from_core = {"d": c_d, "g": c_g, "q": c_q, "o": c_o}
+    from_hi = {"d": hi_d, "g": hi_g, "q": hi_q, "o": hi_o}
+    from_lo = {"d": lo_d, "g": lo_g, "q": lo_q, "o": lo_o}
+
+    def core_part(kind, i, core):
+        if kind == "d":
+            size = hidden // 4
+            return gd_ref.at[many(core * (hidden // 2) + i * size, size)]
+        to = flip(z, i, 2)
+        if kind == "g":
+            return gu_ref.at[core, many(to * depth, depth)]
+        if kind == "q":
+            return qkv_ref.at[many(to * depth + core * (depth // 2), depth // 2)]
+        return wo_ref.at[many(to * rows_o + core * (rows_o // 2), rows_o // 2)]
+
+    def hi_part(kind, hi):
+        if kind == "d":
+            return many(hi * (hidden // 8), hidden // 8), slice(None)
+        if kind == "g":
+            return many(hi * (depth // 2), depth // 2), slice(None)
+        if kind == "q":
+            return slice(None), lanes(hi * (heads_width // 2), heads_width // 2)
+        return many(hi * (rows_o // 4), rows_o // 4), slice(None)
+
+    def lo_part(kind, hi, lo):
+        if kind == "d":
+            return many(hi * (hidden // 8) + lo * (hidden // 16), hidden // 16), slice(None)
+        if kind == "g":
+            return (
+                many(hi * (depth // 2), depth // 2),
+                lanes(lo * (hidden // 2), hidden // 2),
+            )
+        if kind == "q":
+            start = hi * (heads_width // 2) + lo * (heads_width // 4)
+            return slice(None), lanes(start, heads_width // 4)
+        return many(hi * (rows_o // 4) + lo * (rows_o // 8), rows_o // 8), slice(None)
+
+    def fin_part(kind, i, where, core):
+        rows_at, cols_at = where
+        if kind == "g":
+            return fin_gu.at[core, i, rows_at, cols_at]
+        ref, base, size = {
+            "d": (fin_d, core * (hidden // 2) + i * (hidden // 4), hidden // 4),
+            "q": (fin_qkv, core * (depth // 2), depth // 2),
+            "o": (fin_wo, core * (rows_o // 2), rows_o // 2),
+        }[kind]
+        if isinstance(rows_at, slice):
+            rows_at = many(base, size)
+        else:
+            rows_at = many(base + rows_at.start, rows_at.size)
+        return ref.at[rows_at, cols_at]
+
+    def add(ref, where, other):
+        rows_at, cols_at = where
+        start = 0 if isinstance(rows_at, slice) else rows_at.start
+        n_rows = other.shape[0]
+        slab = 16
+
+        @pl.loop(0, n_rows // slab)
+        def _(n):
+            here = pl.ds(pl.multiple_of(start + n * slab, slab), slab)
+            there = pl.ds(pl.multiple_of(n * slab, slab), slab)
+            ref[here, cols_at] = (
+                ref[here, cols_at].astype(F32) + other[there, :].astype(F32)
+            ).astype(BF16)
+
+    whole = (slice(None), slice(None))
+    loads, cores, his, los, lines = [], [], [], [], []
+    for j, (kind, i, first_x) in enumerate(chunks):
+        hi, lo, mask_hi, mask_lo = at.halves(first_x)
+        mine = own[kind].at[i]
+        loads.append(pltpu.make_async_copy(core_part(kind, i, c), mine, load_sem.at[j]))
+        cores.append(remote(core_part(kind, i, 1 - c), from_core[kind].at[i],
+                            c_send.at[j], c_recv.at[j], at.plane(1)))
+        his.append(remote(mine.at[hi_part(kind, 1 - hi)], from_hi[kind].at[i],
+                          hi_send.at[j], hi_recv.at[j], at.plane(mask_hi)))
+        los.append(remote(mine.at[lo_part(kind, hi, 1 - lo)], from_lo[kind].at[i],
+                          lo_send.at[j], lo_recv.at[j], at.plane(mask_lo)))
+        piece = mine.at[lo_part(kind, hi, lo)]
+        line = None
+        if kind == "g" and i:
+            line = remote(piece, fin_part(kind, z, lo_part(kind, hi, lo), c),
+                          z_send.at[j], z_recv.at[j], at.line(i))
+        elif kind in "qo" and i:
+            line = remote(piece, {"q": z_q, "o": z_o}[kind].at[i],
+                          z_send.at[j], z_recv.at[j], at.line(i))
+        lines.append(line)
+
+    rounds = [("d", 0, 0), ("d", 1, 1)] + [("g", m, 2 + m) for m in range(n_fsdp)]
+    rounds += [("q", 0, 2 + n_fsdp), ("o", 0, 2 + 2 * n_fsdp)]
+    puts, hands = [], []
+    for r, (kind, i, j) in enumerate(rounds):
+        hi, lo, mask_hi, mask_lo = at.halves(chunks[j][2])
+        which = flip(z, i, 2) if kind == "g" else i
+        piece = fin_part(kind, which, lo_part(kind, hi, lo), c)
+        half = fin_part(kind, which, hi_part(kind, hi), c)
+        full = fin_part(kind, which, whole, c)
+        put = None
+        if not (kind == "g" and i):
+            put = pltpu.make_async_copy(
+                own[kind].at[i].at[lo_part(kind, hi, lo)], piece, put_sem.at[r]
+            )
+        puts.append(put)
+        hands.append([
+            remote(part, part, ag_send.at[r, k], ag_recv.at[r, k], at.plane(mask))
+            for k, (part, mask) in enumerate(((piece, mask_lo), (half, mask_hi), (full, 1)))
+        ])
+
+    gain_copies = [
+        remote(gains_ref, gain_in.at[k], gain_send.at[k], gain_recv.at[k], at.plane(k))
+        for k in range(1, n_seq)
+    ]
+    gain_lines = [
+        remote(gain_line.at[0], gain_line.at[m], gain_send.at[n_seq + m], gain_recv.at[n_seq + m],
+               at.line(m))
+        for m in range(1, n_fsdp)
+    ]
+
+    n = len(chunks)
+    for j in range(n):
+        loads[j].start()
+        cores[j].start()
+    for copy in gain_copies:
+        copy.start()
+
+    def take_core(j):
+        kind, i, _ = chunks[j]
+        loads[j].wait()
+        cores[j].wait_recv()
+        add(own[kind].at[i], whole, from_core[kind].at[i])
+        his[j].start()
+
+    def take_hi(j):
+        kind, i, first_x = chunks[j]
+        hi, lo, _, _ = at.halves(first_x)
+        his[j].wait_recv()
+        add(own[kind].at[i], hi_part(kind, hi), from_hi[kind].at[i])
+        los[j].start()
+
+    def take_lo(j):
+        kind, i, first_x = chunks[j]
+        hi, lo, _, _ = at.halves(first_x)
+        los[j].wait_recv()
+        add(own[kind].at[i], lo_part(kind, hi, lo), from_lo[kind].at[i])
+        if lines[j] is not None:
+            lines[j].start()
+
+    def begin_hand(r):
+        kind, i, j = rounds[r]
+        hi, lo, _, _ = at.halves(chunks[j][2])
+        if kind == "g" and i:
+            lines[j].wait_recv()
+        if kind in "qo":
+            for m in range(1, n_fsdp):
+                lines[j + m].wait_recv()
+                add(own[kind].at[0], lo_part(kind, hi, lo), {"q": z_q, "o": z_o}[kind].at[m])
+        if puts[r] is not None:
+            puts[r].start()
+            puts[r].wait()
+        hands[r][0].start()
+
+    def pass_on(r, k):
+        hands[r][k - 1].wait_recv()
+        hands[r][k].start()
+
+    first = [6, 7, 8, 10, 11, 12] + [15, 19]
+    for t in range(26):
+        for r, when in enumerate(first):
+            if t == when + 4:
+                pass_on(r, 2)
+            if t == when + 2:
+                pass_on(r, 1)
+            if t == when:
+                begin_hand(r)
+        if 0 <= t - 4 < n:
+            take_lo(t - 4)
+        if 0 <= t - 2 < n:
+            take_hi(t - 2)
+        if t < n:
+            take_core(t)
+        if t == 6:
+            total = gains_ref[...]
+            for k, copy in enumerate(gain_copies):
+                copy.wait_recv()
+                total = total + gain_in[k + 1]
+            gain_line[0] = total
+            for copy in gain_lines:
+                copy.start()
+    total = gain_line[0]
+    for m, copy in enumerate(gain_lines):
+        copy.wait_recv()
+        total = total + gain_line[m + 1]
+    gains_out[...] = total
+    for r in range(len(rounds)):
+        hands[r][2].wait_recv()
+        for k in range(3):
+            hands[r][k].wait_send()
+    for j in range(n):
+        cores[j].wait_send()
+        his[j].wait_send()
+        los[j].wait_send()
+        if lines[j] is not None:
+            lines[j].wait_send()
+    for copy in gain_copies + gain_lines:
+        copy.wait_send()
+
+
+def sum_grads(n_seq, n_fsdp, ggu, gd, gqkv, gwo, gains):
+    _, width, hidden = ggu.shape
+    depth = width // n_fsdp
+    heads_width = gqkv.shape[1]
+    rows_o = gwo.shape[0] // n_fsdp
+    in_vmem = pl.BlockSpec(memory_space=pltpu.VMEM)
+    anywhere = pl.BlockSpec(memory_space=pl.ANY)
+    n_chunks = 2 + 3 * n_fsdp
+    n_rounds = 4 + n_fsdp
+
+    def blocks(d, g, q, o):
+        return [
+            pltpu.VMEM((2,) + d, BF16),
+            pltpu.VMEM((n_fsdp,) + g, BF16),
+            pltpu.VMEM((n_fsdp,) + q, BF16),
+            pltpu.VMEM((n_fsdp,) + o, BF16),
+        ]
+
+    core_size = blocks(
+        (hidden // 4, width), (depth, hidden), (depth // 2, heads_width), (rows_o // 2, width)
+    )
+    hi_size = blocks(
+        (hidden // 8, width),
+        (depth // 2, hidden),
+        (depth // 2, heads_width // 2),
+        (rows_o // 4, width),
+    )
+    lo_size = blocks(
+        (hidden // 16, width),
+        (depth // 2, hidden // 2),
+        (depth // 2, heads_width // 4),
+        (rows_o // 8, width),
+    )
+    chunk_sems = pltpu.SemaphoreType.DMA((n_chunks,))
+    return pl.pallas_call(
+        functools.partial(grads_kernel, n_seq, n_fsdp),
+        out_shape=[
+            jax.ShapeDtypeStruct((2, n_fsdp, depth, hidden), BF16),
+            jax.ShapeDtypeStruct((hidden, width), BF16),
+            jax.ShapeDtypeStruct((depth, heads_width), BF16),
+            jax.ShapeDtypeStruct((rows_o, width), BF16),
+            jax.ShapeDtypeStruct(gains.shape, F32),
+        ],
+        in_specs=[anywhere] * 4 + [in_vmem],
+        out_specs=[anywhere] * 4 + [in_vmem],
+        scratch_shapes=core_size
+        + core_size
+        + hi_size
+        + lo_size
+        + lo_size[2:]
+        + [
+            pltpu.VMEM((n_seq,) + gains.shape, F32),
+            pltpu.VMEM((n_fsdp,) + gains.shape, F32),
+        ]
+        + [chunk_sems] * 9
+        + [
+            pltpu.SemaphoreType.DMA((n_rounds,)),
+            pltpu.SemaphoreType.DMA((n_rounds, 3)),
+            pltpu.SemaphoreType.DMA((n_rounds, 3)),
+            pltpu.SemaphoreType.DMA((n_seq + n_fsdp,)),
+            pltpu.SemaphoreType.DMA((n_seq + n_fsdp,)),
+        ],
+        compiler_params=pltpu.CompilerParams(
+            collective_id=4, has_side_effects=True, vmem_limit_bytes=60 << 20
+        ),
+        name="sum_weight_grads",
+    )(ggu, gd, gqkv, gwo, gains)
+
+
+def shards(n_seq, n_fsdp, *args):
+    w_query, w_key, w_output, w_gate = args[4], args[5], args[9], args[12]
+    depth, hidden = w_gate.shape
+    rows_here = args[0].shape[1]
+    heads_width = w_query.shape[1] + 2 * w_key.shape[1]
+    fits = (
+        n_seq == 8
+        and n_fsdp == 4
+        and args[0].shape[0] == 1
+        and depth % 32 == 0
+        and rows_here % 16 == 0
+        and w_output.shape[0] % 128 == 0
+        and heads_width % 512 == 0
+        and w_output.shape[1] % 384 == 0
+        and hidden % n_fsdp == 0
+        and (hidden // n_fsdp) % 16 == 0
+    )
+    return (shards_fused if fits else shards_plain)(*((n_seq, n_fsdp) if fits else ()), *args)
+
+
+def shards_fused(
+    n_seq,
+    n_fsdp,
+    inputs,
+    segments,
+    cotangent,
+    gain_attn_in,
+    w_query,
+    w_key,
+    w_value,
+    gain_query,
+    gain_key,
+    w_output,
+    gain_attn_out,
+    gain_ffn_in,
+    w_gate,
+    w_up,
+    w_down,
+    gain_ffn_out,
+):
+    rows_here, width = inputs.shape[1:]
+    head_width = w_key.shape[1]
+    query_width = w_query.shape[1]
+    head_count = query_width // head_width
+    depth, ffn_width = w_gate.shape
+    share = ffn_width // n_fsdp
+    padded = -(-share // HID_TILE) * HID_TILE
+    reach = (WINDOW - 2 + rows_here) // rows_here
+    score_scale = head_width ** (-0.5)
+    place = lax.axis_index("seq")
+    line = lax.axis_index("fsdp")
+    first_row = place * rows_here
+    tokens = inputs[0].astype(F32)
+    seg_here = segments[0]
+
+    def blocked(weight):
+        by_share = weight.reshape(depth, n_fsdp, share).transpose(1, 0, 2)
+        return jnp.pad(by_share, ((0, 0), (0, 0), (0, padded - share)))
+
+    gu_blocks = jnp.stack([blocked(w_gate), blocked(w_up)])
+    qkv_shard = jnp.concatenate([w_query, w_key, w_value], axis=1)
+    pack_width = -(-depth // 128) * 128
+    gains = (gain_attn_in, gain_attn_out, gain_ffn_in, gain_ffn_out, gain_query, gain_key)
+    pack = jnp.stack([jnp.pad(g, (0, pack_width - g.shape[0])) for g in gains])
+    pack = jnp.pad(pack, ((0, 16 - len(gains)), (0, 0)))
+    segs = jnp.broadcast_to(segments, (8, rows_here))
+    gu_all, qkv_all, wo_all, pack_all, seg_all = spread(
+        n_seq, n_fsdp, gu_blocks, qkv_shard, w_output, pack, segs
+    )
+    g_attn_in, g_attn_out, g_ffn_in, g_ffn_out, g_query, g_key = (
+        pack_all[:, i, : g.shape[0]].reshape(-1).astype(F32) for i, g in enumerate(gains)
+    )
+
+    positions = first_row + jnp.arange(rows_here, dtype=jnp.int32)
+    angles_at = angles(positions - seg_here, head_width)
+    normed_one, pull_one = jax.vjp(norm_rows, tokens, g_attn_in)
+    h_one = normed_one.astype(BF16)
+    qkv_raw = dot_nn(h_one, qkv_all)
+    q_raw = qkv_raw[:, :query_width]
+    k_raw = qkv_raw[:, query_width : query_width + head_width]
+    v_low = qkv_raw[:, query_width + head_width :].astype(BF16)
+
+    def prepare(q_in, k_in, gq_in, gk_in):
+        q_rows = q_in.reshape(q_in.shape[0], head_count, head_width)
+        q_fin = rotate(norm_rows(q_rows, gq_in), angles_at[:, None, :])
+        k_fin = rotate(norm_rows(k_in, gk_in), angles_at)
+        return (q_fin, k_fin)
+
+    (q_fin, k_fin), pull_prep = jax.vjp(prepare, q_raw, k_raw, g_query, g_key)
+    q_low = q_fin.astype(BF16).reshape(rows_here * head_count, head_width)
+    kv_low = jnp.concatenate([k_fin.astype(BF16), v_low], axis=1)
+    kv_rows = from_blocks_behind(n_seq, reach, kv_low).reshape(-1, 2 * head_width)
+    key_rows, value_rows = kv_rows[:, :head_width], kv_rows[:, head_width:]
+    seg_twice = jnp.concatenate([seg_all[:, 0], seg_all[:, 0]], axis=0)
+    key_segs = lax.dynamic_slice(
+        seg_twice, (place + n_seq - reach, jnp.int32(0)), (reach + 1, rows_here)
+    ).reshape(-1)
+    key_place = (
+        first_row - reach * rows_here + jnp.arange((reach + 1) * rows_here, dtype=jnp.int32)
+    )
+    distance = positions[:, None] - key_place[None, :]
+    allowed = (
+        (distance >= 0)
+        & (distance < WINDOW)
+        & (key_place[None, :] >= 0)
+        & (seg_here[:, None] == key_segs[None, :])
+    )
+    scores = (outer_cols(q_low, key_rows) * score_scale).reshape(rows_here, head_count, -1)
+    masked = jnp.where(allowed[:, None, :], scores, masked_value)
+    attn_probs = jax.nn.softmax(masked, axis=-1).reshape(rows_here * head_count, -1)
+    probs_low = attn_probs.astype(BF16)
+    attended = dot_nn(probs_low, value_rows)
+    att_low = attended.reshape(rows_here, query_width).astype(BF16)
+    o_raw = dot_nn(att_low, wo_all)
+    branch_att, pull_att = jax.vjp(norm_rows, o_raw, g_attn_out)
+    middle = tokens + branch_att
+    h_two = norm_rows(middle, g_ffn_in).astype(BF16)
+
+    ffn_gains = jnp.pad(jnp.stack([g_ffn_out, g_ffn_in]), ((0, 6), (0, 0)))
+    outputs, d_middle, ggu, gd, d_ffn_gains = feed_forward(
+        n_seq, n_fsdp, h_two, middle, cotangent[0], ffn_gains, gu_all, w_down
+    )
+
+    d_oraw, d_gattn_out = pull_att(d_middle)
+    d_olow = d_oraw.astype(BF16)
+    grad_wo = inner_rows(att_low, d_olow)
+    d_att_low = outer_cols(d_olow, wo_all).astype(BF16)
+    d_att_low = d_att_low.reshape(rows_here * head_count, head_width)
+    d_probs = outer_cols(d_att_low, value_rows)
+    d_scores = attn_probs * (d_probs - jnp.sum(attn_probs * d_probs, axis=-1, keepdims=True))
+    ds_low = d_scores.astype(BF16)
+    d_qfin = dot_nn(ds_low, key_rows) * score_scale
+    d_kv = jnp.concatenate(
+        [inner_rows(ds_low, q_low) * score_scale, inner_rows(probs_low, d_att_low)], axis=1
+    ).reshape(reach + 1, rows_here, 2 * head_width)
+    d_kv_sum = return_to_blocks(n_seq, reach, d_kv[:reach].astype(BF16), d_kv[reach])
+    d_kfin, d_vsum = d_kv_sum[:, :head_width], d_kv_sum[:, head_width:]
+    d_qraw, d_kraw, d_gquery, d_gkey = pull_prep(
+        (d_qfin.reshape(rows_here, head_count, head_width), d_kfin)
+    )
+    d_qkv = jnp.concatenate([d_qraw, d_kraw, d_vsum], axis=1).astype(BF16)
+    d_hone = outer_cols(d_qkv, qkv_all)
+    grad_qkv = inner_rows(h_one, d_qkv)
+    d_tok_norm, d_gattn_in = pull_one(d_hone)
+    d_inputs = d_middle + d_tok_norm
+
+    def wide(vector):
+        return jnp.pad(vector, (0, width - vector.shape[0]))
+
+    gain_rows = jnp.stack(
+        [d_gattn_in, d_gattn_out, d_ffn_gains[1], d_ffn_gains[0], wide(d_gquery), wide(d_gkey)]
+    )
+    gain_rows = jnp.pad(gain_rows, ((0, 2), (0, 0)))
+    fin_gu, fin_d, fin_qkv, fin_wo, gain_sums = sum_grads(
+        n_seq, n_fsdp, ggu, gd, grad_qkv.astype(BF16), grad_wo.astype(BF16), gain_rows
+    )
+
+    def unblocked(blocks):
+        return blocks[:, :, :share].transpose(1, 0, 2).reshape(depth, ffn_width).astype(F32)
+
+    def mine(row, gain):
+        size = gain.shape[0]
+        return lax.dynamic_slice(gain_sums[row], (line * size,), (size,))
+
+    fin_qkv = fin_qkv.astype(F32)
+    return (
+        outputs[None],
+        d_inputs[None],
+        mine(0, gain_attn_in),
+        fin_qkv[:, :query_width],
+        fin_qkv[:, query_width : query_width + head_width],
+        fin_qkv[:, query_width + head_width :],
+        mine(4, gain_query),
+        mine(5, gain_key),
+        fin_wo.astype(F32),
+        mine(1, gain_attn_out),
+        mine(2, gain_ffn_in),
+        unblocked(fin_gu[0]),
+        unblocked(fin_gu[1]),
+        fin_d[:share].astype(F32),
+        mine(3, gain_ffn_out),
+    )
+
+
 def solution(mesh):
     placed = (
         P("fsdp", "seq", None),
@@ -364,7 +1345,7 @@
         P("fsdp"),
     )
     return jax.shard_map(
-        shards,
+        functools.partial(shards, mesh.shape["seq"], mesh.shape["fsdp"]),
         mesh=mesh,
         in_specs=placed,
         out_specs=(

time: 3190 us -> 604 us (0.19)
  the two profiles are of different devices: /device:TPU:9 before, /device:TPU:0 now
where the time goes in v1:
time: 604 us; the launch traced here: 594 us
  Pallas kernels  429 us (71%)
  local copies, waits for them, and re-layouts  101 us (17%)
  other arithmetic  42.4 us (7%)
  matrix products  19.5 us (3%)
    pallas_call x1, Pallas kernels, sum_grads(): pl.pallas_call(functools.partial(grads_kernel, n_seq, n_fsdp), out_shape=...  167 us
    pallas_call x1, Pallas kernels, feed_forward(): pl.pallas_call(functools.partial(ffn_kernel, n_seq, n_fsdp), out_shape=[j...  123 us
    pallas_call x1, Pallas kernels, spread(): pl.pallas_call(functools.partial(spread_kernel, n_seq, n_fsdp), out_shape...  115 us
    convert_element_type x4, local copies, waits for them, and re-layouts, unblocked(): blocks[:, :, :share].transpose(1, 0, 2).reshape(depth, ffn_width)  45.2 us
    reshape x4, local copies, waits for them, and re-layouts, blocked(): by_share = weight.reshape(depth, n_fsdp, share).transpose(1, 0, 2)  27.3 us
    pallas_call x1, Pallas kernels, from_blocks_behind(): pl.pallas_call(functools.partial(behind_kernel, n_seq, reach), out_shape=...  14.2 us

profile of v1, /device:TPU:0, one launch (start us, length us, event | category | flops | bytes accessed | tf_op | source)
XLA Modules:
  0.0 593.8 jit_solution(4800250853769651185)
XLA Ops:
  0.6 9.9 %reshape.384 = bf16[288,4,1728]{2,1,0:T(4,128)(2,1)} reshape(bf16[288,6912]{1,0:T(8,128)(2,1)} %param.29) | data formatting | bytes 7962624 | tf_op jit(solution)/shard_map/reshape | solution.py:1200
  10.5 4.7 copy.62
  15.2 9.9 %reshape.383 = bf16[288,4,1728]{2,1,0:T(4,128)(2,1)} reshape(bf16[288,6912]{1,0:T(8,128)(2,1)} %param.28) | data formatting | bytes 7962624 | tf_op jit(solution)/shard_map/reshape | solution.py:1200
  25.1 2.8 copy.63
  28.5 2.3 pad_bitcast_fusion
  30.9 6.1 %pad_maximum_fusion.gu_ref = bf16[2,4,288,1792]{3,2,1,0:T(8,128)(2,1)} fusion(bf16[1,4,288,1792]{3,2,1,0:T(8,128)(2,1)S(1)} %get-tuple-element.93, bf16[1,4,288,1792]{3,2,1,0:T(8,128)(2,1)} %get-tuple-element.94), kind=kLoop, calls=%fused_computation | loop fusion | flops 4128768 | bytes 16515072 | tf_op jit(solution)/shard_map/stack | solution.py:1203
  37.1 1.0 pad_maximum_fusion.1.qkv_ref
  39.5 114.8 %spread_weights.1 = (bf16[2,1152,1792]{2,1,0:T(8,128)(2,1)}, bf16[1152,1536]{1,0:T(8,128)(2,1)}, bf16[1024,1152]{1,0:T(8,128)(2,1)}, bf16[4,16,384]{2,1,0:T(8,128)(2,1)}, s32[8,8,128]{2,1,0:T(8,128)}) custom-call(bf16[2,4,288,1792]{3,2,1,0:T(8,128)(2,1)} %pad_maximum_fusion.gu_ref, bf16[288,1536]{1,0:T(8,128)(2,1)} %pad_maximum_fusion.1.qkv_ref, ...), custom_call_target="tpu_custom_call" | custom-call | tf_op jit(solution)/shard_map/spread_weights/pallas_call | solution.py:522
  154.2 0.9 convert_reduce_fusion
  155.5 2.7 fusion.37
  158.4 0.8 convert_reduce_fusion.4
  160.5 14.2 %keys_values_behind.1 = bf16[5,128,512]{2,1,0:T(8,128)(2,1)} custom-call(bf16[128,512]{1,0:T(8,128)(2,1)} %pad_maximum_fusion.9.kv_ref), custom_call_target="tpu_custom_call" | custom-call | tf_op jit(solution)/shard_map/keys_values_behind/pallas_call | solution.py:563
  179.2 1.2 convolution_convert_fusion.3
  180.4 1.1 convert_element_type.178
  183.0 1.0 multiply_reduce_fusion.3
  184.0 1.9 multiply_convert_fusion.1.h_ref
  185.9 0.9 slice_reduce_fusion
  187.6 122.6 %feed_forward.1 = (bf16[128,1152]{1,0:T(8,128)(2,1)}, f32[128,1152]{1,0:T(8,128)}, bf16[2,1152,1792]{2,1,0:T(8,128)(2,1)}, bf16[1792,1152]{1,0:T(8,128)(2,1)}, f32[8,1152]{1,0:T(8,128)}) custom-call(bf16[128,1152]{1,0:T(8,128)(2,1)} %multiply_convert_fusion.1.h_ref, f32[128,1152]{1,0:T(8,128)} %get-tuple-element.61.mid_ref, bf16[128,1152]{1,0:T(8,128)(2,1)} %bitcast.70, ...), custom_call_target="tpu_custom_call" | custom-call | tf_op jit(solution)/shard_map/feed_forward/pallas_call | solution.py:807
  310.3 2.0 multiply_reduce_fusion.1
  312.3 1.4 fusion.9
  313.7 1.6 convolution_convert_fusion.2
  315.3 1.1 reshape.387
  316.5 2.0 multiply_reduce_fusion
  320.5 0.8 fusion.4
  322.1 10.6 %keys_values_return.1 = f32[128,512]{1,0:T(8,128)} custom-call(bf16[4,128,512]{2,1,0:T(8,128)(2,1)} %bitcast.62, f32[128,512]{1,0:T(8,128)} %pad_maximum_fusion.3.own_ref), custom_call_target="tpu_custom_call" | custom-call | tf_op jit(solution)/shard_map/keys_values_return/pallas_call | solution.py:594
  332.8 0.9 slice.209
  333.7 1.2 fusion.43
  334.9 1.0 multiply_reduce_fusion.8
  336.0 1.0 fusion.27
  337.0 1.3 convolution_multiply_fusion.2
  339.9 3.4 fusion.8
  343.3 1.0 fusion.11
  344.3 3.0 convolution_convert_fusion.qkv_ref
  347.3 2.2 convolution_convert_fusion.1.wo_ref
  349.5 0.9 fusion.69
  351.1 166.5 %sum_weight_grads.1 = (bf16[2,4,288,1792]{3,2,1,0:T(8,128)(2,1)}, bf16[1792,1152]{1,0:T(8,128)(2,1)}, bf16[288,1536]{1,0:T(8,128)(2,1)}, bf16[256,1152]{1,0:T(8,128)(2,1)}, f32[8,1152]{1,0:T(8,128)}) custom-call(bf16[2,1152,1792]{2,1,0:T(8,128)(2,1)} %get-tuple-element.37.gu_ref, bf16[1792,1152]{1,0:T(8,128)(2,1)} %get-tuple-element.38.gd_ref, ...), custom_call_target="tpu_custom_call" | custom-call | tf_op jit(solution)/shard_map/sum_weight_grads/pallas_call | solution.py:1109
  517.6 1.1 fusion.68
  519.4 2.2 slice.161
  521.6 0.9 fusion.67
  523.6 1.1 convert_element_type.193
  526.0 5.1 slice_bitcast_fusion
  531.2 3.8 convert_bitcast_fusion.1
  535.0 11.8 %copy.55 = f32[288,4,1728]{2,1,0:T(4,128)} copy(f32[288,4,1728]{2,0,1:T(8,128)} %convert_bitcast_fusion.1) | data formatting | bytes 15925248 | tf_op jit(solution)/shard_map/convert_element_type | solution.py:1302
  546.9 10.8 %reshape.398 = f32[288,6912]{1,0:T(8,128)} reshape(f32[288,4,1728]{2,1,0:T(4,128)} %copy.55) | data formatting | bytes 15925248 | tf_op jit(solution)/shard_map/convert_element_type | solution.py:1302
  557.7 6.0 %convert_bitcast_fusion = f32[288,4,1728]{2,0,1:T(8,128)} fusion(bf16[4,288,1792]{2,1,0:T(8,128)(2,1)} %get-tuple-element.62), kind=kLoop, calls=%fused_computation.1 | loop fusion | flops 1990656 | bytes 11943936 | tf_op jit(solution)/shard_map/convert_element_type | solution.py:1302
  563.7 11.8 %copy.56 = f32[288,4,1728]{2,1,0:T(4,128)} copy(f32[288,4,1728]{2,0,1:T(8,128)} %convert_bitcast_fusion) | data formatting | bytes 15925248 | tf_op jit(solution)/shard_map/convert_element_type | solution.py:1302
  575.6 10.7 %reshape.399 = f32[288,6912]{1,0:T(8,128)} reshape(f32[288,4,1728]{2,1,0:T(4,128)} %copy.56) | data formatting | bytes 15925248 | tf_op jit(solution)/shard_map/convert_element_type | solution.py:1302
  586.2 5.9 slice_convert_fusion
  (197 shorter events, 19.5 us)
Async XLA Ops:
  25.1 3.4 copy-start
  30.8 6.2 %copy-start.17 = (bf16[288,1024]{1,0:T(8,128)(2,1)S(1)}, bf16[288,1024]{1,0:T(8,128)(2,1)}, u32[]{:S(2)}) copy-start(bf16[288,1024]{1,0:T(8,128)(2,1)} %param.20) | copy-start | bytes 1769476
  30.8 6.2 %copy-start.20 = (bf16[288,256]{1,0:T(8,128)(2,1)S(1)}, bf16[288,256]{1,0:T(8,128)(2,1)}, u32[]{:S(2)}) copy-start(bf16[288,256]{1,0:T(8,128)(2,1)} %param.22) | copy-start | bytes 442372
  30.8 6.2 %copy-start.21 = (bf16[288,256]{1,0:T(8,128)(2,1)S(1)}, bf16[288,256]{1,0:T(8,128)(2,1)}, u32[]{:S(2)}) copy-start(bf16[288,256]{1,0:T(8,128)(2,1)} %param.21) | copy-start | bytes 442372
  30.8 7.2 %copy-start.47 = (bf16[288]{0:T(512)(128)(2,1)S(1)}, bf16[288]{0:T(512)(128)(2,1)}, u32[]{:S(2)}) copy-start(bf16[288]{0:T(512)(128)(2,1)} %param.19) | copy-start | bytes 1732
  30.8 7.2 %copy-start.48 = (bf16[288]{0:T(512)(128)(2,1)S(1)}, bf16[288]{0:T(512)(128)(2,1)}, u32[]{:S(2)}) copy-start(bf16[288]{0:T(512)(128)(2,1)} %param.26) | copy-start | bytes 1732
  30.8 7.2 %copy-start.49 = (bf16[288]{0:T(512)(128)(2,1)S(1)}, bf16[288]{0:T(512)(128)(2,1)}, u32[]{:S(2)}) copy-start(bf16[288]{0:T(512)(128)(2,1)} %param.27) | copy-start | bytes 1732
  30.9 7.3 %copy-start.50 = (bf16[288]{0:T(512)(128)(2,1)S(1)}, bf16[288]{0:T(512)(128)(2,1)}, u32[]{:S(2)}) copy-start(bf16[288]{0:T(512)(128)(2,1)} %param.31) | copy-start | bytes 1732
  30.9 7.3 %copy-start.55 = (bf16[64]{0:T(256)(128)(2,1)S(1)}, bf16[64]{0:T(256)(128)(2,1)}, u32[]{:S(2)}) copy-start(bf16[64]{0:T(256)(128)(2,1)} %param.23) | copy-start | bytes 388
  30.9 7.3 %copy-start.56 = (bf16[64]{0:T(256)(128)(2,1)S(1)}, bf16[64]{0:T(256)(128)(2,1)}, u32[]{:S(2)}) copy-start(bf16[64]{0:T(256)(128)(2,1)} %param.24) | copy-start | bytes 388
  30.9 8.0 %copy-start.44 = (s32[1,128]{1,0:T(1,128)S(1)}, s32[1,128]{1,0:T(1,128)}, u32[]{:S(2)}) copy-start(s32[1,128]{1,0:T(1,128)} %param.17) | copy-start | bytes 1540
  39.5 115.9 %copy-start.1 = (bf16[1,128,1152]{2,1,0:T(8,128)(2,1)S(1)}, bf16[1,128,1152]{2,1,0:T(8,128)(2,1)}, u32[]{:S(2)}) copy-start(bf16[1,128,1152]{2,1,0:T(8,128)(2,1)} %param.16) | copy-start | bytes 884740
  155.5 2.8 copy-start.51
  155.5 2.8 copy-start.33
  158.2 18.4 %copy-start.7 = (f32[128,1536]{1,0:T(8,128)}, f32[128,1536]{1,0:T(8,128)S(1)}, u32[]{:S(2)}) copy-start(f32[128,1536]{1,0:T(8,128)S(1)} %fusion.37) | copy-start | bytes 2359300
  158.3 18.4 %copy-start.45 = (f32[128]{0:T(128)}, f32[128]{0:T(128)S(1)}, u32[]{:S(2)}) copy-start(f32[128]{0:T(128)S(1)} %multiply_power_fusion) | copy-start | bytes 1540
  158.3 16.4 %copy-start.42 = (f32[128]{0:T(128)}, f32[128]{0:T(128)S(1)}, u32[]{:S(2)}) copy-start(f32[128]{0:T(128)S(1)} %get-tuple-element.95) | copy-start | bytes 1540
  159.3 17.4 %copy-start.29 = (f32[256]{0:T(256)}, f32[256]{0:T(256)S(1)}, u32[]{:S(2)}) copy-start(f32[256]{0:T(256)S(1)} %reshape.395) | copy-start | bytes 3076
  159.4 16.2 %copy-start.53 = (f32[128]{0:T(128)}, f32[128]{0:T(128)S(1)}, u32[]{:S(2)}) copy-start(f32[128]{0:T(128)S(1)} %multiply_reduce_fusion.10) | copy-start | bytes 1540
  159.4 16.1 %copy-start.40 = (f32[128]{0:T(128)}, f32[128]{0:T(128)S(1)}, u32[]{:S(2)}) copy-start(f32[128]{0:T(128)S(1)} %fusion.59) | copy-start | bytes 1540
  159.8 17.6 %copy-start.13 = (f32[128,128]{1,0:T(8,128)}, f32[128,128]{1,0:T(8,128)S(1)}, u32[]{:S(2)}) copy-start(f32[128,128]{1,0:T(8,128)S(1)} %get-tuple-element.82) | copy-start | bytes 196612
  159.8 17.6 %copy-start.15 = (f32[128,128]{1,0:T(8,128)}, f32[128,128]{1,0:T(8,128)S(1)}, u32[]{:S(2)}) copy-start(f32[128,128]{1,0:T(8,128)S(1)} %get-tuple-element.83) | copy-start | bytes 196612
  176.8 1.3 copy-start.31
  177.0 1.5 copy-start.27
  177.4 1.8 copy-start.12
  178.1 2.3 copy-start.35
  179.2 2.3 copy-start.2
  181.5 2.5 copy-start.9
  182.9 127.3 %copy-start.39 = (f32[128]{0:T(128)}, f32[128]{0:T(128)S(1)}, u32[]{:S(2)}) copy-start(f32[128]{0:T(128)S(1)} %fusion.60) | copy-start | bytes 1540
  313.7 2.7 copy-start.36
  313.7 2.7 copy-start.38
  316.4 2.1 copy-start.6
  320.5 13.2 %copy-start.43 = (f32[128]{0:T(128)S(1)}, f32[128]{0:T(128)}, u32[]{:S(2)}) copy-start(f32[128]{0:T(128)} %copy-done.42) | copy-start | bytes 1540
  320.5 13.2 %copy-start.46 = (f32[128]{0:T(128)S(1)}, f32[128]{0:T(128)}, u32[]{:S(2)}) copy-start(f32[128]{0:T(128)} %copy-done.45) | copy-start | bytes 1540
  320.5 14.4 %copy-start.30 = (f32[256]{0:T(256)S(1)}, f32[256]{0:T(256)}, u32[]{:S(2)}) copy-start(f32[256]{0:T(256)} %copy-done.29) | copy-start | bytes 3076
  320.5 14.4 %copy-start.41 = (f32[128]{0:T(128)S(1)}, f32[128]{0:T(128)}, u32[]{:S(2)}) copy-start(f32[128]{0:T(128)} %copy-done.40) | copy-start | bytes 1540
  320.5 15.4 %copy-start.54 = (f32[128]{0:T(128)S(1)}, f32[128]{0:T(128)}, u32[]{:S(2)}) copy-start(f32[128]{0:T(128)} %copy-done.53) | copy-start | bytes 1540
  322.1 16.4 %copy-start.14 = (f32[128,128]{1,0:T(8,128)S(1)}, f32[128,128]{1,0:T(8,128)}, u32[]{:S(2)}) copy-start(f32[128,128]{1,0:T(8,128)} %copy-done.13) | copy-start | bytes 196612
  322.1 16.4 %copy-start.16 = (f32[128,128]{1,0:T(8,128)S(1)}, f32[128,128]{1,0:T(8,128)}, u32[]{:S(2)}) copy-start(f32[128,128]{1,0:T(8,128)} %copy-done.15) | copy-start | bytes 196612
  332.8 6.0 %copy-start.32 = (f32[256]{0:T(256)S(1)}, f32[256]{0:T(256)}, u32[]{:S(2)}) copy-start(f32[256]{0:T(256)} %copy-done.31) | copy-start | bytes 3076
  337.0 2.3 copy-start.28
  339.8 3.4 copy-start.52
  339.8 3.4 copy-start.4
  344.3 3.0 copy-start.10
  347.3 2.2 copy-start.26
  517.6 4.0 copy-start.8
  517.6 6.0 %copy-start.18 = (bf16[256,1152]{1,0:T(8,128)(2,1)S(1)}, bf16[256,1152]{1,0:T(8,128)(2,1)}, u32[]{:S(2)}) copy-start(bf16[256,1152]{1,0:T(8,128)(2,1)} %get-tuple-element.42) | copy-start | bytes 1769476
  586.2 6.6 %copy-start.19 = (bf16[128,1152]{1,0:T(8,128)(2,1)S(1)}, bf16[128,1152]{1,0:T(8,128)(2,1)}, u32[]{:S(2)}) copy-start(bf16[128,1152]{1,0:T(8,128)(2,1)} %get-tuple-element.35) | copy-start | bytes 884740
  (9 other events, 9.1 us)

commit v2 on v0

--- a/solution.py
+++ b/solution.py
@@ -1,6 +1,10 @@
+import functools
+
 import jax
 import jax.numpy as jnp
 from jax import lax
+from jax.experimental import pallas as pl
+from jax.experimental.pallas import tpu as pltpu
 from jax.sharding import PartitionSpec as P
 
 WINDOW = 512
@@ -60,7 +64,7 @@
     )
 
 
-def shards(
+def shards_plain(
     inputs,
     segments,
     cotangent,
@@ -344,6 +348,1158 @@
     )
 
 
+MESH = pl.DeviceIdType.MESH
+BF16 = jnp.bfloat16
+F32 = jnp.float32
+GELU_RATE = 0.7978845608028654
+GELU_CUBE = 0.044715
+HID_TILE = 256
+ATT_IN, ATT_OUT, FFN_IN, FFN_OUT, QUERY, KEY = range(6)
+
+
+def bit_of(value, mask):
+    return lax.rem(lax.div(value, mask), 2)
+
+
+def flip(value, masks, bits):
+    for b in range(bits):
+        if (masks >> b) & 1:
+            value = value + (1 << b) * (1 - 2 * bit_of(value, 1 << b))
+    return value
+
+
+def greet(devices):
+    barrier = pltpu.get_barrier_semaphore()
+    for device in devices:
+        pl.semaphore_signal(barrier, inc=1, device_id=device, device_id_type=MESH)
+    pl.semaphore_wait(barrier, len(devices))
+
+
+def remote(src, dst, send, recv, device):
+    return pltpu.make_async_remote_copy(
+        src_ref=src, dst_ref=dst, send_sem=send, recv_sem=recv,
+        device_id=device, device_id_type=MESH,
+    )
+
+
+def many(offset, size):
+    return pl.ds(pl.multiple_of(offset, size if size % 128 == 0 else 16), size)
+
+
+def lanes(offset, size):
+    return pl.ds(pl.multiple_of(offset, 128), size)
+
+
+def window_start(z, share):
+    if isinstance(z, int):
+        return z * share // 128 * 128
+    return lax.div(z * share, 128) * 128
+
+
+def window_width(share, n_fsdp):
+    widest = max((z + 1) * share - window_start(z, share) for z in range(n_fsdp))
+    return -(-widest // HID_TILE) * HID_TILE
+
+
+def dot_nt(left, right):
+    return lax.dot_general(left, right, (((1,), (1,)), ((), ())), preferred_element_type=F32)
+
+
+def dot_nn(left, right):
+    return jnp.dot(left, right, preferred_element_type=F32)
+
+
+def norm_scale(rows_in):
+    return lax.rsqrt(jnp.mean(rows_in * rows_in, axis=-1, keepdims=True) + epsilon)
+
+
+def norm_back(rows_in, gain, scale, upstream):
+    pulled = upstream * gain
+    inner = jnp.mean(pulled * rows_in, axis=-1, keepdims=True)
+    d_rows = scale * pulled - rows_in * (scale * scale * scale * inner)
+    return d_rows, jnp.sum(upstream * rows_in * scale, axis=0, keepdims=True)
+
+
+def turn(rows_in, cosine, sine_part):
+    half = rows_in.shape[-1] // 2
+    lower, upper = rows_in[:, :half], rows_in[:, half:]
+    return jnp.concatenate(
+        [lower * cosine - upper * sine_part, upper * cosine + lower * sine_part], axis=-1
+    )
+
+
+class Place:
+    def __init__(self):
+        self.s = lax.axis_index("seq")
+        self.z = lax.axis_index("fsdp")
+        self.c = bit_of(self.s, 1)
+        self.x = bit_of(self.s, 2)
+        self.y = bit_of(self.s, 4)
+
+    def plane(self, masks):
+        return (flip(self.s, masks, 3), self.z)
+
+    def line(self, masks):
+        return (self.s, flip(self.z, masks, 2))
+
+    def halves(self, first_x):
+        if first_x:
+            return self.x, self.y, 2, 4
+        return self.y, self.x, 4, 2
+
+
+def layer_kernel(
+    n_seq, n_fsdp, share, reach, head_count,
+    x_ref, cot_ref, rates_ref, pack_ref, seg_ref,
+    gate_ref, up_ref, wq_ref, wk_ref, wv_ref, wo_ref, wd_ref,
+    out_ref, dx_out, gains_out, fin_gu, fin_d, fin_qkv, fin_wo,
+    qkv_s, wo_s, w_in, w_down, pack_all, seg_all, gains, allowed, turns,
+    h1_s, raw_s, q_s, kv_own, kv_s, p_s, att_s, o_s, mid_s,
+    h_all, df_all, bent_s, act, d_in, h_turn, part_out, part_in, relay_in, total,
+    own_d, own_g, own_o, own_q, hi_d, hi_g, hi_o, hi_q, lo_d, lo_g, lo_o, lo_q, line_o, line_q,
+    do_s, datt_s, dkv_s, dkv_send, dkv_came, dqkv_s, dgains, gain_in, gain_line,
+    w_send, w_recv, own_sem, pack_send, pack_recv, seg_send, seg_recv, kv_send, kv_recv,
+    ex_send, ex_recv, relay_sem, dkv_ssem, dkv_rsem,
+    c_send, c_recv, hi_send, hi_recv, lo_send, lo_recv, z_send, z_recv, oq_send, oq_recv,
+    put_sem, ag_send, ag_recv, gain_send, gain_recv,
+):
+    at = Place()
+    s, z, c = at.s, at.z, at.c
+    rows, width = x_ref.shape
+    depth = width // n_fsdp
+    hidden = w_in.shape[2]
+    head_width = wk_ref.shape[1]
+    query_width = head_count * head_width
+    heads_width = query_width + 2 * head_width
+    rows_o = wo_ref.shape[0]
+    n_hid = hidden // HID_TILE
+    third = width // 3
+    middle_z = (z > 0) & (z < n_fsdp - 1)
+    tokens = n_fsdp * rows
+
+    def hid(n):
+        return lanes(n * HID_TILE, HID_TILE)
+
+    def outs(n):
+        return lanes(n * third, third)
+
+    skipped = z * share - window_start(z, share)
+    spare = hidden - share
+    if spare:
+        w_down[pl.ds(0, spare)] = jnp.zeros((spare, width), BF16)
+        w_down[pl.ds(share, spare)] = jnp.zeros((spare, width), BF16)
+    here_z = many(z * depth, depth)
+    own_copies = [
+        pltpu.make_async_copy(src, dst, own_sem.at[i])
+        for i, (src, dst) in enumerate((
+            (wq_ref, qkv_s.at[here_z, pl.ds(0, query_width)]),
+            (wk_ref, qkv_s.at[here_z, pl.ds(query_width, head_width)]),
+            (wv_ref, qkv_s.at[here_z, pl.ds(query_width + head_width, head_width)]),
+            (wo_ref, wo_s.at[many(z * rows_o, rows_o)]),
+            (wd_ref, w_down.at[many(skipped, share)]),
+            (gate_ref.at[:, lanes(window_start(z, share), hidden)], w_in.at[0, here_z]),
+            (up_ref.at[:, lanes(window_start(z, share), hidden)], w_in.at[1, here_z]),
+        ))
+    ]
+    seg_all[s] = jnp.broadcast_to(seg_ref[...], seg_all.shape[1:])
+    pack_all[z] = jnp.broadcast_to(pack_ref[...], pack_all.shape[1:])
+    greet([at.plane(k) for k in range(1, n_seq)] + [at.line(m) for m in range(1, n_fsdp)])
+
+    packs = [
+        remote(pack_all.at[z], pack_all.at[z], pack_send.at[m], pack_recv.at[m], at.line(m))
+        for m in range(1, n_fsdp)
+    ]
+    seg_copies = [
+        remote(seg_all.at[s], seg_all.at[s], seg_send.at[k], seg_recv.at[k], at.plane(k))
+        for k in range(1, n_seq)
+    ]
+    kv_copies = [
+        remote(kv_own, kv_s.at[reach - o], kv_send.at[o - 1], kv_recv.at[o - 1],
+               (lax.rem(s + o, n_seq), z))
+        for o in range(1, reach + 1)
+    ]
+
+    def w_region(kind, whose, hi, lo, level):
+        base = whose * depth
+        if kind == "q":
+            cols = (
+                lanes(hi * (query_width // 2) + lo * (query_width // 4), query_width // 4),
+                lanes(hi * (query_width // 2), query_width // 2),
+                pl.ds(0, query_width),
+            )[level]
+            return qkv_s.at[many(base + c * (depth // 2), depth // 2), cols]
+        if kind == "kv":
+            start = query_width + c * head_width
+            if level == 0:
+                start = start + lo * (head_width // 2)
+            cols = lanes(start, head_width if level else head_width // 2)
+            if level == 2:
+                return qkv_s.at[many(base, depth), cols]
+            return qkv_s.at[many(base + hi * (depth // 2), depth // 2), cols]
+        if kind == "wo":
+            start = whose * rows_o + c * (rows_o // 2)
+            if level < 2:
+                start = start + hi * (rows_o // 4)
+            if level < 1:
+                start = start + lo * (rows_o // 8)
+            return wo_s.at[many(start, rows_o // (8, 4, 2)[level])]
+        if level == 2:
+            return w_in.at[c, many(base, depth)]
+        here = many(base + hi * (depth // 2), depth // 2)
+        if level == 1:
+            return w_in.at[c, here]
+        return w_in.at[c, here, lanes(lo * (hidden // 2), hidden // 2)]
+
+    def w_sources(kind, to, hi, lo):
+        if kind == "q":
+            cols = lanes(hi * (query_width // 2) + lo * (query_width // 4), query_width // 4)
+            return [wq_ref.at[many(c * (depth // 2), depth // 2), cols]]
+        if kind == "wo":
+            start = c * (rows_o // 2) + hi * (rows_o // 4) + lo * (rows_o // 8)
+            return [wo_ref.at[many(start, rows_o // 8)]]
+        here = many(hi * (depth // 2), depth // 2)
+        if kind == "kv":
+            cols = lanes(lo * (head_width // 2), head_width // 2)
+            return [ref.at[here, cols] for ref in (wk_ref, wv_ref)]
+        cols = lanes(window_start(to, share) + lo * (hidden // 2), hidden // 2)
+        return [ref.at[here, cols] for ref in (gate_ref, up_ref)]
+
+    items = []
+    for k, kind in enumerate(("q", "kv", "wo", "gu")):
+        for m in range(1, n_fsdp):
+            items.append((kind, m, (m % 2 == 1) != (kind in ("kv", "wo"))))
+    steps, starts = [], []
+    for i, (kind, m, first_x) in enumerate(items):
+        hi, lo, mask_hi, mask_lo = at.halves(first_x)
+        there = flip(z, m, 2)
+        firsts = [
+            remote(src, w_region(kind, z, hi, lo, 0), w_send.at[i, 0], w_recv.at[i, 0], at.line(m))
+            for src in w_sources(kind, there, hi, lo)
+        ]
+        starts.append(firsts)
+        steps.append([firsts[0]] + [
+            remote(w_region(kind, there, hi, lo, k), w_region(kind, there, hi, lo, k),
+                   w_send.at[i, k + 1], w_recv.at[i, k + 1], at.plane(mask))
+            for k, mask in enumerate((mask_lo, mask_hi, 1))
+        ])
+
+    def begin_weight(i):
+        if len(starts[i]) == 1:
+            starts[i][0].start()
+        else:
+            for core, first in enumerate(starts[i]):
+                pl.when(c == core)(first.start)
+
+    def move_weight(i, stage):
+        steps[i][stage - 1].wait_recv()
+        steps[i][stage].start()
+
+    n_items = len(items)
+    n_att = n_items - (n_fsdp - 1)
+    n_qkv = 2 * (n_fsdp - 1)
+    for copy in packs + seg_copies:
+        copy.start()
+    for i in range(n_att):
+        begin_weight(i)
+    for copy in own_copies:
+        copy.start()
+
+    for copy in seg_copies:
+        copy.wait_recv()
+    across = lax.broadcasted_iota(jnp.int32, (rows, rows), 0)
+    along = lax.broadcasted_iota(jnp.int32, (rows, rows), 1)
+    seg_here = jnp.broadcast_to(seg_ref[...].astype(F32), (rows, rows)).T
+    for o in range(reach, -1, -1):
+        key_seg = seg_all[lax.rem(s + n_seq - o, n_seq), 0:1, :].astype(F32)
+        apart = across - along + o * rows
+        fine = (apart >= 0) & (apart < WINDOW) & (seg_here == key_seg) & (s >= o)
+        allowed[:, pl.ds((reach - o) * rows, rows)] = jnp.where(fine, 1.0, 0.0)
+    angle = ((s * rows + across).astype(F32) - seg_here) * rates_ref[...]
+    turns[0] = jnp.cos(angle)
+    turns[1] = jnp.sin(angle)
+    for copy in packs:
+        copy.wait_recv()
+    gains[...] = jnp.zeros(gains.shape, F32)
+    start = 0
+    for row in range(6):
+        size = (depth if row < QUERY else head_width // n_fsdp)
+        for block in range(n_fsdp):
+            gains[row : row + 1, block * size : (block + 1) * size] = pack_all[
+                block, 0:1, start : start + size
+            ]
+        start += size
+
+    def gain(row):
+        return gains[row : row + 1, : (width if row < QUERY else head_width)]
+
+    x = x_ref[...].astype(F32)
+    h1_s[...] = (x * norm_scale(x) * gain(ATT_IN)).astype(BF16)
+
+    for t in range(n_att + 2):
+        for stage in (3, 2, 1):
+            i = t - (stage - 1)
+            if 0 <= i < n_att:
+                move_weight(i, stage)
+        if t == n_att - 1:
+            for i in range(n_att, n_items):
+                begin_weight(i)
+    for i in range(n_qkv):
+        steps[i][3].wait_recv()
+    for copy in own_copies[:3]:
+        copy.wait()
+
+    gu_moves = []
+    for t in range(n_fsdp + 1):
+        gu_moves.append(
+            [(n_att + t - (k - 1), k) for k in (3, 2, 1) if 0 <= t - (k - 1) < n_fsdp - 1]
+        )
+
+    def move_gu(t):
+        for i, stage in gu_moves[t]:
+            move_weight(i, stage)
+
+    tile = heads_width // 3
+
+    @pl.loop(0, 3)
+    def _(n):
+        cols = lanes(n * tile, tile)
+        raw_s[:, cols] = dot_nn(h1_s[...], qkv_s[:, cols])
+
+    k_raw = raw_s[:, query_width : query_width + head_width]
+    kv_own[:, :head_width] = turn(
+        k_raw * norm_scale(k_raw) * gain(KEY), turns[0], turns[1]
+    ).astype(BF16)
+    kv_own[:, head_width:] = raw_s[:, query_width + head_width :].astype(BF16)
+    for copy in kv_copies:
+        copy.start()
+    kv_s[reach] = kv_own[...]
+    for h in range(head_count):
+        q_raw = raw_s[:, h * head_width : (h + 1) * head_width]
+        q_fin = q_raw * norm_scale(q_raw) * gain(QUERY)
+        q_s[h] = turn(q_fin, turns[0], turns[1]).astype(BF16)
+    for i in range(n_qkv, n_att):
+        steps[i][3].wait_recv()
+    own_copies[3].wait()
+    move_gu(0)
+    for copy in kv_copies:
+        copy.wait_recv()
+
+    def keys():
+        return kv_s[:, :, :head_width].reshape((reach + 1) * rows, head_width)
+
+    def values():
+        return kv_s[:, :, head_width:].reshape((reach + 1) * rows, head_width)
+
+    for h in range(head_count):
+        scores = dot_nt(q_s[h], keys()) * (head_width**-0.5)
+        masked = jnp.where(allowed[...] > 0.5, scores, masked_value)
+        grown = jnp.exp(masked - jnp.max(masked, axis=-1, keepdims=True))
+        probs = grown / jnp.sum(grown, axis=-1, keepdims=True)
+        p_s[h] = probs
+        att_s[:, h * head_width : (h + 1) * head_width] = dot_nn(
+            probs.astype(BF16), values()
+        ).astype(BF16)
+        if h == 1:
+            move_gu(1)
+        if h == 3:
+            move_gu(2)
+
+    @pl.loop(0, 3)
+    def _(n):
+        o_s[:, outs(n)] = dot_nn(att_s[...], wo_s[:, outs(n)])
+
+    o_raw = o_s[...]
+    middle = x_ref[...].astype(F32) + o_raw * norm_scale(o_raw) * gain(ATT_OUT)
+    mid_s[...] = middle
+    h_all[0] = (middle * norm_scale(middle) * gain(FFN_IN)).astype(BF16)
+
+    def exchange(phase, src, dst):
+        return {
+            m: remote(src(m), dst(m), ex_send.at[phase, m], ex_recv.at[phase, m], at.line(m))
+            for m in range(1, n_fsdp)
+        }
+
+    last = n_fsdp - 1
+    send_h = exchange(0, lambda m: h_all.at[0], lambda m: h_all.at[m])
+    send_f = exchange(1, lambda m: part_out.at[m - 1], lambda m: part_in.at[0, m - 1])
+    send_df = exchange(2, lambda m: df_all.at[0], lambda m: df_all.at[m])
+    send_dh = exchange(3, lambda m: part_out.at[m - 1], lambda m: part_in.at[1, m - 1])
+    onward = {
+        phase: remote(rows_all.at[2], rows_all.at[last],
+                      relay_sem.at[phase], ex_recv.at[phase, last], at.line(1))
+        for phase, rows_all in ((0, h_all), (2, df_all))
+    }
+    by_way = {
+        phase: remote(part_out.at[last - 1], relay_in.at[phase // 2],
+                      relay_sem.at[phase], relay_sem.at[phase + 3], at.line(1))
+        for phase in (1, 3)
+    }
+
+    def send_rows(copies):
+        copies[1].start()
+        copies[2].start()
+        pl.when(middle_z)(copies[last].start)
+
+    def take_rows(copies, phase, m):
+        copies[m].wait_recv()
+        if m == 2:
+            pl.when(middle_z)(onward[phase].start)
+
+    def send_part(copies, phase, m):
+        if m == 1:
+            copies[1].start()
+        elif m == 2:
+            pl.when(~middle_z)(copies[2].start)
+        elif m == last:
+            pl.when(~middle_z)(by_way[phase].start)
+
+            @pl.when(middle_z)
+            def _():
+                copies[last].start()
+                by_way[phase].wait_recv()
+                part_out[1] = (
+                    part_out[1].astype(F32) + relay_in[phase // 2].astype(F32)
+                ).astype(BF16)
+                copies[2].start()
+
+    def take_parts(copies):
+        copies[1].wait_recv()
+        copies[2].wait_recv()
+        pl.when(middle_z)(copies[last].wait_recv)
+
+    def rows_sent(copies, phase):
+        copies[1].wait_send()
+        copies[2].wait_send()
+
+        @pl.when(middle_z)
+        def _():
+            copies[last].wait_send()
+            onward[phase].wait_send()
+
+    def parts_sent(copies, phase):
+        copies[1].wait_send()
+        copies[2].wait_send()
+        pl.when(middle_z)(copies[last].wait_send)
+        pl.when(~middle_z)(by_way[phase].wait_send)
+
+    send_rows(send_h)
+
+    @pl.when(~middle_z)
+    def _():
+        part_in[0, last - 1] = jnp.zeros((rows, width), BF16)
+        part_in[1, last - 1] = jnp.zeros((rows, width), BF16)
+
+    move_gu(3)
+    move_gu(4)
+    for i in range(n_att, n_items):
+        steps[i][3].wait_recv()
+    for copy in own_copies[4:]:
+        copy.wait()
+
+    for m in range(n_fsdp):
+        if m:
+            take_rows(send_h, 0, m)
+
+        @pl.loop(0, n_hid)
+        def _(n):
+            rows_h = h_all[m]
+            gate = dot_nn(rows_h, w_in[0, :, hid(n)])
+            up = dot_nn(rows_h, w_in[1, :, hid(n)])
+            squared = gate * gate
+            bent = jnp.tanh(GELU_RATE * (gate + GELU_CUBE * squared * gate))
+            gelu = 0.5 * gate * (1.0 + bent)
+            slope = 0.5 * (1.0 + bent) + 0.5 * gate * (1.0 - bent * bent) * (
+                GELU_RATE * (1.0 + 3.0 * GELU_CUBE * squared)
+            )
+            bent_s[pl.ds(m * rows, rows), hid(n)] = gelu.astype(BF16)
+            bent_s[pl.ds(tokens + m * rows, rows), hid(n)] = (slope * up).astype(BF16)
+            act[m, :, hid(n)] = (gelu * up).astype(BF16)
+
+        @pl.loop(0, 3)
+        def _(n):
+            part = dot_nn(act[m], w_down[:, outs(n)])
+            if m:
+                part_out[m - 1, :, outs(n)] = part.astype(BF16)
+            else:
+                total[:, outs(n)] = part
+
+        if m:
+            send_part(send_f, 1, m)
+
+    for m in range(n_fsdp):
+        h_turn[:, pl.ds(m * rows, rows)] = h_all[m].T
+    for i in range(n_att, n_items):
+        for k in range(4):
+            steps[i][k].wait_send()
+
+    take_parts(send_f)
+    f_raw = total[...]
+    for m in range(1, n_fsdp):
+        f_raw = f_raw + part_in[0, m - 1].astype(F32)
+    cot = cot_ref[...].astype(F32)
+    scale = norm_scale(f_raw)
+    d_f, d_gain = norm_back(f_raw, gain(FFN_OUT), scale, cot)
+    df_all[0] = d_f.astype(BF16)
+    send_rows(send_df)
+    out_ref[...] = (mid_s[...] + f_raw * scale * gain(FFN_OUT)).astype(BF16)
+    dgains[...] = jnp.zeros(dgains.shape, F32)
+    dgains[FFN_OUT : FFN_OUT + 1, :] = d_gain
+    parts_sent(send_f, 1)
+
+    for m in range(n_fsdp):
+        if m:
+            take_rows(send_df, 2, m)
+
+        @pl.loop(0, n_hid)
+        def _(n):
+            d_act = dot_nt(df_all[m], w_down[hid(n), :])
+            gelu = bent_s[pl.ds(m * rows, rows), hid(n)].astype(F32)
+            slope = bent_s[pl.ds(tokens + m * rows, rows), hid(n)].astype(F32)
+            d_in[0, m, :, hid(n)] = (d_act * slope).astype(BF16)
+            d_in[1, m, :, hid(n)] = (d_act * gelu).astype(BF16)
+
+        @pl.loop(0, 3)
+        def _(n):
+            part = dot_nt(d_in[0, m], w_in[0, outs(n), :]) + dot_nt(
+                d_in[1, m], w_in[1, outs(n), :]
+            )
+            if m:
+                part_out[m - 1, :, outs(n)] = part.astype(BF16)
+            else:
+                total[:, outs(n)] = part
+
+        if m:
+            send_part(send_dh, 3, m)
+
+    chunks = [("d", 0, True), ("d", 1, False)]
+    chunks += [("g", m, m % 2 == 0) for m in range(n_fsdp)]
+    chunks += [("o", 0, False), ("q", 0, True)]
+    n_ffn = 2 + n_fsdp
+    half_d = hidden // 4
+
+    def mine_of(kind, i):
+        if kind == "d":
+            return own_d.at[pl.ds(i * half_d, half_d)]
+        return {"g": own_g, "o": own_o, "q": own_q}[kind].at[i]
+
+    def hi_part(kind, hi):
+        if kind == "d":
+            return many(hi * (half_d // 2), half_d // 2), slice(None)
+        if kind == "g":
+            return many(hi * (depth // 2), depth // 2), slice(None)
+        if kind == "q":
+            return slice(None), lanes(hi * (heads_width // 2), heads_width // 2)
+        return many(hi * (rows_o // 4), rows_o // 4), slice(None)
+
+    def lo_part(kind, hi, lo):
+        if kind == "d":
+            return many(hi * (half_d // 2) + lo * (half_d // 4), half_d // 4), slice(None)
+        if kind == "g":
+            return (
+                many(hi * (depth // 2), depth // 2),
+                lanes(lo * (hidden // 2), hidden // 2),
+            )
+        if kind == "q":
+            start = hi * (heads_width // 2) + lo * (heads_width // 4)
+            return slice(None), lanes(start, heads_width // 4)
+        return many(hi * (rows_o // 4) + lo * (rows_o // 8), rows_o // 8), slice(None)
+
+    def fin_part(kind, i, where, core):
+        rows_at, cols_at = where
+        if kind == "g":
+            return fin_gu.at[core, i, rows_at, cols_at]
+        ref, base, size = {
+            "d": (fin_d, core * (hidden // 2) + i * half_d, half_d),
+            "q": (fin_qkv, core * (depth // 2), depth // 2),
+            "o": (fin_wo, core * (rows_o // 2), rows_o // 2),
+        }[kind]
+        if isinstance(rows_at, slice):
+            rows_at = many(base, size)
+        else:
+            rows_at = many(base + rows_at.start, rows_at.size)
+        return ref.at[rows_at, cols_at]
+
+    def add(ref, where, other):
+        rows_at, cols_at = where
+        start = 0 if isinstance(rows_at, slice) else rows_at.start
+        slab = 16
+
+        @pl.loop(0, other.shape[0] // slab)
+        def _(n):
+            here = pl.ds(pl.multiple_of(start + n * slab, slab), slab)
+            there = pl.ds(pl.multiple_of(n * slab, slab), slab)
+            ref[here, cols_at] = (
+                ref[here, cols_at].astype(F32) + other[there, :].astype(F32)
+            ).astype(BF16)
+
+    whole = (slice(None), slice(None))
+    from_hi = {"d": hi_d, "g": hi_g, "o": hi_o, "q": hi_q}
+    from_lo = {"d": lo_d, "g": lo_g, "o": lo_o, "q": lo_q}
+    his, los, lines = [], [], []
+    for j, (kind, i, first_x) in enumerate(chunks):
+        hi, lo, mask_hi, mask_lo = at.halves(first_x)
+        mine = mine_of(kind, i)
+        his.append(remote(mine.at[hi_part(kind, 1 - hi)], from_hi[kind].at[i],
+                          hi_send.at[j], hi_recv.at[j], at.plane(mask_hi)))
+        los.append(remote(mine.at[lo_part(kind, hi, 1 - lo)], from_lo[kind].at[i],
+                          lo_send.at[j], lo_recv.at[j], at.plane(mask_lo)))
+        line = None
+        if kind == "g" and i:
+            line = remote(mine.at[lo_part(kind, hi, lo)],
+                          fin_part(kind, z, lo_part(kind, hi, lo), c),
+                          z_send.at[j], z_recv.at[j], at.line(i))
+        lines.append(line)
+    stage = {
+        "d": lambda i: w_down.at[pl.ds(i * half_d, half_d)],
+        "g": lambda i: bent_s.at[pl.ds(i * depth, depth)],
+        "q": lambda i: w_in.at[0, pl.ds(i * (depth // 2), depth // 2), pl.ds(0, heads_width)],
+        "o": lambda i: w_in.at[1, pl.ds(i * (rows_o // 2), rows_o // 2), pl.ds(0, width)],
+    }
+    to_core = [("d", 0), ("d", 1)]
+    to_core += [(kind, m) for kind in "goq" for m in range(n_fsdp)]
+    cores = {
+        key: remote(stage[key[0]](key[1]), mine_of(*key), c_send.at[k], c_recv.at[k], at.plane(1))
+        for k, key in enumerate(to_core)
+    }
+    line_sums = {}
+    for k, (kind, ref) in enumerate((("o", line_o), ("q", line_q))):
+        for m in range(1, n_fsdp):
+            line_sums[kind, m] = remote(mine_of(kind, m), ref.at[m - 1],
+                                        oq_send.at[k, m], oq_recv.at[k, m], at.line(m))
+
+    puts, hands = [], []
+    for j, (kind, i, first_x) in enumerate(chunks):
+        hi, lo, mask_hi, mask_lo = at.halves(first_x)
+        which = flip(z, i, 2) if kind == "g" else i
+        piece = fin_part(kind, which, lo_part(kind, hi, lo), c)
+        half = fin_part(kind, which, hi_part(kind, hi), c)
+        full = fin_part(kind, which, whole, c)
+        put = None
+        if lines[j] is None:
+            put = pltpu.make_async_copy(
+                mine_of(kind, i).at[lo_part(kind, hi, lo)], piece, put_sem.at[j]
+            )
+        puts.append(put)
+        hands.append([
+            remote(part, part, ag_send.at[j, k], ag_recv.at[j, k], at.plane(mask))
+            for k, (part, mask) in enumerate(((piece, mask_lo), (half, mask_hi), (full, 1)))
+        ])
+
+    def take_hi(j):
+        kind, i, first_x = chunks[j]
+        hi, lo, _, _ = at.halves(first_x)
+        his[j].wait_recv()
+        add(mine_of(kind, i), hi_part(kind, hi), from_hi[kind].at[i])
+        los[j].start()
+
+    def take_lo(j):
+        kind, i, first_x = chunks[j]
+        hi, lo, _, _ = at.halves(first_x)
+        los[j].wait_recv()
+        add(mine_of(kind, i), lo_part(kind, hi, lo), from_lo[kind].at[i])
+        if lines[j] is not None:
+            lines[j].start()
+        else:
+            puts[j].start()
+
+    def begin_hand(j):
+        if lines[j] is not None:
+            lines[j].wait_recv()
+        else:
+            puts[j].wait()
+        hands[j][0].start()
+
+    def hand_on(j, k):
+        hands[j][k - 1].wait_recv()
+        hands[j][k].start()
+
+    def down_grads(core, dst, adds):
+        @pl.loop(0, hidden // 256)
+        def _(n):
+            left = act[:, :, lanes(core * (hidden // 2) + n * 128, 128)].reshape(tokens, 128).T
+            here = pl.ds(pl.multiple_of(n * 128, 128), 128)
+            for k in range(3):
+                right = df_all[:, :, k * third : (k + 1) * third].reshape(tokens, third)
+                grads = dot_nn(left, right)
+                if adds:
+                    grads = grads + dst[here, k * third : (k + 1) * third].astype(F32)
+                dst[here, k * third : (k + 1) * third] = grads.astype(BF16)
+
+    def in_grads(core, m, dst, adds):
+        left_at = many(flip(z, m, 2) * depth, depth)
+
+        @pl.loop(0, n_hid)
+        def _(n):
+            right = d_in[core, :, :, hid(n)].reshape(tokens, HID_TILE)
+            grads = dot_nn(h_turn[left_at, :], right)
+            if adds:
+                grads = grads + dst[:, hid(n)].astype(F32)
+            dst[:, hid(n)] = grads.astype(BF16)
+
+    down_grads(1 - c, w_down, False)
+    cores["d", 0].start()
+    cores["d", 1].start()
+    for m in range(n_fsdp):
+        in_grads(1 - c, m, stage["g"](m), False)
+        cores["g", m].start()
+    cores["d", 0].wait_recv()
+    cores["d", 1].wait_recv()
+    down_grads(c, own_d, True)
+    his[0].start()
+    his[1].start()
+    for m in range(n_fsdp):
+        cores["g", m].wait_recv()
+        in_grads(c, m, own_g.at[m], True)
+        his[2 + m].start()
+
+    dkv_copies = [
+        remote(dkv_send.at[reach - o], dkv_came.at[o - 1], dkv_ssem.at[o - 1], dkv_rsem.at[o - 1],
+               (lax.rem(s + n_seq - o, n_seq), z))
+        for o in range(1, reach + 1)
+    ]
+    gain_copies = [
+        remote(dgains, gain_in.at[k], gain_send.at[k], gain_recv.at[k], at.plane(k))
+        for k in range(1, n_seq)
+    ]
+    gain_lines = [
+        remote(gain_line.at[0], gain_line.at[m], gain_send.at[n_seq + m], gain_recv.at[n_seq + m],
+               at.line(m))
+        for m in range(1, n_fsdp)
+    ]
+
+    def to_middle():
+        take_parts(send_dh)
+        dh = total[...]
+        for m in range(1, n_fsdp):
+            dh = dh + part_in[1, m - 1].astype(F32)
+        mid = mid_s[...]
+        d_mid, d_gain = norm_back(mid, gain(FFN_IN), norm_scale(mid), dh)
+        d_mid = d_mid + cot_ref[...].astype(F32)
+        mid_s[...] = d_mid
+        dgains[FFN_IN : FFN_IN + 1, :] = d_gain
+        o_raw = o_s[...]
+        d_o, d_gain = norm_back(o_raw, gain(ATT_OUT), norm_scale(o_raw), d_mid)
+        dgains[ATT_OUT : ATT_OUT + 1, :] = d_gain
+        do_s[...] = d_o.astype(BF16)
+        for h in range(head_count):
+            here = pl.ds(h * head_width, head_width)
+            datt_s[h] = dot_nt(do_s[...], wo_s[here, :]).astype(BF16)
+
+    def unturn(rows_in):
+        return turn(rows_in, turns[0], -turns[1])
+
+    def through_head(h):
+        probs = p_s[h]
+        d_att = datt_s[h]
+        d_probs = dot_nt(d_att, values())
+        d_scores = probs * (d_probs - jnp.sum(probs * d_probs, axis=-1, keepdims=True))
+        ds_low = d_scores.astype(BF16)
+        scale = head_width**-0.5
+        d_keys = inner_rows(ds_low, q_s[h]) * scale
+        d_values = inner_rows(probs.astype(BF16), d_att)
+        if h:
+            d_keys = d_keys + dkv_s[:, :head_width]
+            d_values = d_values + dkv_s[:, head_width:]
+        dkv_s[:, :head_width] = d_keys
+        dkv_s[:, head_width:] = d_values
+        cols = slice(h * head_width, (h + 1) * head_width)
+        q_raw = raw_s[:, cols]
+        d_q, d_gain = norm_back(
+            q_raw, gain(QUERY), norm_scale(q_raw), unturn(dot_nn(ds_low, keys()) * scale)
+        )
+        dqkv_s[:, cols] = d_q.astype(BF16)
+        dgains[QUERY : QUERY + 1, :head_width] += d_gain
+
+    def return_keys():
+        for b in range(reach):
+            dkv_send[b] = dkv_s[pl.ds(b * rows, rows), :].astype(BF16)
+        for copy in dkv_copies:
+            copy.start()
+
+    def grad_tiles(left_at, turned, right, n_cols, dst, adds):
+        tile = n_cols // 3
+        for k in range(3):
+            grads = dot_nn(turned[left_at, :], right[:, k * tile : (k + 1) * tile])
+            if adds:
+                grads = grads + dst[:, k * tile : (k + 1) * tile].astype(F32)
+            dst[:, k * tile : (k + 1) * tile] = grads.astype(BF16)
+
+    def core_grads(kind, turned, right, span, n_cols):
+        for m in range(n_fsdp):
+            start = flip(z, m, 2) * span + (1 - c) * (span // 2)
+            grad_tiles(many(start, span // 2), turned, right, n_cols, stage[kind](m), False)
+            cores[kind, m].start()
+        for m in list(range(1, n_fsdp)) + [0]:
+            start = flip(z, m, 2) * span + c * (span // 2)
+            cores[kind, m].wait_recv()
+            grad_tiles(many(start, span // 2), turned, right, n_cols, mine_of(kind, m), True)
+            if m:
+                line_sums[kind, m].start()
+
+    def output_grads():
+        h_turn[pl.ds(0, query_width), pl.ds(0, rows)] = att_s[...].T
+        core_grads("o", h_turn.at[:, pl.ds(0, rows)], do_s, rows_o, width)
+
+    def key_grads():
+        h_turn[:, pl.ds(rows, rows)] = h1_s[...].T
+        d_kv = dkv_s[pl.ds(reach * rows, rows), :]
+        for o in range(reach):
+            dkv_copies[o].wait_recv()
+            d_kv = d_kv + dkv_came[o].astype(F32)
+        k_raw = raw_s[:, query_width : query_width + head_width]
+        d_k, d_gain = norm_back(
+            k_raw, gain(KEY), norm_scale(k_raw), unturn(d_kv[:, :head_width])
+        )
+        dqkv_s[:, query_width : query_width + head_width] = d_k.astype(BF16)
+        dqkv_s[:, query_width + head_width :] = d_kv[:, head_width:].astype(BF16)
+        dgains[KEY : KEY + 1, :head_width] = d_gain
+        core_grads("q", h_turn.at[:, pl.ds(rows, rows)], dqkv_s, depth, heads_width)
+
+    def sum_line(j):
+        kind = chunks[j][0]
+        for m in range(1, n_fsdp):
+            line_sums[kind, m].wait_recv()
+            add(mine_of(kind, 0), whole, {"o": line_o, "q": line_q}[kind].at[m - 1])
+        his[j].start()
+
+    def to_input():
+        x = x_ref[...].astype(F32)
+        d_h = dot_nt(dqkv_s[...], qkv_s[...])
+        d_x, d_gain = norm_back(x, gain(ATT_IN), norm_scale(x), d_h)
+        dx_out[...] = mid_s[...] + d_x
+        dgains[ATT_IN : ATT_IN + 1, :] = d_gain
+        for copy in gain_copies:
+            copy.start()
+
+    def sum_gains():
+        sums = dgains[...]
+        for k, copy in enumerate(gain_copies):
+            copy.wait_recv()
+            sums = sums + gain_in[k + 1]
+        gain_line[0] = sums
+        for copy in gain_lines:
+            copy.start()
+
+    take_hi(0)
+    take_hi(1)
+    to_middle()
+    through_head(0)
+    through_head(1)
+    take_hi(2)
+    take_hi(3)
+    take_lo(0)
+    take_lo(1)
+    through_head(2)
+    through_head(3)
+    return_keys()
+    output_grads()
+    begin_hand(0)
+    begin_hand(1)
+    take_hi(4)
+    take_hi(5)
+    take_lo(2)
+    take_lo(3)
+    key_grads()
+    hand_on(0, 1)
+    hand_on(1, 1)
+    begin_hand(2)
+    begin_hand(3)
+    take_lo(4)
+    take_lo(5)
+    to_input()
+    sum_line(6)
+    hand_on(0, 2)
+    hand_on(1, 2)
+    begin_hand(4)
+    begin_hand(5)
+    hand_on(2, 1)
+    hand_on(3, 1)
+    sum_line(7)
+    take_hi(6)
+    hand_on(2, 2)
+    hand_on(3, 2)
+    take_hi(7)
+    take_lo(6)
+    hand_on(4, 1)
+    hand_on(5, 1)
+    begin_hand(6)
+    take_lo(7)
+    sum_gains()
+    begin_hand(7)
+    hand_on(4, 2)
+    hand_on(5, 2)
+    hand_on(6, 1)
+    hand_on(7, 1)
+    hand_on(6, 2)
+    hand_on(7, 2)
+    sums = gain_line[0]
+    for m, copy in enumerate(gain_lines):
+        copy.wait_recv()
+        sums = sums + gain_line[m + 1]
+    gains_out[...] = sums
+
+    for j in range(len(chunks)):
+        hands[j][2].wait_recv()
+        for k in range(3):
+            hands[j][k].wait_send()
+        his[j].wait_send()
+        los[j].wait_send()
+        if lines[j] is not None:
+            lines[j].wait_send()
+    for copy in list(cores.values()) + list(line_sums.values()):
+        copy.wait_send()
+    for copy in gain_copies + gain_lines + dkv_copies + kv_copies + packs + seg_copies:
+        copy.wait_send()
+    for i in range(n_att):
+        for k in range(4):
+            steps[i][k].wait_send()
+    rows_sent(send_h, 0)
+    rows_sent(send_df, 2)
+    parts_sent(send_dh, 3)
+
+
+def layer(n_seq, n_fsdp, share, hidden, reach, head_count, x, cot, rates, pack, segs,
+          w_gate, w_up, w_query, w_key, w_value, w_output, w_down):
+    rows, width = x.shape
+    depth = width // n_fsdp
+    head_width = w_key.shape[1]
+    query_width = w_query.shape[1]
+    heads_width = query_width + 2 * head_width
+    rows_o = w_output.shape[0]
+    n_items = 4 * (n_fsdp - 1)
+    anywhere = pl.BlockSpec(memory_space=pl.ANY)
+    in_vmem = pl.BlockSpec(memory_space=pltpu.VMEM)
+    shape = jax.ShapeDtypeStruct
+    sems = pltpu.SemaphoreType.DMA
+
+    def low(*size):
+        return pltpu.VMEM(size, BF16)
+
+    def full(*size):
+        return pltpu.VMEM(size, F32)
+
+    return pl.pallas_call(
+        functools.partial(layer_kernel, n_seq, n_fsdp, share, reach, head_count),
+        out_shape=[
+            shape((rows, width), BF16),
+            shape((rows, width), F32),
+            shape((8, width), F32),
+            shape((2, n_fsdp, depth, hidden), BF16),
+            shape((hidden, width), BF16),
+            shape((depth, heads_width), BF16),
+            shape((rows_o, width), BF16),
+        ],
+        in_specs=[in_vmem] * 5 + [anywhere] * 7,
+        out_specs=[in_vmem] * 3 + [anywhere] * 4,
+        scratch_shapes=[
+            low(width, heads_width),
+            low(n_fsdp * rows_o, width),
+            low(2, width, hidden),
+            low(hidden, width),
+            full(n_fsdp, 8, pack.shape[1]),
+            pltpu.VMEM((n_seq, 8, rows), jnp.int32),
+            full(8, width),
+            full(rows, (reach + 1) * rows),
+            full(2, rows, head_width // 2),
+            low(rows, width),
+            full(rows, heads_width),
+            low(head_count, rows, head_width),
+            low(rows, 2 * head_width),
+            low(reach + 1, rows, 2 * head_width),
+            full(head_count, rows, (reach + 1) * rows),
+            low(rows, query_width),
+            full(rows, width),
+            full(rows, width),
+            low(n_fsdp, rows, width),
+            low(n_fsdp, rows, width),
+            low(max(width, 2 * n_fsdp * rows), hidden),
+            low(n_fsdp, rows, hidden),
+            low(2, n_fsdp, rows, hidden),
+            low(width, n_fsdp * rows),
+            low(n_fsdp - 1, rows, width),
+            low(2, n_fsdp - 1, rows, width),
+            low(2, rows, width),
+            full(rows, width),
+            low(hidden // 2, width),
+            low(n_fsdp, depth, hidden),
+            low(n_fsdp, rows_o // 2, width),
+            low(n_fsdp, depth // 2, heads_width),
+            low(2, hidden // 8, width),
+            low(n_fsdp, depth // 2, hidden),
+            low(1, rows_o // 4, width),
+            low(1, depth // 2, heads_width // 2),
+            low(2, hidden // 16, width),
+            low(n_fsdp, depth // 2, hidden // 2),
+            low(1, rows_o // 8, width),
+            low(1, depth // 2, heads_width // 4),
+            low(n_fsdp - 1, rows_o // 2, width),
+            low(n_fsdp - 1, depth // 2, heads_width),
+            low(rows, width),
+            low(head_count, rows, head_width),
+            full((reach + 1) * rows, 2 * head_width),
+            low(reach, rows, 2 * head_width),
+            low(reach, rows, 2 * head_width),
+            low(rows, heads_width),
+            full(8, width),
+            full(n_seq, 8, width),
+            full(n_fsdp, 8, width),
+            sems((n_items, 4)),
+            sems((n_items, 4)),
+            sems((7,)),
+            sems((n_fsdp,)),
+            sems((n_fsdp,)),
+            sems((n_seq,)),
+            sems((n_seq,)),
+            sems((reach,)),
+            sems((reach,)),
+            sems((4, n_fsdp)),
+            sems((4, n_fsdp)),
+            sems((7,)),
+            sems((reach,)),
+            sems((reach,)),
+            sems((2 + 3 * n_fsdp,)),
+            sems((2 + 3 * n_fsdp,)),
+            sems((4 + n_fsdp,)),
+            sems((4 + n_fsdp,)),
+            sems((4 + n_fsdp,)),
+            sems((4 + n_fsdp,)),
+            sems((4 + n_fsdp,)),
+            sems((4 + n_fsdp,)),
+            sems((2, n_fsdp)),
+            sems((2, n_fsdp)),
+            sems((4 + n_fsdp,)),
+            sems((4 + n_fsdp, 3)),
+            sems((4 + n_fsdp, 3)),
+            sems((n_seq + n_fsdp,)),
+            sems((n_seq + n_fsdp,)),
+        ],
+        compiler_params=pltpu.CompilerParams(
+            collective_id=0, has_side_effects=True, vmem_limit_bytes=62 << 20
+        ),
+        name="decoder_layer",
+    )(x, cot, rates, pack, segs, w_gate, w_up, w_query, w_key, w_value, w_output, w_down)
+
+
+def join_kernel(share, wins_ref, gate_ref, up_ref):
+    n_win, hidden = wins_ref.shape[1], wins_ref.shape[3]
+    starts = [window_start(i, share) for i in range(n_win)]
+    for i, ref in enumerate((gate_ref, up_ref)):
+        for w in range(n_win):
+            first = starts[w]
+            last = starts[w + 1] if w + 1 < n_win else first + hidden
+            shared = starts[w - 1] + hidden - first if w else 0
+            if shared:
+                ref[:, first : first + shared] = wins_ref[i, w, :, :shared].astype(F32) + wins_ref[
+                    i, w - 1, :, hidden - shared :
+                ].astype(F32)
+            ref[:, first + shared : last] = wins_ref[i, w, :, shared : last - first].astype(F32)
+
+
+def joined(share, windows):
+    _, n_win, rows, hidden = windows.shape
+    slab = 32
+    wide = pl.BlockSpec((slab, n_win * share), lambda i: (i, 0))
+    return pl.pallas_call(
+        functools.partial(join_kernel, share),
+        grid=(rows // slab,),
+        out_shape=[jax.ShapeDtypeStruct((rows, n_win * share), F32)] * 2,
+        in_specs=[pl.BlockSpec((2, n_win, slab, hidden), lambda i: (0, 0, i, 0))],
+        out_specs=[wide, wide],
+        compiler_params=pltpu.CompilerParams(vmem_limit_bytes=32 << 20),
+        name="join_windows",
+    )(windows)
+
+
+def shards(n_seq, n_fsdp, *args):
+    w_query, w_key, w_output, w_gate = args[4], args[5], args[9], args[12]
+    depth, ffn_width = w_gate.shape
+    rows_here = args[0].shape[1]
+    share = ffn_width // n_fsdp
+    reach = (WINDOW - 2 + rows_here) // rows_here
+    fits = (
+        n_seq == 8
+        and n_fsdp == 4
+        and args[0].shape[0] == 1
+        and reach < n_seq
+        and rows_here % 128 == 0
+        and depth % 32 == 0
+        and w_output.shape[0] % 128 == 0
+        and w_key.shape[1] % 256 == 0
+        and w_query.shape[1] % 512 == 0
+        and w_output.shape[1] % 384 == 0
+        and ffn_width % n_fsdp == 0
+        and share % 16 == 0
+        and window_start(n_fsdp - 1, share) + window_width(share, n_fsdp) == ffn_width
+    )
+    if fits:
+        return shards_fused(n_seq, n_fsdp, *args)
+    return shards_plain(*args)
+
+
+def shards_fused(
+    n_seq,
+    n_fsdp,
+    inputs,
+    segments,
+    cotangent,
+    gain_attn_in,
+    w_query,
+    w_key,
+    w_value,
+    gain_query,
+    gain_key,
+    w_output,
+    gain_attn_out,
+    gain_ffn_in,
+    w_gate,
+    w_up,
+    w_down,
+    gain_ffn_out,
+):
+    rows_here, width = inputs.shape[1:]
+    head_width = w_key.shape[1]
+    query_width = w_query.shape[1]
+    head_count = query_width // head_width
+    share = w_gate.shape[1] // n_fsdp
+    hidden = window_width(share, n_fsdp)
+    reach = (WINDOW - 2 + rows_here) // rows_here
+    line = lax.axis_index("fsdp")
+    gains = (gain_attn_in, gain_attn_out, gain_ffn_in, gain_ffn_out, gain_query, gain_key)
+    pack = jnp.concatenate(gains).astype(F32)[None]
+    rates = 10000.0 ** (-(jnp.arange(head_width // 2, dtype=F32) * 2.0) / head_width)
+    outputs, d_inputs, gain_sums, fin_gu, fin_d, fin_qkv, fin_wo = layer(
+        n_seq, n_fsdp, share, hidden, reach, head_count,
+        inputs[0], cotangent[0], rates[None], pack, segments,
+        w_gate, w_up, w_query, w_key, w_value, w_output, w_down,
+    )
+    grad_gate, grad_up = joined(share, fin_gu)
+    skipped = line * share - window_start(line, share)
+    grad_down = lax.dynamic_slice(fin_d, (skipped, jnp.int32(0)), (share, width)).astype(F32)
+
+    def part(row, gain):
+        size = gain.shape[0]
+        return lax.dynamic_slice(gain_sums[row], (line * size,), (size,))
+
+    fin_qkv = fin_qkv.astype(F32)
+    return (
+        outputs[None],
+        d_inputs[None],
+        part(ATT_IN, gain_attn_in),
+        fin_qkv[:, :query_width],
+        fin_qkv[:, query_width : query_width + head_width],
+        fin_qkv[:, query_width + head_width :],
+        part(QUERY, gain_query),
+        part(KEY, gain_key),
+        fin_wo.astype(F32),
+        part(ATT_OUT, gain_attn_out),
+        part(FFN_IN, gain_ffn_in),
+        grad_gate,
+        grad_up,
+        grad_down,
+        part(FFN_OUT, gain_ffn_out),
+    )
+
+
 def solution(mesh):
     placed = (
         P("fsdp", "seq", None),
@@ -364,7 +1520,7 @@
         P("fsdp"),
     )
     return jax.shard_map(
-        shards,
+        functools.partial(shards, mesh.shape["seq"], mesh.shape["fsdp"]),
         mesh=mesh,
         in_specs=placed,
         out_specs=(

time: 3190 us -> 432 us (0.14)
  waiting for transfers between devices: 2750 us -> 0 us
  Pallas kernels: 0 us -> 406 us
  blocking collectives: 121 us -> 0 us
  matrix products: 110 us -> 0 us
  local copies, waits for them, and re-layouts: 95.5 us -> 15.4 us
  starting transfers between devices: 55.4 us -> 0 us
    all_gather x11 -> x0, waiting for transfers between devices: 1620 us -> none  [the longest x1 268 us: shards(): lax.all_gather(w_gate, 'fsdp', axis=0, tiled=True)]
    reduce_scatter x6 -> x0, waiting for transfers between devices: 864 us -> none  [the longest x1 523 us: shards(): lax.psum_scatter(jnp.concatenate([inner_rows(h_two, dg_low), inner_rows(h...]
    pallas_call x0 -> x2, Pallas kernels: none -> 406 us  [the longest x1 400 us: layer(): pl.pallas_call(functools.partial(layer_kernel, n_seq, n_fsdp, share, reac...]
    unnamed x31 -> x0, waiting for transfers between devices: 257 us -> none
    dot_general x27 -> x0, matrix products: 110 us -> none  [the longest x9 38.9 us: outer_cols(): lax.dot_general(left, right, (((1,), (1,)), ((), ())), preferred_element_...]
    all_gather x6 -> x0, blocking collectives: 79.1 us -> none  [the longest x1 23.8 us: shards(): lax.all_gather(w_value, 'fsdp', axis=0, tiled=True)]
    ppermute x20 -> x0, starting transfers between devices: 53.8 us -> none  [from_behind(): return lax.ppermute(block, axis, route)]
    unnamed x197 -> x8, local copies, waits for them, and re-layouts: 50.3 us -> 4.88 us
  transfers between devices with their start and end apart: 44 -> 0, of which waited for: 34 -> 0; matrix products, arithmetic and copies ran while one was open for 6% -> 0% of each run, Pallas kernels for 0% -> 0%
where the time goes in v2:
time: 432 us
  Pallas kernels  406 us (94%)
  local copies, waits for them, and re-layouts  15.4 us (4%)
  other arithmetic  9.25 us (2%)
    pallas_call x1, Pallas kernels, layer(): pl.pallas_call(functools.partial(layer_kernel, n_seq, n_fsdp, share, reac...  400 us

profile of v2, /device:TPU:9, one launch (start us, length us, event | category | flops | bytes accessed | tf_op | source)
XLA Modules:
  0.0 431.6 jit_solution(11497481650670740347)
XLA Ops:
  0.6 0.5 multiply_power_fusion.rates_ref
  1.2 0.7 concatenate.22
  1.9 0.7 concatenate.23
  2.5 0.7 concatenate.24
  3.2 0.7 concatenate.25
  3.9 0.8 concatenate.28
  4.7 0.6 convert_element_type.19.pack_ref
  5.3 399.6 %decoder_layer.1 = (bf16[128,1152]{1,0:T(8,128)(2,1)}, f32[128,1152]{1,0:T(8,128)}, f32[8,1152]{1,0:T(8,128)}, bf16[2,4,288,1792]{3,2,1,0:T(8,128)(2,1)}, bf16[1...) custom-call(bf16[128,1152]{1,0:T(8,128)(2,1)} %bitcast.11, bf16[128,1152]{1,0:T(8,128)(2,1)} %bitcast.12, ...), custom_call_target="tpu_custom_call" | custom-call | tf_op jit(solution)/shard_map/decoder_layer/pallas_call | solution.py:1281
  404.9 1.0 fusion.7
  406.0 0.7 fusion
  406.6 2.2 slice.36
  408.9 1.8 fusion.6
  410.7 0.6 fusion.4
  411.3 2.2 convert_element_type.21
  413.4 0.7 fusion.2
  414.1 0.0 copy-start
  414.1 3.3 copy-done
  417.4 6.6 %join_windows.1 = (f32[288,6912]{1,0:T(8,128)}, f32[288,6912]{1,0:T(8,128)}) custom-call(bf16[2,4,288,1792]{3,2,1,0:T(8,128)(2,1)S(1)} %copy-done), custom_call_target="tpu_custom_call" | custom-call | tf_op jit(solution)/shard_map/join_windows/pallas_call | solution.py:1402
  424.1 0.0 copy-start.2
  424.1 0.0 copy-start.1
  424.1 6.0 %dynamic-slice_convert_fusion = f32[1728,1152]{1,0:T(8,128)} fusion(bf16[1792,1152]{1,0:T(8,128)(2,1)} %get-tuple-element.32, s32[]{:T(128)S(6)} %select_n.15), kind=kLoop, calls=%fused_computation | loop fusion | flops 1990656 | bytes 11943940 | tf_op jit(solution)/shard_map/convert_element_type | solution.py:1477
  430.0 0.0 copy-done.2
  430.0 0.7 copy.33
  430.7 0.0 copy-done.1
  430.7 0.8 copy.34
Async XLA Ops:
  414.1 3.3 copy-start
  424.1 6.0 %copy-start.2 = (bf16[128,1152]{1,0:T(8,128)(2,1)S(1)}, bf16[128,1152]{1,0:T(8,128)(2,1)}, u32[]{:S(2)}) copy-start(bf16[128,1152]{1,0:T(8,128)(2,1)} %get-tuple-element.24) | copy-start | bytes 884740
  424.1 6.7 %copy-start.1 = (f32[128,1152]{1,0:T(8,128)S(1)}, f32[128,1152]{1,0:T(8,128)}, u32[]{:S(2)}) copy-start(f32[128,1152]{1,0:T(8,128)} %get-tuple-element.25) | copy-start | bytes 1769476

commit v3 on v2

--- a/solution.py
+++ b/solution.py
@@ -457,7 +457,7 @@
     h1_s, raw_s, q_s, kv_own, kv_s, p_s, att_s, o_s, mid_s,
     h_all, df_all, bent_s, act, d_in, h_turn, part_out, part_in, relay_in, total,
     own_d, own_g, own_o, own_q, hi_d, hi_g, hi_o, hi_q, lo_d, lo_g, lo_o, lo_q, line_o, line_q,
-    do_s, datt_s, dkv_s, dkv_send, dkv_came, dqkv_s, dgains, gain_in, gain_line,
+    do_s, datt_s, ds_s, dkv_s, dkv_send, dkv_came, dqkv_s, dgains, gain_in, gain_line,
     w_send, w_recv, own_sem, pack_send, pack_recv, seg_send, seg_recv, kv_send, kv_recv,
     ex_send, ex_recv, relay_sem, dkv_ssem, dkv_rsem,
     c_send, c_recv, hi_send, hi_recv, lo_send, lo_recv, z_send, z_recv, oq_send, oq_recv,
@@ -565,9 +565,10 @@
         return [ref.at[here, cols] for ref in (gate_ref, up_ref)]
 
     items = []
-    for k, kind in enumerate(("q", "kv", "wo", "gu")):
+    for kinds in (("q", "kv"), ("wo",), ("gu",)):
         for m in range(1, n_fsdp):
-            items.append((kind, m, (m % 2 == 1) != (kind in ("kv", "wo"))))
+            for kind in kinds:
+                items.append((kind, m, (m % 2 == 1) != (kind in ("kv", "wo"))))
     steps, starts = [], []
     for i, (kind, m, first_x) in enumerate(items):
         hi, lo, mask_hi, mask_lo = at.halves(first_x)
@@ -597,9 +598,10 @@
     n_items = len(items)
     n_att = n_items - (n_fsdp - 1)
     n_qkv = 2 * (n_fsdp - 1)
+    ahead, lag = 6, 3
     for copy in packs + seg_copies:
         copy.start()
-    for i in range(n_att):
+    for i in range(ahead):
         begin_weight(i)
     for copy in own_copies:
         copy.start()
@@ -613,7 +615,7 @@
         key_seg = seg_all[lax.rem(s + n_seq - o, n_seq), 0:1, :].astype(F32)
         apart = across - along + o * rows
         fine = (apart >= 0) & (apart < WINDOW) & (seg_here == key_seg) & (s >= o)
-        allowed[:, pl.ds((reach - o) * rows, rows)] = jnp.where(fine, 1.0, 0.0)
+        allowed[:, pl.ds((reach - o) * rows, rows)] = jnp.where(fine, 1.0, 0.0).astype(BF16)
     angle = ((s * rows + across).astype(F32) - seg_here) * rates_ref[...]
     turns[0] = jnp.cos(angle)
     turns[1] = jnp.sin(angle)
@@ -635,29 +637,23 @@
     x = x_ref[...].astype(F32)
     h1_s[...] = (x * norm_scale(x) * gain(ATT_IN)).astype(BF16)
 
-    for t in range(n_att + 2):
+    for t in range(n_att + 2 * lag):
         for stage in (3, 2, 1):
-            i = t - (stage - 1)
+            i = t - lag * (stage - 1)
             if 0 <= i < n_att:
                 move_weight(i, stage)
-        if t == n_att - 1:
-            for i in range(n_att, n_items):
-                begin_weight(i)
+                if stage == 1 and i + ahead < n_items:
+                    begin_weight(i + ahead)
     for i in range(n_qkv):
         steps[i][3].wait_recv()
     for copy in own_copies[:3]:
         copy.wait()
 
-    gu_moves = []
-    for t in range(n_fsdp + 1):
-        gu_moves.append(
-            [(n_att + t - (k - 1), k) for k in (3, 2, 1) if 0 <= t - (k - 1) < n_fsdp - 1]
-        )
-
-    def move_gu(t):
-        for i, stage in gu_moves[t]:
-            move_weight(i, stage)
-
+    def move_gu(*moves):
+        for m, stage in moves:
+            move_weight(n_att + m - 1, stage)
+
+    move_gu((1, 1))
     tile = heads_width // 3
 
     @pl.loop(0, 3)
@@ -680,7 +676,7 @@
     for i in range(n_qkv, n_att):
         steps[i][3].wait_recv()
     own_copies[3].wait()
-    move_gu(0)
+    move_gu((2, 1), (1, 2))
     for copy in kv_copies:
         copy.wait_recv()
 
@@ -692,17 +688,12 @@
 
     for h in range(head_count):
         scores = dot_nt(q_s[h], keys()) * (head_width**-0.5)
-        masked = jnp.where(allowed[...] > 0.5, scores, masked_value)
+        masked = jnp.where(allowed[...].astype(F32) > 0.5, scores, masked_value)
         grown = jnp.exp(masked - jnp.max(masked, axis=-1, keepdims=True))
         probs = grown / jnp.sum(grown, axis=-1, keepdims=True)
-        p_s[h] = probs
-        att_s[:, h * head_width : (h + 1) * head_width] = dot_nn(
-            probs.astype(BF16), values()
-        ).astype(BF16)
-        if h == 1:
-            move_gu(1)
-        if h == 3:
-            move_gu(2)
+        p_s[h] = probs.astype(BF16)
+        att_s[:, h * head_width : (h + 1) * head_width] = dot_nn(p_s[h], values()).astype(BF16)
+        move_gu((((3, 1),), ((2, 2),), ((1, 3),), ((3, 2),))[h][0])
 
     @pl.loop(0, 3)
     def _(n):
@@ -740,27 +731,27 @@
         copies[2].start()
         pl.when(middle_z)(copies[last].start)
 
-    def take_rows(copies, phase, m):
-        copies[m].wait_recv()
-        if m == 2:
-            pl.when(middle_z)(onward[phase].start)
+    def relay_rows(copies, phase):
+        copies[2].wait_recv()
+        pl.when(middle_z)(onward[phase].start)
 
     def send_part(copies, phase, m):
         if m == 1:
             copies[1].start()
         elif m == 2:
             pl.when(~middle_z)(copies[2].start)
-        elif m == last:
+        else:
             pl.when(~middle_z)(by_way[phase].start)
-
-            @pl.when(middle_z)
-            def _():
-                copies[last].start()
-                by_way[phase].wait_recv()
-                part_out[1] = (
-                    part_out[1].astype(F32) + relay_in[phase // 2].astype(F32)
-                ).astype(BF16)
-                copies[2].start()
+            pl.when(middle_z)(copies[last].start)
+
+    def send_joint_part(copies, phase):
+        @pl.when(middle_z)
+        def _():
+            by_way[phase].wait_recv()
+            part_out[1] = (
+                part_out[1].astype(F32) + relay_in[phase // 2].astype(F32)
+            ).astype(BF16)
+            copies[2].start()
 
     def take_parts(copies):
         copies[1].wait_recv()
@@ -789,43 +780,39 @@
         part_in[0, last - 1] = jnp.zeros((rows, width), BF16)
         part_in[1, last - 1] = jnp.zeros((rows, width), BF16)
 
-    move_gu(3)
-    move_gu(4)
+    move_gu((2, 3))
+    relay_rows(send_h, 0)
+    move_gu((3, 3))
     for i in range(n_att, n_items):
         steps[i][3].wait_recv()
     for copy in own_copies[4:]:
         copy.wait()
-
-    for m in range(n_fsdp):
-        if m:
-            take_rows(send_h, 0, m)
-
-        @pl.loop(0, n_hid)
-        def _(n):
-            rows_h = h_all[m]
-            gate = dot_nn(rows_h, w_in[0, :, hid(n)])
-            up = dot_nn(rows_h, w_in[1, :, hid(n)])
+    half_h = hidden // 2
+
+    for m in (*range(1, n_fsdp), 0):
+        if m not in (0, 2):
+            send_h[m].wait_recv()
+        for n in range(2):
+            cols = slice(n * half_h, (n + 1) * half_h)
+            gate = dot_nn(h_all[m], w_in[0, :, cols])
+            up = dot_nn(h_all[m], w_in[1, :, cols])
             squared = gate * gate
             bent = jnp.tanh(GELU_RATE * (gate + GELU_CUBE * squared * gate))
             gelu = 0.5 * gate * (1.0 + bent)
             slope = 0.5 * (1.0 + bent) + 0.5 * gate * (1.0 - bent * bent) * (
                 GELU_RATE * (1.0 + 3.0 * GELU_CUBE * squared)
             )
-            bent_s[pl.ds(m * rows, rows), hid(n)] = gelu.astype(BF16)
-            bent_s[pl.ds(tokens + m * rows, rows), hid(n)] = (slope * up).astype(BF16)
-            act[m, :, hid(n)] = (gelu * up).astype(BF16)
-
-        @pl.loop(0, 3)
-        def _(n):
-            part = dot_nn(act[m], w_down[:, outs(n)])
-            if m:
-                part_out[m - 1, :, outs(n)] = part.astype(BF16)
-            else:
-                total[:, outs(n)] = part
-
+            bent_s[pl.ds(m * rows, rows), cols] = gelu.astype(BF16)
+            bent_s[pl.ds(tokens + m * rows, rows), cols] = (slope * up).astype(BF16)
+            act[m, :, cols] = (gelu * up).astype(BF16)
+        part = dot_nn(act[m], w_down[...])
         if m:
+            part_out[m - 1] = part.astype(BF16)
             send_part(send_f, 1, m)
-
+        else:
+            total[...] = part
+
+    send_joint_part(send_f, 1)
     for m in range(n_fsdp):
         h_turn[:, pl.ds(m * rows, rows)] = h_all[m].T
     for i in range(n_att, n_items):
@@ -846,45 +833,20 @@
     dgains[FFN_OUT : FFN_OUT + 1, :] = d_gain
     parts_sent(send_f, 1)
 
-    for m in range(n_fsdp):
-        if m:
-            take_rows(send_df, 2, m)
-
-        @pl.loop(0, n_hid)
-        def _(n):
-            d_act = dot_nt(df_all[m], w_down[hid(n), :])
-            gelu = bent_s[pl.ds(m * rows, rows), hid(n)].astype(F32)
-            slope = bent_s[pl.ds(tokens + m * rows, rows), hid(n)].astype(F32)
-            d_in[0, m, :, hid(n)] = (d_act * slope).astype(BF16)
-            d_in[1, m, :, hid(n)] = (d_act * gelu).astype(BF16)
-
-        @pl.loop(0, 3)
-        def _(n):
-            part = dot_nt(d_in[0, m], w_in[0, outs(n), :]) + dot_nt(
-                d_in[1, m], w_in[1, outs(n), :]
-            )
-            if m:
-                part_out[m - 1, :, outs(n)] = part.astype(BF16)
-            else:
-                total[:, outs(n)] = part
-
-        if m:
-            send_part(send_dh, 3, m)
-
-    chunks = [("d", 0, True), ("d", 1, False)]
+    chunks = [("d", 0, False), ("d", 1, True)]
     chunks += [("g", m, m % 2 == 0) for m in range(n_fsdp)]
     chunks += [("o", 0, False), ("q", 0, True)]
-    n_ffn = 2 + n_fsdp
-    half_d = hidden // 4
+    tiles_d = hidden // 256
+    spans_d = (pl.ds(0, n_fsdp), pl.ds(n_fsdp, tiles_d - n_fsdp))
 
     def mine_of(kind, i):
         if kind == "d":
-            return own_d.at[pl.ds(i * half_d, half_d)]
+            return own_d.at[spans_d[i]]
         return {"g": own_g, "o": own_o, "q": own_q}[kind].at[i]
 
     def hi_part(kind, hi):
         if kind == "d":
-            return many(hi * (half_d // 2), half_d // 2), slice(None)
+            return slice(None), many(hi * 64, 64), slice(None)
         if kind == "g":
             return many(hi * (depth // 2), depth // 2), slice(None)
         if kind == "q":
@@ -893,7 +855,7 @@
 
     def lo_part(kind, hi, lo):
         if kind == "d":
-            return many(hi * (half_d // 2) + lo * (half_d // 4), half_d // 4), slice(None)
+            return slice(None), many(hi * 64 + lo * 32, 32), slice(None)
         if kind == "g":
             return (
                 many(hi * (depth // 2), depth // 2),
@@ -905,11 +867,12 @@
         return many(hi * (rows_o // 4) + lo * (rows_o // 8), rows_o // 8), slice(None)
 
     def fin_part(kind, i, where, core):
+        if kind == "d":
+            return fin_d.at[core, spans_d[i], where[-2], :]
         rows_at, cols_at = where
         if kind == "g":
             return fin_gu.at[core, i, rows_at, cols_at]
         ref, base, size = {
-            "d": (fin_d, core * (hidden // 2) + i * half_d, half_d),
             "q": (fin_qkv, core * (depth // 2), depth // 2),
             "o": (fin_wo, core * (rows_o // 2), rows_o // 2),
         }[kind]
@@ -939,10 +902,23 @@
     for j, (kind, i, first_x) in enumerate(chunks):
         hi, lo, mask_hi, mask_lo = at.halves(first_x)
         mine = mine_of(kind, i)
-        his.append(remote(mine.at[hi_part(kind, 1 - hi)], from_hi[kind].at[i],
-                          hi_send.at[j], hi_recv.at[j], at.plane(mask_hi)))
-        los.append(remote(mine.at[lo_part(kind, hi, 1 - lo)], from_lo[kind].at[i],
-                          lo_send.at[j], lo_recv.at[j], at.plane(mask_lo)))
+        if kind == "q":
+            parts = (
+                own_q.at[:, :, hi_part(kind, 1 - hi)[1]], hi_q,
+                own_q.at[:, :, lo_part(kind, hi, 1 - lo)[1]], lo_q,
+            )
+        else:
+            slot = spans_d[i] if kind == "d" else i
+            parts = (
+                mine.at[hi_part(kind, 1 - hi)], from_hi[kind].at[slot],
+                mine.at[lo_part(kind, hi, 1 - lo)], from_lo[kind].at[slot],
+            )
+        his.append(
+            remote(parts[0], parts[1], hi_send.at[j], hi_recv.at[j], at.plane(mask_hi))
+        )
+        los.append(
+            remote(parts[2], parts[3], lo_send.at[j], lo_recv.at[j], at.plane(mask_lo))
+        )
         line = None
         if kind == "g" and i:
             line = remote(mine.at[lo_part(kind, hi, lo)],
@@ -950,7 +926,7 @@
                           z_send.at[j], z_recv.at[j], at.line(i))
         lines.append(line)
     stage = {
-        "d": lambda i: w_down.at[pl.ds(i * half_d, half_d)],
+        "d": lambda i: part_in.at[0] if i else h_all,
         "g": lambda i: bent_s.at[pl.ds(i * depth, depth)],
         "q": lambda i: w_in.at[0, pl.ds(i * (depth // 2), depth // 2), pl.ds(0, heads_width)],
         "o": lambda i: w_in.at[1, pl.ds(i * (rows_o // 2), rows_o // 2), pl.ds(0, width)],
@@ -964,8 +940,12 @@
     line_sums = {}
     for k, (kind, ref) in enumerate((("o", line_o), ("q", line_q))):
         for m in range(1, n_fsdp):
-            line_sums[kind, m] = remote(mine_of(kind, m), ref.at[m - 1],
-                                        oq_send.at[k, m], oq_recv.at[k, m], at.line(m))
+            part = mine_of(kind, m)
+            if kind == "q":
+                part = part.at[lo_part(kind, at.x, at.y)]
+            line_sums[kind, m] = remote(
+                part, ref.at[m - 1], oq_send.at[k, m], oq_recv.at[k, m], at.line(m)
+            )
 
     puts, hands = [], []
     for j, (kind, i, first_x) in enumerate(chunks):
@@ -985,20 +965,33 @@
             for k, (part, mask) in enumerate(((piece, mask_lo), (half, mask_hi), (full, 1)))
         ])
 
+    def add_all(kind, i, where, came):
+        if kind == "d":
+            for n in range(spans_d[i].start, spans_d[i].start + spans_d[i].size):
+                add(own_d.at[n], where[1:], came.at[n])
+        elif kind == "q":
+            for m in range(n_fsdp):
+                add(own_q.at[m], where, came.at[m])
+        else:
+            add(mine_of(kind, i), where, came.at[i])
+
     def take_hi(j):
         kind, i, first_x = chunks[j]
         hi, lo, _, _ = at.halves(first_x)
         his[j].wait_recv()
-        add(mine_of(kind, i), hi_part(kind, hi), from_hi[kind].at[i])
+        add_all(kind, i, hi_part(kind, hi), from_hi[kind])
         los[j].start()
 
     def take_lo(j):
         kind, i, first_x = chunks[j]
         hi, lo, _, _ = at.halves(first_x)
         los[j].wait_recv()
-        add(mine_of(kind, i), lo_part(kind, hi, lo), from_lo[kind].at[i])
+        add_all(kind, i, lo_part(kind, hi, lo), from_lo[kind])
         if lines[j] is not None:
             lines[j].start()
+        elif kind == "q":
+            for m in range(1, n_fsdp):
+                line_sums[kind, m].start()
         else:
             puts[j].start()
 
@@ -1013,40 +1006,62 @@
         hands[j][k - 1].wait_recv()
         hands[j][k].start()
 
-    def down_grads(core, dst, adds):
-        @pl.loop(0, hidden // 256)
-        def _(n):
+    def down_stage(n):
+        return h_all.at[n] if n < n_fsdp else part_in.at[0, n - n_fsdp]
+
+    def down_grads(core, dst_of, adds):
+        right = df_all[...].reshape(tokens, width)
+        for n in range(tiles_d):
             left = act[:, :, lanes(core * (hidden // 2) + n * 128, 128)].reshape(tokens, 128).T
-            here = pl.ds(pl.multiple_of(n * 128, 128), 128)
-            for k in range(3):
-                right = df_all[:, :, k * third : (k + 1) * third].reshape(tokens, third)
-                grads = dot_nn(left, right)
-                if adds:
-                    grads = grads + dst[here, k * third : (k + 1) * third].astype(F32)
-                dst[here, k * third : (k + 1) * third] = grads.astype(BF16)
+            grads = dot_nn(left, right)
+            dst = dst_of[n] if adds else dst_of(n)
+            if adds:
+                grads = grads + dst[...].astype(F32)
+            dst[...] = grads.astype(BF16)
 
     def in_grads(core, m, dst, adds):
         left_at = many(flip(z, m, 2) * depth, depth)
 
-        @pl.loop(0, n_hid)
-        def _(n):
-            right = d_in[core, :, :, hid(n)].reshape(tokens, HID_TILE)
-            grads = dot_nn(h_turn[left_at, :], right)
+        for n in range(2):
+            cols = slice(n * half_h, (n + 1) * half_h)
+            grads = dot_nn(h_turn[left_at, :], d_in[core, :, :, cols].reshape(tokens, half_h))
             if adds:
-                grads = grads + dst[:, hid(n)].astype(F32)
-            dst[:, hid(n)] = grads.astype(BF16)
-
-    down_grads(1 - c, w_down, False)
-    cores["d", 0].start()
-    cores["d", 1].start()
+                grads = grads + dst[:, cols].astype(F32)
+            dst[:, cols] = grads.astype(BF16)
+
+    rows_sent(send_h, 0)
+    for m in range(n_fsdp):
+        if m == 1:
+            relay_rows(send_df, 2)
+        if m not in (0, 2):
+            send_df[m].wait_recv()
+        if m == last:
+            down_grads(1 - c, down_stage, False)
+            cores["d", 0].start()
+            cores["d", 1].start()
+        for n in range(2):
+            cols = slice(n * half_h, (n + 1) * half_h)
+            d_act = dot_nt(df_all[m], w_down[cols, :])
+            slope = bent_s[pl.ds(tokens + m * rows, rows), cols].astype(F32)
+            d_in[0, m, :, cols] = (d_act * slope).astype(BF16)
+            gelu = bent_s[pl.ds(m * rows, rows), cols].astype(F32)
+            d_in[1, m, :, cols] = (d_act * gelu).astype(BF16)
+        part = dot_nt(d_in[0, m], w_in[0]) + dot_nt(d_in[1, m], w_in[1])
+        if m:
+            part_out[m - 1] = part.astype(BF16)
+            send_part(send_dh, 3, m)
+        else:
+            total[...] = part
+
+    cores["d", 0].wait_recv()
+    cores["d", 1].wait_recv()
+    down_grads(c, own_d.at, True)
+    his[0].start()
+    his[1].start()
+    send_joint_part(send_dh, 3)
     for m in range(n_fsdp):
         in_grads(1 - c, m, stage["g"](m), False)
         cores["g", m].start()
-    cores["d", 0].wait_recv()
-    cores["d", 1].wait_recv()
-    down_grads(c, own_d, True)
-    his[0].start()
-    his[1].start()
     for m in range(n_fsdp):
         cores["g", m].wait_recv()
         in_grads(c, m, own_g.at[m], True)
@@ -1089,19 +1104,13 @@
         return turn(rows_in, turns[0], -turns[1])
 
     def through_head(h):
-        probs = p_s[h]
+        probs = p_s[h].astype(F32)
         d_att = datt_s[h]
         d_probs = dot_nt(d_att, values())
         d_scores = probs * (d_probs - jnp.sum(probs * d_probs, axis=-1, keepdims=True))
         ds_low = d_scores.astype(BF16)
         scale = head_width**-0.5
-        d_keys = inner_rows(ds_low, q_s[h]) * scale
-        d_values = inner_rows(probs.astype(BF16), d_att)
-        if h:
-            d_keys = d_keys + dkv_s[:, :head_width]
-            d_values = d_values + dkv_s[:, head_width:]
-        dkv_s[:, :head_width] = d_keys
-        dkv_s[:, head_width:] = d_values
+        ds_s[h] = ds_low
         cols = slice(h * head_width, (h + 1) * head_width)
         q_raw = raw_s[:, cols]
         d_q, d_gain = norm_back(
@@ -1111,8 +1120,18 @@
         dgains[QUERY : QUERY + 1, :head_width] += d_gain
 
     def return_keys():
-        for b in range(reach):
-            dkv_send[b] = dkv_s[pl.ds(b * rows, rows), :].astype(BF16)
+        for side, left, right, scale in (
+            (0, ds_s, q_s, head_width**-0.5),
+            (1, p_s, datt_s, 1.0),
+        ):
+            cols = slice(side * head_width, (side + 1) * head_width)
+            d_side = scale * inner_rows(
+                left[...].reshape(head_count * rows, (reach + 1) * rows),
+                right[...].reshape(head_count * rows, head_width),
+            )
+            for b in range(reach):
+                dkv_send[b, :, cols] = d_side[b * rows : (b + 1) * rows].astype(BF16)
+            dkv_s[:, cols] = d_side[reach * rows :]
         for copy in dkv_copies:
             copy.start()
 
@@ -1133,8 +1152,10 @@
             start = flip(z, m, 2) * span + c * (span // 2)
             cores[kind, m].wait_recv()
             grad_tiles(many(start, span // 2), turned, right, n_cols, mine_of(kind, m), True)
-            if m:
+            if m and kind == "o":
                 line_sums[kind, m].start()
+        if kind == "q":
+            his[-1].start()
 
     def output_grads():
         h_turn[pl.ds(0, query_width), pl.ds(0, rows)] = att_s[...].T
@@ -1142,7 +1163,7 @@
 
     def key_grads():
         h_turn[:, pl.ds(rows, rows)] = h1_s[...].T
-        d_kv = dkv_s[pl.ds(reach * rows, rows), :]
+        d_kv = dkv_s[...]
         for o in range(reach):
             dkv_copies[o].wait_recv()
             d_kv = d_kv + dkv_came[o].astype(F32)
@@ -1157,10 +1178,11 @@
 
     def sum_line(j):
         kind = chunks[j][0]
+        where = lo_part(kind, at.x, at.y) if kind == "q" else whole
         for m in range(1, n_fsdp):
             line_sums[kind, m].wait_recv()
-            add(mine_of(kind, 0), whole, {"o": line_o, "q": line_q}[kind].at[m - 1])
-        his[j].start()
+            add(mine_of(kind, 0), where, {"o": line_o, "q": line_q}[kind].at[m - 1])
+        (puts if kind == "q" else his)[j].start()
 
     def to_input():
         x = x_ref[...].astype(F32)
@@ -1189,46 +1211,46 @@
     take_hi(3)
     take_lo(0)
     take_lo(1)
+    begin_hand(0)
+    begin_hand(1)
     through_head(2)
     through_head(3)
     return_keys()
     output_grads()
-    begin_hand(0)
-    begin_hand(1)
     take_hi(4)
     take_hi(5)
     take_lo(2)
     take_lo(3)
     key_grads()
+    begin_hand(2)
     hand_on(0, 1)
     hand_on(1, 1)
-    begin_hand(2)
-    begin_hand(3)
     take_lo(4)
     take_lo(5)
+    begin_hand(3)
     to_input()
-    sum_line(6)
     hand_on(0, 2)
     hand_on(1, 2)
+    sum_line(6)
+    hand_on(2, 1)
     begin_hand(4)
     begin_hand(5)
-    hand_on(2, 1)
+    take_hi(7)
     hand_on(3, 1)
-    sum_line(7)
+    hand_on(2, 2)
+    sum_gains()
     take_hi(6)
-    hand_on(2, 2)
-    hand_on(3, 2)
-    take_hi(7)
-    take_lo(6)
+    take_lo(7)
     hand_on(4, 1)
     hand_on(5, 1)
+    hand_on(3, 2)
+    take_lo(6)
     begin_hand(6)
-    take_lo(7)
-    sum_gains()
+    sum_line(7)
     begin_hand(7)
+    hand_on(6, 1)
     hand_on(4, 2)
     hand_on(5, 2)
-    hand_on(6, 1)
     hand_on(7, 1)
     hand_on(6, 2)
     hand_on(7, 2)
@@ -1253,7 +1275,6 @@
     for i in range(n_att):
         for k in range(4):
             steps[i][k].wait_send()
-    rows_sent(send_h, 0)
     rows_sent(send_df, 2)
     parts_sent(send_dh, 3)
 
@@ -1285,7 +1306,7 @@
             shape((rows, width), F32),
             shape((8, width), F32),
             shape((2, n_fsdp, depth, hidden), BF16),
-            shape((hidden, width), BF16),
+            shape((2, hidden // 256, 128, width), BF16),
             shape((depth, heads_width), BF16),
             shape((rows_o, width), BF16),
         ],
@@ -1299,14 +1320,14 @@
             full(n_fsdp, 8, pack.shape[1]),
             pltpu.VMEM((n_seq, 8, rows), jnp.int32),
             full(8, width),
-            full(rows, (reach + 1) * rows),
+            low(rows, (reach + 1) * rows),
             full(2, rows, head_width // 2),
             low(rows, width),
             full(rows, heads_width),
             low(head_count, rows, head_width),
             low(rows, 2 * head_width),
             low(reach + 1, rows, 2 * head_width),
-            full(head_count, rows, (reach + 1) * rows),
+            low(head_count, rows, (reach + 1) * rows),
             low(rows, query_width),
             full(rows, width),
             full(rows, width),
@@ -1320,23 +1341,24 @@
             low(2, n_fsdp - 1, rows, width),
             low(2, rows, width),
             full(rows, width),
-            low(hidden // 2, width),
+            low(hidden // 256, 128, width),
             low(n_fsdp, depth, hidden),
             low(n_fsdp, rows_o // 2, width),
             low(n_fsdp, depth // 2, heads_width),
-            low(2, hidden // 8, width),
+            low(hidden // 256, 64, width),
             low(n_fsdp, depth // 2, hidden),
             low(1, rows_o // 4, width),
-            low(1, depth // 2, heads_width // 2),
-            low(2, hidden // 16, width),
+            low(n_fsdp, depth // 2, heads_width // 2),
+            low(hidden // 256, 32, width),
             low(n_fsdp, depth // 2, hidden // 2),
             low(1, rows_o // 8, width),
-            low(1, depth // 2, heads_width // 4),
+            low(n_fsdp, depth // 2, heads_width // 4),
             low(n_fsdp - 1, rows_o // 2, width),
-            low(n_fsdp - 1, depth // 2, heads_width),
+            low(n_fsdp - 1, depth // 2, heads_width // 4),
             low(rows, width),
             low(head_count, rows, head_width),
-            full((reach + 1) * rows, 2 * head_width),
+            low(head_count, rows, (reach + 1) * rows),
+            full(rows, 2 * head_width),
             low(reach, rows, 2 * head_width),
             low(reach, rows, 2 * head_width),
             low(rows, heads_width),
@@ -1374,7 +1396,7 @@
             sems((n_seq + n_fsdp,)),
         ],
         compiler_params=pltpu.CompilerParams(
-            collective_id=0, has_side_effects=True, vmem_limit_bytes=62 << 20
+            collective_id=0, has_side_effects=True, vmem_limit_bytes=63 << 20
         ),
         name="decoder_layer",
     )(x, cot, rates, pack, segs, w_gate, w_up, w_query, w_key, w_value, w_output, w_down)
@@ -1421,7 +1443,8 @@
         and n_fsdp == 4
         and args[0].shape[0] == 1
         and reach < n_seq
-        and rows_here % 128 == 0
+        and rows_here == 128
+        and window_width(share, n_fsdp) == 256 * (2 * n_fsdp - 1)
         and depth % 32 == 0
         and w_output.shape[0] % 128 == 0
         and w_key.shape[1] % 256 == 0
@@ -1474,7 +1497,7 @@
     )
     grad_gate, grad_up = joined(share, fin_gu)
     skipped = line * share - window_start(line, share)
-    grad_down = lax.dynamic_slice(fin_d, (skipped, jnp.int32(0)), (share, width)).astype(F32)
+    grad_down = lax.dynamic_slice(fin_d.reshape(hidden, width), (skipped, jnp.int32(0)), (share, width)).astype(F32)
 
     def part(row, gain):
         size = gain.shape[0]

time: 432 us -> 333 us (0.77); the launches traced: 432 us -> 326 us
  Pallas kernels: 406 us -> 301 us
    pallas_call x1, Pallas kernels: 400 us -> 294 us  [layer(): pl.pallas_call(functools.partial(layer_kernel, n_seq, n_fsdp, share, reac...]
where the time goes in v3:
time: 333 us; the launch traced here: 326 us
  Pallas kernels  301 us (90%)
  local copies, waits for them, and re-layouts  15.4 us (5%)
  other arithmetic  9.25 us (3%)
    pallas_call x1, Pallas kernels, layer(): pl.pallas_call(functools.partial(layer_kernel, n_seq, n_fsdp, share, reac...  294 us

profile of v3, /device:TPU:9, one launch (start us, length us, event | category | flops | bytes accessed | tf_op | source)
XLA Modules:
  0.0 326.5 jit_solution(1676686239092597442)
XLA Ops:
  0.6 0.5 multiply_power_fusion.rates_ref
  1.2 0.7 concatenate.22
  1.9 0.7 concatenate.23
  2.5 0.7 concatenate.24
  3.2 0.7 concatenate.25
  3.9 0.8 concatenate.28
  4.7 0.6 convert_element_type.19.pack_ref
  5.3 294.1 %decoder_layer.1 = (bf16[128,1152]{1,0:T(8,128)(2,1)}, f32[128,1152]{1,0:T(8,128)}, f32[8,1152]{1,0:T(8,128)}, bf16[2,4,288,1792]{3,2,1,0:T(8,128)(2,1)}, bf16[2...) custom-call(bf16[128,1152]{1,0:T(8,128)(2,1)} %bitcast.13, ...), custom_call_target="tpu_custom_call" | custom-call | tf_op jit(solution)/shard_map/decoder_layer/pallas_call | solution.py:1302
  299.4 1.0 fusion.7
  300.5 0.7 fusion
  301.1 2.2 slice.36
  303.3 1.8 fusion.6
  305.2 0.6 fusion.4
  305.8 2.2 convert_element_type.21
  307.9 0.7 fusion.2
  308.6 0.0 copy-start
  308.6 3.3 %copy-done = bf16[2,4,288,1792]{3,2,1,0:T(8,128)(2,1)S(1)} copy-done((bf16[2,4,288,1792]{3,2,1,0:T(8,128)(2,1)S(1)}, bf16[2,4,288,1792]{3,2,1,0:T(8,128)(2,1)}, u32[]{:S(2)}) %copy-start) | copy-done | bytes 8257560
  311.9 6.6 %join_windows.1 = (f32[288,6912]{1,0:T(8,128)}, f32[288,6912]{1,0:T(8,128)}) custom-call(bf16[2,4,288,1792]{3,2,1,0:T(8,128)(2,1)S(1)} %copy-done), custom_call_target="tpu_custom_call" | custom-call | tf_op jit(solution)/shard_map/join_windows/pallas_call | solution.py:1424
  318.5 0.0 copy-start.2
  318.5 0.0 copy-start.1
  318.6 6.0 %dynamic-slice_convert_fusion = f32[1728,1152]{1,0:T(8,128)} fusion(bf16[1792,1152]{1,0:T(8,128)(2,1)} %bitcast.11, s32[]{:T(128)S(6)} %select_n.15), kind=kLoop, calls=%fused_computation | loop fusion | flops 1990656 | bytes 11943940 | tf_op jit(solution)/shard_map/convert_element_type | solution.py:1500
  324.5 0.0 copy-done.2
  324.5 0.7 copy.33
  325.2 0.0 copy-done.1
  325.2 0.8 copy.34
Async XLA Ops:
  308.6 3.3 %copy-start = (bf16[2,4,288,1792]{3,2,1,0:T(8,128)(2,1)S(1)}, bf16[2,4,288,1792]{3,2,1,0:T(8,128)(2,1)}, u32[]{:S(2)}) copy-start(bf16[2,4,288,1792]{3,2,1,0:T(8,128)(2,1)} %get-tuple-element.29.wins_ref) | copy-start | bytes 24772612
  318.5 6.0 %copy-start.2 = (bf16[128,1152]{1,0:T(8,128)(2,1)S(1)}, bf16[128,1152]{1,0:T(8,128)(2,1)}, u32[]{:S(2)}) copy-start(bf16[128,1152]{1,0:T(8,128)(2,1)} %get-tuple-element.24) | copy-start | bytes 884740
  318.5 6.7 %copy-start.1 = (f32[128,1152]{1,0:T(8,128)S(1)}, f32[128,1152]{1,0:T(8,128)}, u32[]{:S(2)}) copy-start(f32[128,1152]{1,0:T(8,128)} %get-tuple-element.25) | copy-start | bytes 1769476

commit v4 on v3

--- a/solution.py
+++ b/solution.py
@@ -2,6 +2,7 @@
 
 import jax
 import jax.numpy as jnp
+import numpy as np
 from jax import lax
 from jax.experimental import pallas as pl
 from jax.experimental.pallas import tpu as pltpu
@@ -450,9 +451,10 @@
 
 def layer_kernel(
     n_seq, n_fsdp, share, reach, head_count,
-    x_ref, cot_ref, rates_ref, pack_ref, seg_ref,
+    x_ref, cot_ref, rates_ref, seg_ref,
+    gain_a, gain_b, gain_c, gain_d, gain_e, gain_f,
     gate_ref, up_ref, wq_ref, wk_ref, wv_ref, wo_ref, wd_ref,
-    out_ref, dx_out, gains_out, fin_gu, fin_d, fin_qkv, fin_wo,
+    small_out, fin_gu, fin_d,
     qkv_s, wo_s, w_in, w_down, pack_all, seg_all, gains, allowed, turns,
     h1_s, raw_s, q_s, kv_own, kv_s, p_s, att_s, o_s, mid_s,
     h_all, df_all, bent_s, act, d_in, h_turn, part_out, part_in, relay_in, total,
@@ -502,7 +504,11 @@
         ))
     ]
     seg_all[s] = jnp.broadcast_to(seg_ref[...], seg_all.shape[1:])
-    pack_all[z] = jnp.broadcast_to(pack_ref[...], pack_all.shape[1:])
+    start = 0
+    for ref in (gain_a, gain_b, gain_c, gain_d, gain_e, gain_f):
+        size = ref.shape[0]
+        pack_all[z, 0:1, start : start + size] = ref[...].astype(F32).reshape(1, size)
+        start += size
     greet([at.plane(k) for k in range(1, n_seq)] + [at.line(m) for m in range(1, n_fsdp)])
 
     packs = [
@@ -519,7 +525,7 @@
         for o in range(1, reach + 1)
     ]
 
-    def w_region(kind, whose, hi, lo, level):
+    def w_region(kind, sub, whose, hi, lo, level):
         base = whose * depth
         if kind == "q":
             cols = (
@@ -543,46 +549,58 @@
             if level < 1:
                 start = start + lo * (rows_o // 8)
             return wo_s.at[many(start, rows_o // (8, 4, 2)[level])]
+        skip, size = sub
         if level == 2:
-            return w_in.at[c, many(base, depth)]
-        here = many(base + hi * (depth // 2), depth // 2)
+            return [
+                w_in.at[c, many(base + half * (depth // 2) + skip, size)] for half in range(2)
+            ]
+        here = many(base + hi * (depth // 2) + skip, size)
         if level == 1:
             return w_in.at[c, here]
         return w_in.at[c, here, lanes(lo * (hidden // 2), hidden // 2)]
 
-    def w_sources(kind, to, hi, lo):
+    def w_sources(kind, sub, to, hi, lo):
         if kind == "q":
             cols = lanes(hi * (query_width // 2) + lo * (query_width // 4), query_width // 4)
             return [wq_ref.at[many(c * (depth // 2), depth // 2), cols]]
         if kind == "wo":
             start = c * (rows_o // 2) + hi * (rows_o // 4) + lo * (rows_o // 8)
             return [wo_ref.at[many(start, rows_o // 8)]]
-        here = many(hi * (depth // 2), depth // 2)
         if kind == "kv":
+            here = many(hi * (depth // 2), depth // 2)
             cols = lanes(lo * (head_width // 2), head_width // 2)
             return [ref.at[here, cols] for ref in (wk_ref, wv_ref)]
+        skip, size = sub
+        here = many(hi * (depth // 2) + skip, size)
         cols = lanes(window_start(to, share) + lo * (hidden // 2), hidden // 2)
         return [ref.at[here, cols] for ref in (gate_ref, up_ref)]
 
     items = []
-    for kinds in (("q", "kv"), ("wo",), ("gu",)):
+    for kinds in (("q", "kv"), ("wo",)):
         for m in range(1, n_fsdp):
             for kind in kinds:
-                items.append((kind, m, (m % 2 == 1) != (kind in ("kv", "wo"))))
+                items.append((kind, m, (m % 2 == 1) != (kind in ("kv", "wo")), None))
+    n_att = len(items)
+    for m in range(1, n_fsdp):
+        items.append(("gu", m, m % 2 == 1, (0, depth // 2)))
     steps, starts = [], []
-    for i, (kind, m, first_x) in enumerate(items):
+    for i, (kind, m, first_x, sub) in enumerate(items):
         hi, lo, mask_hi, mask_lo = at.halves(first_x)
         there = flip(z, m, 2)
         firsts = [
-            remote(src, w_region(kind, z, hi, lo, 0), w_send.at[i, 0], w_recv.at[i, 0], at.line(m))
-            for src in w_sources(kind, there, hi, lo)
+            remote(src, w_region(kind, sub, z, hi, lo, 0), w_send.at[i, 0], w_recv.at[i, 0],
+                   at.line(m))
+            for src in w_sources(kind, sub, there, hi, lo)
         ]
         starts.append(firsts)
-        steps.append([firsts[0]] + [
-            remote(w_region(kind, there, hi, lo, k), w_region(kind, there, hi, lo, k),
-                   w_send.at[i, k + 1], w_recv.at[i, k + 1], at.plane(mask))
-            for k, mask in enumerate((mask_lo, mask_hi, 1))
-        ])
+        stages = [firsts[:1]]
+        for k, mask in enumerate((mask_lo, mask_hi, 1)):
+            parts = w_region(kind, sub, there, hi, lo, k)
+            stages.append([
+                remote(part, part, w_send.at[i, k + 1 + n], w_recv.at[i, k + 1 + n], at.plane(mask))
+                for n, part in enumerate(parts if isinstance(parts, list) else [parts])
+            ])
+        steps.append(stages)
 
     def begin_weight(i):
         if len(starts[i]) == 1:
@@ -591,12 +609,21 @@
             for core, first in enumerate(starts[i]):
                 pl.when(c == core)(first.start)
 
+    def weight_here(i, stage):
+        for copy in steps[i][stage]:
+            copy.wait_recv()
+
     def move_weight(i, stage):
-        steps[i][stage - 1].wait_recv()
-        steps[i][stage].start()
+        weight_here(i, stage - 1)
+        for copy in steps[i][stage]:
+            copy.start()
+
+    def weight_sent(i):
+        for copies in steps[i]:
+            for copy in copies:
+                copy.wait_send()
 
     n_items = len(items)
-    n_att = n_items - (n_fsdp - 1)
     n_qkv = 2 * (n_fsdp - 1)
     ahead, lag = 6, 3
     for copy in packs + seg_copies:
@@ -606,6 +633,16 @@
     for copy in own_copies:
         copy.start()
 
+    def weight_steps(t):
+        for stage in (3, 2, 1):
+            i = t - lag * (stage - 1)
+            if 0 <= i < n_att:
+                move_weight(i, stage)
+                if stage == 1 and i + ahead < n_items:
+                    begin_weight(i + ahead)
+
+    weight_steps(0)
+    weight_steps(1)
     for copy in seg_copies:
         copy.wait_recv()
     across = lax.broadcasted_iota(jnp.int32, (rows, rows), 0)
@@ -637,21 +674,16 @@
     x = x_ref[...].astype(F32)
     h1_s[...] = (x * norm_scale(x) * gain(ATT_IN)).astype(BF16)
 
-    for t in range(n_att + 2 * lag):
-        for stage in (3, 2, 1):
-            i = t - lag * (stage - 1)
-            if 0 <= i < n_att:
-                move_weight(i, stage)
-                if stage == 1 and i + ahead < n_items:
-                    begin_weight(i + ahead)
+    for t in range(2, n_att + 2 * lag):
+        weight_steps(t)
     for i in range(n_qkv):
-        steps[i][3].wait_recv()
+        weight_here(i, 3)
     for copy in own_copies[:3]:
         copy.wait()
 
     def move_gu(*moves):
-        for m, stage in moves:
-            move_weight(n_att + m - 1, stage)
+        for k, stage in moves:
+            move_weight(n_att + k - 1, stage)
 
     move_gu((1, 1))
     tile = heads_width // 3
@@ -674,9 +706,9 @@
         q_fin = q_raw * norm_scale(q_raw) * gain(QUERY)
         q_s[h] = turn(q_fin, turns[0], turns[1]).astype(BF16)
     for i in range(n_qkv, n_att):
-        steps[i][3].wait_recv()
+        weight_here(i, 3)
     own_copies[3].wait()
-    move_gu((2, 1), (1, 2))
+    move_gu((1, 2))
     for copy in kv_copies:
         copy.wait_recv()
 
@@ -693,7 +725,6 @@
         probs = grown / jnp.sum(grown, axis=-1, keepdims=True)
         p_s[h] = probs.astype(BF16)
         att_s[:, h * head_width : (h + 1) * head_width] = dot_nn(p_s[h], values()).astype(BF16)
-        move_gu((((3, 1),), ((2, 2),), ((1, 3),), ((3, 2),))[h][0])
 
     @pl.loop(0, 3)
     def _(n):
@@ -727,13 +758,21 @@
     }
 
     def send_rows(copies):
-        copies[1].start()
         copies[2].start()
         pl.when(middle_z)(copies[last].start)
+        copies[1].start()
 
     def relay_rows(copies, phase):
-        copies[2].wait_recv()
-        pl.when(middle_z)(onward[phase].start)
+        @pl.when(middle_z)
+        def _():
+            copies[2].wait_recv()
+            onward[phase].start()
+
+    def take_rows(copies, m):
+        if m == 2:
+            pl.when(~middle_z)(copies[2].wait_recv)
+        elif m:
+            copies[m].wait_recv()
 
     def send_part(copies, phase, m):
         if m == 1:
@@ -780,18 +819,22 @@
         part_in[0, last - 1] = jnp.zeros((rows, width), BF16)
         part_in[1, last - 1] = jnp.zeros((rows, width), BF16)
 
+    move_gu((2, 1))
+    move_gu((3, 1))
+    move_gu((2, 2))
+    move_gu((1, 3))
+    move_gu((3, 2))
+    relay_rows(send_h, 0)
     move_gu((2, 3))
-    relay_rows(send_h, 0)
     move_gu((3, 3))
     for i in range(n_att, n_items):
-        steps[i][3].wait_recv()
+        weight_here(i, 3)
     for copy in own_copies[4:]:
         copy.wait()
     half_h = hidden // 2
 
-    for m in (*range(1, n_fsdp), 0):
-        if m not in (0, 2):
-            send_h[m].wait_recv()
+    for m in range(n_fsdp - 1, -1, -1):
+        take_rows(send_h, m)
         for n in range(2):
             cols = slice(n * half_h, (n + 1) * half_h)
             gate = dot_nn(h_all[m], w_in[0, :, cols])
@@ -816,8 +859,7 @@
     for m in range(n_fsdp):
         h_turn[:, pl.ds(m * rows, rows)] = h_all[m].T
     for i in range(n_att, n_items):
-        for k in range(4):
-            steps[i][k].wait_send()
+        weight_sent(i)
 
     take_parts(send_f)
     f_raw = total[...]
@@ -828,7 +870,7 @@
     d_f, d_gain = norm_back(f_raw, gain(FFN_OUT), scale, cot)
     df_all[0] = d_f.astype(BF16)
     send_rows(send_df)
-    out_ref[...] = (mid_s[...] + f_raw * scale * gain(FFN_OUT)).astype(BF16)
+    small_out[pl.ds(rows, rows), :] = mid_s[...] + f_raw * scale * gain(FFN_OUT)
     dgains[...] = jnp.zeros(dgains.shape, F32)
     dgains[FFN_OUT : FFN_OUT + 1, :] = d_gain
     parts_sent(send_f, 1)
@@ -868,20 +910,18 @@
 
     def fin_part(kind, i, where, core):
         if kind == "d":
-            return fin_d.at[core, spans_d[i], where[-2], :]
+            span = spans_d[i]
+            tiles = pl.ds(core * tiles_d + span.start, span.size)
+            return fin_d.at[tiles, where[-2], :]
         rows_at, cols_at = where
         if kind == "g":
-            return fin_gu.at[core, i, rows_at, cols_at]
-        ref, base, size = {
-            "q": (fin_qkv, core * (depth // 2), depth // 2),
-            "o": (fin_wo, core * (rows_o // 2), rows_o // 2),
-        }[kind]
-        if isinstance(rows_at, slice):
-            rows_at = many(base, size)
-        else:
-            rows_at = many(base + rows_at.start, rows_at.size)
-        return ref.at[rows_at, cols_at]
-
+            return fin_gu.at[core * n_fsdp + i, rows_at, cols_at]
+        if kind == "o":
+            return fin_d.at[2 * tiles_d + core, rows_at, :]
+        base = core * (depth // 2)
+        if isinstance(cols_at, slice):
+            cols_at = pl.ds(0, heads_width)
+        return fin_gu.at[2 * n_fsdp, many(base, depth // 2), cols_at]
     def add(ref, where, other):
         rows_at, cols_at = where
         start = 0 if isinstance(rows_at, slice) else rows_at.start
@@ -1033,8 +1073,7 @@
     for m in range(n_fsdp):
         if m == 1:
             relay_rows(send_df, 2)
-        if m not in (0, 2):
-            send_df[m].wait_recv()
+        take_rows(send_df, m)
         if m == last:
             down_grads(1 - c, down_stage, False)
             cores["d", 0].start()
@@ -1188,7 +1227,7 @@
         x = x_ref[...].astype(F32)
         d_h = dot_nt(dqkv_s[...], qkv_s[...])
         d_x, d_gain = norm_back(x, gain(ATT_IN), norm_scale(x), d_h)
-        dx_out[...] = mid_s[...] + d_x
+        small_out[pl.ds(0, rows), :] = mid_s[...] + d_x
         dgains[ATT_IN : ATT_IN + 1, :] = d_gain
         for copy in gain_copies:
             copy.start()
@@ -1258,7 +1297,16 @@
     for m, copy in enumerate(gain_lines):
         copy.wait_recv()
         sums = sums + gain_line[m + 1]
-    gains_out[...] = sums
+    for row in range(6):
+        size = depth if row < QUERY else head_width // n_fsdp
+        for block in range(n_fsdp):
+
+            @pl.when(z == block)
+            def _():
+                small_out[2 * rows + row : 2 * rows + row + 1, :size] = sums[
+                    row : row + 1, block * size : (block + 1) * size
+                ]
+
 
     for j in range(len(chunks)):
         hands[j][2].wait_recv()
@@ -1273,13 +1321,12 @@
     for copy in gain_copies + gain_lines + dkv_copies + kv_copies + packs + seg_copies:
         copy.wait_send()
     for i in range(n_att):
-        for k in range(4):
-            steps[i][k].wait_send()
+        weight_sent(i)
     rows_sent(send_df, 2)
     parts_sent(send_dh, 3)
 
 
-def layer(n_seq, n_fsdp, share, hidden, reach, head_count, x, cot, rates, pack, segs,
+def layer(n_seq, n_fsdp, share, hidden, reach, head_count, x, cot, rates, segs, gains,
           w_gate, w_up, w_query, w_key, w_value, w_output, w_down):
     rows, width = x.shape
     depth = width // n_fsdp
@@ -1302,22 +1349,18 @@
     return pl.pallas_call(
         functools.partial(layer_kernel, n_seq, n_fsdp, share, reach, head_count),
         out_shape=[
-            shape((rows, width), BF16),
-            shape((rows, width), F32),
-            shape((8, width), F32),
-            shape((2, n_fsdp, depth, hidden), BF16),
-            shape((2, hidden // 256, 128, width), BF16),
-            shape((depth, heads_width), BF16),
-            shape((rows_o, width), BF16),
+            shape((2 * rows + 8, width), F32),
+            shape((2 * n_fsdp + 1, depth, hidden), BF16),
+            shape((hidden // 128 + 2, 128, width), BF16),
         ],
-        in_specs=[in_vmem] * 5 + [anywhere] * 7,
-        out_specs=[in_vmem] * 3 + [anywhere] * 4,
+        in_specs=[in_vmem] * 10 + [anywhere] * 7,
+        out_specs=[in_vmem] + [anywhere] * 2,
         scratch_shapes=[
             low(width, heads_width),
             low(n_fsdp * rows_o, width),
             low(2, width, hidden),
             low(hidden, width),
-            full(n_fsdp, 8, pack.shape[1]),
+            full(n_fsdp, 8, -(-sum(g.shape[0] for g in gains) // 128) * 128),
             pltpu.VMEM((n_seq, 8, rows), jnp.int32),
             full(8, width),
             low(rows, (reach + 1) * rows),
@@ -1365,8 +1408,8 @@
             full(8, width),
             full(n_seq, 8, width),
             full(n_fsdp, 8, width),
-            sems((n_items, 4)),
-            sems((n_items, 4)),
+            sems((n_items, 5)),
+            sems((n_items, 5)),
             sems((7,)),
             sems((n_fsdp,)),
             sems((n_fsdp,)),
@@ -1399,37 +1442,113 @@
             collective_id=0, has_side_effects=True, vmem_limit_bytes=63 << 20
         ),
         name="decoder_layer",
-    )(x, cot, rates, pack, segs, w_gate, w_up, w_query, w_key, w_value, w_output, w_down)
-
-
-def join_kernel(share, wins_ref, gate_ref, up_ref):
-    n_win, hidden = wins_ref.shape[1], wins_ref.shape[3]
+    )(x, cot, rates, segs, *gains, w_gate, w_up, w_query, w_key, w_value, w_output, w_down)
+
+
+def finish_kernel(
+    share, skip_ref, wins_ref, d0_ref, d1_ref, d2_ref, qkv_ref, wo_ref, small_ref,
+    gate_ref, up_ref, down_ref, wq_ref, wk_ref, wv_ref, wo_out, out_ref, dx_ref, *gain_outs,
+):
+    n_win, hidden = wins_ref.shape[0] // 2, wins_ref.shape[2]
     starts = [window_start(i, share) for i in range(n_win)]
     for i, ref in enumerate((gate_ref, up_ref)):
         for w in range(n_win):
+            at = i * n_win + w
             first = starts[w]
             last = starts[w + 1] if w + 1 < n_win else first + hidden
             shared = starts[w - 1] + hidden - first if w else 0
             if shared:
-                ref[:, first : first + shared] = wins_ref[i, w, :, :shared].astype(F32) + wins_ref[
-                    i, w - 1, :, hidden - shared :
+                ref[:, first : first + shared] = wins_ref[at, :, :shared].astype(F32) + wins_ref[
+                    at - 1, :, hidden - shared :
                 ].astype(F32)
-            ref[:, first + shared : last] = wins_ref[i, w, :, shared : last - first].astype(F32)
-
-
-def joined(share, windows):
-    _, n_win, rows, hidden = windows.shape
+            ref[:, first + shared : last] = wins_ref[at, :, shared : last - first].astype(F32)
+    for k, ref in enumerate((d0_ref, d1_ref, d2_ref)):
+        down_ref[pl.ds(k * ref.shape[0], ref.shape[0]), :] = ref[...].astype(F32)
+    start = 0
+    for ref in (wq_ref, wk_ref, wv_ref):
+        size = ref.shape[1]
+        ref[...] = qkv_ref[0, :, start : start + size].astype(F32)
+        start += size
+    wo_out[...] = wo_ref[...].astype(F32)
+
+    @pl.when(pl.program_id(0) == 0)
+    def _():
+        rows_here = dx_ref.shape[0]
+        dx_ref[...] = small_ref[:rows_here]
+        out_ref[...] = small_ref[rows_here : 2 * rows_here].astype(BF16)
+        for row, ref in enumerate(gain_outs):
+            ref[...] = small_ref[2 * rows_here + row, : ref.shape[0]]
+
+
+def finish(share, skipped, gain_sizes, query_width, head_width, rows_o, windows, tiles, small):
+    n_win, rows, hidden = windows.shape
+    n_win = n_win // 2
+    width = tiles.shape[2]
+    rows_here = small.shape[0] // 2 - 4
     slab = 32
-    wide = pl.BlockSpec((slab, n_win * share), lambda i: (i, 0))
+    steps = rows // slab
+    down_slab = share // steps // 3
+    heads_width = query_width + 2 * head_width
+    down = tiles.reshape(-1, width)
+    start_o = (down.shape[0] - rows_o) // slab
+    shape = jax.ShapeDtypeStruct
+
+    def slabs(n_rows, n_cols, n_slabs):
+        return pl.BlockSpec(
+            (n_rows, n_cols), lambda i, skip: (jnp.minimum(i, n_slabs - 1), 0)
+        )
+
+    def down_part(k):
+        return pl.BlockSpec((down_slab, width), lambda i, skip: (3 * i + k + skip[0], 0))
+
+    def whole(array_shape):
+        return pl.BlockSpec(array_shape, lambda i, skip: (0,) * len(array_shape))
+
     return pl.pallas_call(
-        functools.partial(join_kernel, share),
-        grid=(rows // slab,),
-        out_shape=[jax.ShapeDtypeStruct((rows, n_win * share), F32)] * 2,
-        in_specs=[pl.BlockSpec((2, n_win, slab, hidden), lambda i: (0, 0, i, 0))],
-        out_specs=[wide, wide],
-        compiler_params=pltpu.CompilerParams(vmem_limit_bytes=32 << 20),
-        name="join_windows",
-    )(windows)
+        functools.partial(finish_kernel, share),
+        grid_spec=pltpu.PrefetchScalarGridSpec(
+            num_scalar_prefetch=1,
+            grid=(steps,),
+            in_specs=[
+                pl.BlockSpec((2 * n_win, slab, hidden), lambda i, skip: (0, i, 0)),
+                down_part(0),
+                down_part(1),
+                down_part(2),
+                pl.BlockSpec((1, slab, heads_width), lambda i, skip: (2 * n_win, i, 0)),
+                pl.BlockSpec(
+                    (slab, width),
+                    lambda i, skip: (start_o + jnp.minimum(i, rows_o // slab - 1), 0),
+                ),
+                whole(small.shape),
+            ],
+            out_specs=[
+                slabs(slab, n_win * share, steps),
+                slabs(slab, n_win * share, steps),
+                slabs(3 * down_slab, width, steps),
+                slabs(slab, query_width, steps),
+                slabs(slab, head_width, steps),
+                slabs(slab, head_width, steps),
+                slabs(slab, width, rows_o // slab),
+                whole((rows_here, width)),
+                whole((rows_here, width)),
+            ]
+            + [whole((size,)) for size in gain_sizes],
+        ),
+        out_shape=[
+            shape((rows, n_win * share), F32),
+            shape((rows, n_win * share), F32),
+            shape((share, width), F32),
+            shape((rows, query_width), F32),
+            shape((rows, head_width), F32),
+            shape((rows, head_width), F32),
+            shape((rows_o, width), F32),
+            shape((rows_here, width), BF16),
+            shape((rows_here, width), F32),
+        ]
+        + [shape((size,), F32) for size in gain_sizes],
+        compiler_params=pltpu.CompilerParams(vmem_limit_bytes=48 << 20),
+        name="finish",
+    )((skipped // down_slab).reshape(1), windows, down, down, down, windows, down, small)
 
 
 def shards(n_seq, n_fsdp, *args):
@@ -1446,12 +1565,14 @@
         and rows_here == 128
         and window_width(share, n_fsdp) == 256 * (2 * n_fsdp - 1)
         and depth % 32 == 0
-        and w_output.shape[0] % 128 == 0
+        and w_output.shape[0] == 256
         and w_key.shape[1] % 256 == 0
         and w_query.shape[1] % 512 == 0
         and w_output.shape[1] % 384 == 0
         and ffn_width % n_fsdp == 0
         and share % 16 == 0
+        and rows_here // 2 * (share // 64) * 2 == rows_here * (depth // 32) * 3
+        and (share - window_start(1, share)) % 64 == 0
         and window_start(n_fsdp - 1, share) + window_width(share, n_fsdp) == ffn_width
     )
     if fits:
@@ -1488,38 +1609,35 @@
     reach = (WINDOW - 2 + rows_here) // rows_here
     line = lax.axis_index("fsdp")
     gains = (gain_attn_in, gain_attn_out, gain_ffn_in, gain_ffn_out, gain_query, gain_key)
-    pack = jnp.concatenate(gains).astype(F32)[None]
-    rates = 10000.0 ** (-(jnp.arange(head_width // 2, dtype=F32) * 2.0) / head_width)
-    outputs, d_inputs, gain_sums, fin_gu, fin_d, fin_qkv, fin_wo = layer(
+    rates = 10000.0 ** (-(np.arange(head_width // 2, dtype=np.float32) * 2.0) / head_width)
+    small, fin_gu, fin_d = layer(
         n_seq, n_fsdp, share, hidden, reach, head_count,
-        inputs[0], cotangent[0], rates[None], pack, segments,
+        inputs[0], cotangent[0], jnp.asarray(rates, F32)[None], segments, gains,
         w_gate, w_up, w_query, w_key, w_value, w_output, w_down,
     )
-    grad_gate, grad_up = joined(share, fin_gu)
-    skipped = line * share - window_start(line, share)
-    grad_down = lax.dynamic_slice(fin_d.reshape(hidden, width), (skipped, jnp.int32(0)), (share, width)).astype(F32)
-
-    def part(row, gain):
-        size = gain.shape[0]
-        return lax.dynamic_slice(gain_sums[row], (line * size,), (size,))
-
-    fin_qkv = fin_qkv.astype(F32)
+    (
+        grad_gate, grad_up, grad_down, grad_q, grad_k, grad_v, grad_o, outputs, d_inputs,
+        g_attn_in, g_attn_out, g_ffn_in, g_ffn_out, g_query, g_key,
+    ) = finish(
+        share, line * share - window_start(line, share), [g.shape[0] for g in gains],
+        query_width, head_width, w_output.shape[0], fin_gu, fin_d, small,
+    )
     return (
         outputs[None],
         d_inputs[None],
-        part(ATT_IN, gain_attn_in),
-        fin_qkv[:, :query_width],
-        fin_qkv[:, query_width : query_width + head_width],
-        fin_qkv[:, query_width + head_width :],
-        part(QUERY, gain_query),
-        part(KEY, gain_key),
-        fin_wo.astype(F32),
-        part(ATT_OUT, gain_attn_out),
-        part(FFN_IN, gain_ffn_in),
+        g_attn_in,
+        grad_q,
+        grad_k,
+        grad_v,
+        g_query,
+        g_key,
+        grad_o,
+        g_attn_out,
+        g_ffn_in,
         grad_gate,
         grad_up,
         grad_down,
-        part(FFN_OUT, gain_ffn_out),
+        g_ffn_out,
     )
 
 

time: 333 us -> 308 us (0.925)
  the two profiles are of different devices: /device:TPU:9 before, /device:TPU:19 now
where the time goes in v4:
time: 308 us; the launch traced here: 304 us
  Pallas kernels  299 us (97%)
  local copies, waits for them, and re-layouts  3.61 us (1%)
    pallas_call x1, Pallas kernels, layer(): pl.pallas_call(functools.partial(layer_kernel, n_seq, n_fsdp, share, reac...  285 us
    pallas_call x1, Pallas kernels, finish(): pl.pallas_call(functools.partial(finish_kernel, share), grid_spec=pltpu.P...  13.4 us

profile of v4, /device:TPU:19, one launch (start us, length us, event | category | flops | bytes accessed | tf_op | source)
XLA Modules:
  0.0 303.6 jit_solution(6428836828565803788)
XLA Ops:
  0.7 285.4 %decoder_layer.1 = (f32[264,1152]{1,0:T(8,128)}, bf16[9,288,1792]{2,1,0:T(8,128)(2,1)}, bf16[16,128,1152]{2,1,0:T(8,128)(2,1)}) custom-call(bf16[128,1152]{1,0:T(8,128)(2,1)} %bitcast.10, bf16[128,1152]{1,0:T(8,128)(2,1)} %bitcast.11, f32[1,128]{1,0:T(1,128)} %constant.33.rates_ref, s32[1,128]{1,0:T(1,128)} %seg_ref.1, bf16[288]{0:T(512)(128)(2,1)} %gain_a.1, ...), custom_call_target="tpu_custom_call" | custom-call | tf_op jit(solution)/shard_map/decoder_layer/pallas_call | solution.py:1349
  286.1 0.0 copy-start
  286.1 2.3 copy-done
  288.5 0.0 copy-start.1
  288.5 1.3 copy-done.1
  289.7 13.4 %finish.1 = (f32[288,6912]{1,0:T(8,128)}, f32[288,6912]{1,0:T(8,128)}, f32[1728,1152]{1,0:T(8,128)}, f32[288,1024]{1,0:T(8,128)}, f32[288,256]{1,0:T(8,128)}, /*...) custom-call(s32[1]{0:T(128)} %bitcast.skip_ref, ...), custom_call_target="tpu_custom_call" | custom-call | tf_op jit(solution)/shard_map/finish/pallas_call | solution.py:1507
Async XLA Ops:
  286.1 2.3 copy-start
  288.5 1.3 copy-start.1

commit v5 on v4

--- a/solution.py
+++ b/solution.py
@@ -579,7 +579,7 @@
     for kinds in (("q", "kv"), ("wo",)):
         for m in range(1, n_fsdp):
             for kind in kinds:
-                items.append((kind, m, (m % 2 == 1) != (kind in ("kv", "wo")), None))
+                items.append((kind, m, (m % 2 == 1) == (kind in ("kv", "wo")), None))
     n_att = len(items)
     for m in range(1, n_fsdp):
         items.append(("gu", m, m % 2 == 1, (0, depth // 2)))
@@ -709,6 +709,7 @@
         weight_here(i, 3)
     own_copies[3].wait()
     move_gu((1, 2))
+    move_gu((2, 1))
     for copy in kv_copies:
         copy.wait_recv()
 
@@ -726,6 +727,7 @@
         p_s[h] = probs.astype(BF16)
         att_s[:, h * head_width : (h + 1) * head_width] = dot_nn(p_s[h], values()).astype(BF16)
 
+    move_gu((3, 1))
     @pl.loop(0, 3)
     def _(n):
         o_s[:, outs(n)] = dot_nn(att_s[...], wo_s[:, outs(n)])
@@ -819,8 +821,6 @@
         part_in[0, last - 1] = jnp.zeros((rows, width), BF16)
         part_in[1, last - 1] = jnp.zeros((rows, width), BF16)
 
-    move_gu((2, 1))
-    move_gu((3, 1))
     move_gu((2, 2))
     move_gu((1, 3))
     move_gu((3, 2))
@@ -1546,7 +1546,7 @@
             shape((rows_here, width), F32),
         ]
         + [shape((size,), F32) for size in gain_sizes],
-        compiler_params=pltpu.CompilerParams(vmem_limit_bytes=48 << 20),
+        compiler_params=pltpu.CompilerParams(vmem_limit_bytes=63 << 20),
         name="finish",
     )((skipped // down_slab).reshape(1), windows, down, down, down, windows, down, small)
 

time: 308 us -> 303 us (0.984)
  the two profiles are of different devices: /device:TPU:19 before, /device:TPU:9 now
where the time goes in v5:
time: 303 us; the launch traced here: 298 us
  Pallas kernels  296 us (98%)
    pallas_call x1, Pallas kernels, layer(): pl.pallas_call(functools.partial(layer_kernel, n_seq, n_fsdp, share, reac...  280 us
    pallas_call x1, Pallas kernels, finish(): pl.pallas_call(functools.partial(finish_kernel, share), grid_spec=pltpu.P...  16.1 us

profile of v5, /device:TPU:9, one launch (start us, length us, event | category | flops | bytes accessed | tf_op | source)
XLA Modules:
  0.0 297.5 jit_solution(9975018272056066574)
XLA Ops:
  0.7 280.3 %decoder_layer.1 = (f32[264,1152]{1,0:T(8,128)}, bf16[9,288,1792]{2,1,0:T(8,128)(2,1)}, bf16[16,128,1152]{2,1,0:T(8,128)(2,1)}) custom-call(bf16[128,1152]{1,0:T(8,128)(2,1)} %bitcast.10, bf16[128,1152]{1,0:T(8,128)(2,1)} %bitcast.11, f32[1,128]{1,0:T(1,128)} %constant.33.rates_ref, s32[1,128]{1,0:T(1,128)} %seg_ref.1, bf16[288]{0:T(512)(128)(2,1)} %gain_a.1, ...), custom_call_target="tpu_custom_call" | custom-call | tf_op jit(solution)/shard_map/decoder_layer/pallas_call | solution.py:1349
  281.0 16.1 %finish.1 = (f32[288,6912]{1,0:T(8,128)}, f32[288,6912]{1,0:T(8,128)}, f32[1728,1152]{1,0:T(8,128)}, f32[288,1024]{1,0:T(8,128)}, f32[288,256]{1,0:T(8,128)}, /*...) custom-call(s32[1]{0:T(128)} %bitcast.skip_ref, ...), custom_call_target="tpu_custom_call" | custom-call | tf_op jit(solution)/shard_map/finish/pallas_call | solution.py:1507

commit v6 on v5

--- a/solution.py
+++ b/solution.py
@@ -1246,51 +1246,51 @@
     to_middle()
     through_head(0)
     through_head(1)
+    through_head(2)
+    through_head(3)
+    return_keys()
+    output_grads()
     take_hi(2)
     take_hi(3)
     take_lo(0)
     take_lo(1)
     begin_hand(0)
     begin_hand(1)
-    through_head(2)
-    through_head(3)
-    return_keys()
-    output_grads()
+    key_grads()
     take_hi(4)
     take_hi(5)
     take_lo(2)
     take_lo(3)
-    key_grads()
     begin_hand(2)
+    sum_line(6)
     hand_on(0, 1)
     hand_on(1, 1)
     take_lo(4)
     take_lo(5)
+    to_input()
     begin_hand(3)
-    to_input()
     hand_on(0, 2)
     hand_on(1, 2)
-    sum_line(6)
+    take_hi(7)
     hand_on(2, 1)
     begin_hand(4)
     begin_hand(5)
-    take_hi(7)
+    take_hi(6)
     hand_on(3, 1)
+    take_lo(7)
     hand_on(2, 2)
     sum_gains()
-    take_hi(6)
-    take_lo(7)
+    take_lo(6)
+    begin_hand(6)
     hand_on(4, 1)
     hand_on(5, 1)
-    hand_on(3, 2)
-    take_lo(6)
-    begin_hand(6)
     sum_line(7)
     begin_hand(7)
+    hand_on(3, 2)
     hand_on(6, 1)
+    hand_on(7, 1)
     hand_on(4, 2)
     hand_on(5, 2)
-    hand_on(7, 1)
     hand_on(6, 2)
     hand_on(7, 2)
     sums = gain_line[0]

time: 303 us -> 299 us (0.987)
    pallas_call x1, Pallas kernels: 280 us -> 277 us  [layer(): pl.pallas_call(functools.partial(layer_kernel, n_seq, n_fsdp, share, reac...]
where the time goes in v6:
time: 299 us; the launch traced here: 294 us
  Pallas kernels  293 us (98%)
    pallas_call x1, Pallas kernels, layer(): pl.pallas_call(functools.partial(layer_kernel, n_seq, n_fsdp, share, reac...  277 us
    pallas_call x1, Pallas kernels, finish(): pl.pallas_call(functools.partial(finish_kernel, share), grid_spec=pltpu.P...  16.1 us

profile of v6, /device:TPU:9, one launch (start us, length us, event | category | flops | bytes accessed | tf_op | source)
XLA Modules:
  0.0 293.8 jit_solution(1850897896005737312)
XLA Ops:
  0.7 276.5 %decoder_layer.1 = (f32[264,1152]{1,0:T(8,128)}, bf16[9,288,1792]{2,1,0:T(8,128)(2,1)}, bf16[16,128,1152]{2,1,0:T(8,128)(2,1)}) custom-call(bf16[128,1152]{1,0:T(8,128)(2,1)} %bitcast.10, bf16[128,1152]{1,0:T(8,128)(2,1)} %bitcast.11, f32[1,128]{1,0:T(1,128)} %constant.33.rates_ref, s32[1,128]{1,0:T(1,128)} %seg_ref.1, bf16[288]{0:T(512)(128)(2,1)} %gain_a.1, ...), custom_call_target="tpu_custom_call" | custom-call | tf_op jit(solution)/shard_map/decoder_layer/pallas_call | solution.py:1349
  277.2 16.1 %finish.1 = (f32[288,6912]{1,0:T(8,128)}, f32[288,6912]{1,0:T(8,128)}, f32[1728,1152]{1,0:T(8,128)}, f32[288,1024]{1,0:T(8,128)}, f32[288,256]{1,0:T(8,128)}, /*...) custom-call(s32[1]{0:T(128)} %bitcast.skip_ref, ...), custom_call_target="tpu_custom_call" | custom-call | tf_op jit(solution)/shard_map/finish/pallas_call | solution.py:1507

commit v7 on v6

--- a/solution.py
+++ b/solution.py
@@ -686,12 +686,7 @@
             move_weight(n_att + k - 1, stage)
 
     move_gu((1, 1))
-    tile = heads_width // 3
-
-    @pl.loop(0, 3)
-    def _(n):
-        cols = lanes(n * tile, tile)
-        raw_s[:, cols] = dot_nn(h1_s[...], qkv_s[:, cols])
+    raw_s[...] = dot_nn(h1_s[...], qkv_s[...])
 
     k_raw = raw_s[:, query_width : query_width + head_width]
     kv_own[:, :head_width] = turn(
@@ -728,11 +723,8 @@
         att_s[:, h * head_width : (h + 1) * head_width] = dot_nn(p_s[h], values()).astype(BF16)
 
     move_gu((3, 1))
-    @pl.loop(0, 3)
-    def _(n):
-        o_s[:, outs(n)] = dot_nn(att_s[...], wo_s[:, outs(n)])
-
-    o_raw = o_s[...]
+    o_raw = dot_nn(att_s[...], wo_s[...])
+    o_s[...] = o_raw
     middle = x_ref[...].astype(F32) + o_raw * norm_scale(o_raw) * gain(ATT_OUT)
     mid_s[...] = middle
     h_all[0] = (middle * norm_scale(middle) * gain(FFN_IN)).astype(BF16)

time: 299 us -> 299 us (level)
  no operation moved by 1% of the time
where the time goes in v7:
time: 299 us; the launch traced here: 293 us
  Pallas kernels  292 us (98%)
    pallas_call x1, Pallas kernels, layer(): pl.pallas_call(functools.partial(layer_kernel, n_seq, n_fsdp, share, reac...  276 us
    pallas_call x1, Pallas kernels, finish(): pl.pallas_call(functools.partial(finish_kernel, share), grid_spec=pltpu.P...  16.1 us

profile of v7, /device:TPU:9, one launch (start us, length us, event | category | flops | bytes accessed | tf_op | source)
XLA Modules:
  0.0 293.4 jit_solution(5705080983028002377)
XLA Ops:
  0.7 276.2 %decoder_layer.1 = (f32[264,1152]{1,0:T(8,128)}, bf16[9,288,1792]{2,1,0:T(8,128)(2,1)}, bf16[16,128,1152]{2,1,0:T(8,128)(2,1)}) custom-call(bf16[128,1152]{1,0:T(8,128)(2,1)} %bitcast.10, bf16[128,1152]{1,0:T(8,128)(2,1)} %bitcast.11, f32[1,128]{1,0:T(1,128)} %constant.33.rates_ref, s32[1,128]{1,0:T(1,128)} %seg_ref.1, bf16[288]{0:T(512)(128)(2,1)} %gain_a.1, ...), custom_call_target="tpu_custom_call" | custom-call | tf_op jit(solution)/shard_map/decoder_layer/pallas_call | solution.py:1341
  276.9 16.1 %finish.1 = (f32[288,6912]{1,0:T(8,128)}, f32[288,6912]{1,0:T(8,128)}, f32[1728,1152]{1,0:T(8,128)}, f32[288,1024]{1,0:T(8,128)}, f32[288,256]{1,0:T(8,128)}, /*...) custom-call(s32[1]{0:T(128)} %bitcast.skip_ref, ...), custom_call_target="tpu_custom_call" | custom-call | tf_op jit(solution)/shard_map/finish/pallas_call | solution.py:1499
